TPU v7x, 32 devices: a whole 2x2x4 slice. The times are simulated.
32 devices in a mesh: context: 8 (over z, x), head: 4 (over y, core).
Axes of the slice: x: 2, y: 2, z: 4, core: 2. Of those that a mesh axis runs over, the one named last changes fastest.
Arguments:
- queries: bfloat16 [4096, 4096], P(('context', 'head')), may hold values from -6 to 6
- key_input: bfloat16 [4096, 4096], P(('context', 'head')), may hold values from -32 to 32
- value_input: bfloat16 [4096, 4096], P(('context', 'head')), may hold values from -32 to 32
- gate_input: bfloat16 [4096, 4096], P(('context', 'head')), may hold values from -6 to 6
- decay_logit: float32 [4096, 32], P(('context', 'head')), may hold values from -5 to 16
- beta_logit: float32 [4096, 32], P(('context', 'head')), may hold values from -9 to 9
- decay_bias: float32 [32], P('head'), may hold values from -16 to -3
- norm_gain: float32 [128], replicated, may hold values from 0.1 to 1.9
- doc_start: int32 [64], P('context'), may hold values from 0 to 1, as said below
Outputs:
- layer_output: bfloat16 [4096, 4096], P(('context', 'head'))
Inputs may be any that keep to these rules, and one draw needn't show every extreme that they name: `doc_start`: exactly one of the groups 1 to max(3, 8) holds a 1; apart from it, 1 appears only in the last max(2, 8) groups.
All inputs are finite; a program needn't handle non-finite values.
Results may differ from a plain program's by a relative error of at most 0.013.
Values may be sent and summed in bfloat16 or wider, within the bound.
No kernel may reach another device: no remote copies, remote signals or barrier semaphores. Data moves between devices by JAX's collectives and lax.ppermute only.
A program may use at most 192 MiB of HBM per device.

v0:
```python
import jax
import jax.numpy as jnp
from jax import lax
from jax.sharding import PartitionSpec as P

C = 64


PRECISE = lax.Precision.HIGHEST


def carried_in(shard, axis, join, neutral):
    place = lax.axis_index(axis)
    gathered = jax.tree.map(
        lambda a, kind: lax.all_gather(a.astype(kind), axis),
        shard,
        jax.tree.map(lambda a: jnp.bfloat16 if a.dtype == jnp.float32 else a.dtype, shard),
    )
    state = jax.tree.map(lambda a, e: jnp.zeros_like(a) + jnp.asarray(e, a.dtype), shard, neutral)

    def one(hop, state):
        return join(
            state,
            jax.tree.map(
                lambda a, own: lax.dynamic_index_in_dim(a, hop, 0, False).astype(own.dtype),
                gathered,
                shard,
            ),
        )

    return lax.fori_loop(0, place, one, state)


def gated_norm(core_rows, gate_input, norm_gain):
    row_count = core_rows.shape[0]
    widened = core_rows.astype(jnp.float32).reshape(row_count, -1, norm_gain.shape[0])
    scaled = widened * lax.rsqrt(jnp.mean(widened * widened, axis=-1, keepdims=True) + 1e-06)
    gate_wide = gate_input.astype(jnp.float32).reshape(widened.shape)
    result = scaled * norm_gain * jax.nn.silu(gate_wide)
    return result.reshape(row_count, -1).astype(jnp.bfloat16)


def carried_part(query_blocks, gammas, query_mix, solved_keys, entering):
    through = (
        jnp.einsum("nthd,nhde->nthe", query_blocks, entering, precision=PRECISE)
        * gammas[:, :, :, None]
    )
    key_state = jnp.einsum("nhsd,nhde->nhse", solved_keys, entering, precision=PRECISE)
    return through - jnp.einsum("nhts,nhse->nthe", query_mix, key_state, precision=PRECISE)


def compose(earlier, later):
    product = jnp.einsum("hde,hef->hdf", later[0], earlier[0], precision=PRECISE)
    summed = jnp.einsum("hde,hef->hdf", later[0], earlier[1], precision=PRECISE) + later[1]
    return (product, summed)


def body(
    queries,
    key_input,
    value_input,
    gate_input,
    decay_logit,
    beta_logit,
    decay_bias,
    norm_gain,
    doc_start,
):
    query_rows, key_rows, value_rows = (
        lax.all_to_all(queries, "head", split_axis=1, concat_axis=0, tiled=True),
        lax.all_to_all(key_input, "head", split_axis=1, concat_axis=0, tiled=True),
        lax.all_to_all(value_input, "head", split_axis=1, concat_axis=0, tiled=True),
    )
    decay_rows, beta_rows = (
        lax.all_to_all(
            decay_logit.astype(jnp.bfloat16), "head", split_axis=1, concat_axis=0, tiled=True
        ).astype(decay_logit.dtype),
        lax.all_to_all(
            beta_logit.astype(jnp.bfloat16), "head", split_axis=1, concat_axis=0, tiled=True
        ).astype(beta_logit.dtype),
    )
    length = decay_rows.shape[0]
    head_count = decay_rows.shape[1]
    groups = length // C
    key_width = key_rows.shape[1] // head_count
    value_width = value_rows.shape[1] // head_count
    log_decay = -jax.nn.softplus(decay_rows + decay_bias[None, :])
    beta_gate = jax.nn.sigmoid(beta_rows)
    query_blocks = query_rows.reshape(groups, C, head_count, key_width)
    raw_keys = key_rows.reshape(groups, C, head_count, key_width).astype(jnp.float32)
    normed = (
        raw_keys * lax.rsqrt(jnp.sum(raw_keys * raw_keys, axis=-1, keepdims=True) + 1e-06)
    ).astype(jnp.bfloat16)
    value_blocks = value_rows.reshape(groups, C, head_count, value_width)
    cum_decay = jnp.cumsum(log_decay.reshape(groups, C, head_count), axis=1)
    beta_blocks = beta_gate.reshape(groups, C, head_count)
    row_index = lax.broadcasted_iota(jnp.int32, (C, C), 0)
    column_index = lax.broadcasted_iota(jnp.int32, (C, C), 1)
    cum_heads = jnp.transpose(cum_decay, (0, 2, 1))
    decay_gap = cum_heads[:, :, :, None] - cum_heads[:, :, None, :]
    strict = jnp.exp(jnp.where(row_index > column_index, decay_gap, -jnp.inf))
    inclusive = jnp.exp(jnp.where(row_index >= column_index, decay_gap, -jnp.inf))
    key_gram = jnp.einsum("nthd,nshd->nhts", normed, normed, preferred_element_type=jnp.float32)
    query_gram = jnp.einsum(
        "nthd,nshd->nhts", query_blocks, normed, preferred_element_type=jnp.float32
    )
    lower_part = jnp.transpose(beta_blocks, (0, 2, 1))[:, :, :, None] * strict * key_gram
    scaled_keys = (beta_blocks * jnp.exp(cum_decay))[:, :, :, None] * normed
    scaled_values = beta_blocks[:, :, :, None] * value_blocks
    right_side = jnp.transpose(jnp.concatenate([scaled_keys, scaled_values], axis=-1), (0, 2, 1, 3))
    solved = jax.scipy.linalg.solve_triangular(
        jnp.eye(C, dtype=jnp.float32) + lower_part, right_side, lower=True, unit_diagonal=True
    )
    solved_keys = solved[:, :, :, :key_width]
    solved_values = solved[:, :, :, key_width:]
    query_mix = inclusive * query_gram
    gammas = jnp.exp(cum_decay)
    last_cum = cum_decay[:, -1, :]
    back_keys = jnp.exp(last_cum[:, None, :] - cum_decay)[:, :, :, None] * normed
    keep_mask = 1.0 - doc_start.astype(jnp.float32)
    identity = jnp.eye(key_width, dtype=jnp.float32)
    transition = keep_mask[:, None, None, None] * (
        jnp.exp(last_cum)[:, :, None, None] * identity
        - jnp.einsum("nthd,nhte->nhde", back_keys, solved_keys, precision=PRECISE)
    )
    update = jnp.einsum("nthd,nhte->nhde", back_keys, solved_values, precision=PRECISE)
    eye_state = jnp.broadcast_to(identity, (head_count, key_width, key_width))
    zero_state = jnp.zeros((head_count, key_width, value_width), jnp.float32)

    def extend(carry, group_terms):
        step_matrix, step_update = group_terms
        product = jnp.einsum("hde,hef->hdf", step_matrix, carry[0], precision=PRECISE)
        summed = jnp.einsum("hde,hef->hdf", step_matrix, carry[1], precision=PRECISE) + step_update
        return ((product, summed), carry)

    totals, prefixes = lax.scan(extend, (eye_state, zero_state), (transition, update))
    local_out = jnp.einsum("nhts,nhse->nthe", query_mix, solved_values, precision=PRECISE)
    carried = carried_in(totals, "context", compose, (eye_state, zero_state))[1]
    entering = keep_mask[:, None, None, None] * (
        prefixes[1] + jnp.einsum("nhde,hef->nhdf", prefixes[0], carried, precision=PRECISE)
    )
    core_blocks = local_out + carried_part(query_blocks, gammas, query_mix, solved_keys, entering)
    core_rows = core_blocks.reshape(length, head_count * value_width).astype(jnp.bfloat16)
    returned = lax.all_to_all(core_rows, "head", split_axis=0, concat_axis=1, tiled=True)
    return gated_norm(returned, gate_input, norm_gain)


def solution(mesh):
    return jax.shard_map(
        body,
        mesh=mesh,
        in_specs=(
            P(("context", "head"), None),
            P(("context", "head"), None),
            P(("context", "head"), None),
            P(("context", "head"), None),
            P(("context", "head"), None),
            P(("context", "head"), None),
            P("head"),
            P(),
            P("context"),
        ),
        out_specs=P(("context", "head"), None),
        check_vma=False,
    )
```

profile of v0, /device:TPU:1, one launch (start us, length us, event | category | flops | bytes accessed | tf_op | source)
XLA Modules:
  0.0 596.1 jit_solution(8341804300681900571)
XLA Ops:
  7.9 4.3 all-to-all-start.1
  14.4 2.3 copy.154
  17.8 3.3 all-to-all-start
  21.4 6.3 %fusion.60 = f32[8,64,8]{2,0,1:T(8,128)S(1)} fusion(f32[8,64,8]{2,0,1:T(8,128)S(1)} %copy.104), kind=kOutput, calls=%fused_computation.102 | output fusion | flops 258048 | bytes 32768 | tf_op jit(solution)/shard_map/jit(cumsum)/reduce_window_sum | solution.py:95
  27.8 3.5 all-to-all-start.2
  32.1 12.8 %all-to-all-done.2 = bf16[128,4,1024]{2,0,1:T(8,128)(2,1)S(1)} async-done(((bf16[128,4,1024]{2,0,1:T(8,128)(2,1)}), bf16[128,4,1024]{2,0,1:T(8,128)(2,1)S(1)}, u32[]{:S(2)}, u32[]{:S(2)}) %all-to-all-start.2) | async-done | bytes 1048608 | tf_op jit(solution)/shard_map/all_to_all | solution.py:71
  44.9 5.1 all-to-all-start.3
  51.4 2.4 convert_multiply_fusion.3
  56.0 315.3 %custom-call.4 = f32[8,8,1,64,64]{3,4,2,1,0:T(8,128)} custom-call(f32[8,8,1,64,64]{4,3,2,1,0:T(8,128)S(1)} %fusion.31), custom_call_target="InvertDiagBlocksLowerTriangular" | custom-call | tf_op jit(solution)/shard_map/jit(_solve_triangular)/vmap(vmap())/triangular_solve | solution.py:111
  375.5 4.2 fusion.14
  379.7 8.9 %fusion.18 = f32[8,8,128,128]{3,2,1,0:T(8,128)} fusion(bf16[8,64,8,128]{3,1,2,0:T(8,128)(2,1)S(1)} %copy-done.5, f32[8,8,64,256]{3,2,1,0:T(8,128)S(1)} %fusion.14, f32[8,64,8]{1,2,0:T(8,128)S(1)} %copy.119), kind=kOutput, calls=%fused_computation.33 | convolution fusion | flops 806354944 | bytes 7372800 | tf_op jit(solution)/shard_map/nthd,nhte->nhde/dot_general | solution.py:126
  388.7 9.7 %subtract_multiply_fusion = f32[8,8,128,128]{3,2,1,0:T(8,128)} fusion(bf16[8,64,8,128]{3,1,2,0:T(8,128)(2,1)S(1)} %copy-done.5, f32[128,128]{1,0:T(8,128)S(1)} %fusion.52, f32[8,8]{1,0:T(8,128)S(1)} %fusion.57, f32[8]{0:T(128)S(1)} %convert_subtract_fusion, f32[8,8,64,256]{3,2,1,0:T(8,128)S(1)} %fusion.14, f32[8,64,8]{1,2,0:T(8,128)S(1)} %copy.119), kind=kOutput, calls=%fused_computation.24 | convolution fusion | flops 809500672 | bytes 7442944 | tf_op jit(solution)/shard_map/nthd,nhte->nhde/dot_general | solution.py:124
  398.4 38.4 %while.30 = (s32[]{:T(128)}, f32[8,128,128]{2,1,0:T(8,128)S(1)}, f32[8,128,128]{2,1,0:T(8,128)S(1)}, f32[8,8,128,128]{3,2,1,0:T(8,128)}, f32[8,8,128,128]{3,2,1,...) while((s32[]{:T(128)}, f32[8,128,128]{2,1,0:T(8,128)S(1)}, ...), condition=%wide.region_3.4_spmd.clone, body=%wide.region_2.3_spmd.clone.sunk | while | flops 403046400 | bytes 7866472 | solution.py:136
  439.5 3.6 all-to-all-start.4
  443.2 13.6 %all-to-all-done.4 = bf16[128,4,1024]{2,0,1:T(8,128)(2,1)S(1)} async-done(((bf16[128,4,1024]{2,0,1:T(8,128)(2,1)}), bf16[128,4,1024]{2,0,1:T(8,128)(2,1)S(1)}, u32[]{:S(2)}, u32[]{:S(2)}) %all-to-all-start.4) | async-done | bytes 1048608 | tf_op jit(solution)/shard_map/all_to_all | solution.py:70
  462.5 24.9 %all-gather.5.cloned.1.call-done = bf16[64,128,128]{2,1,0:T(8,128)(2,1)} async-done(((bf16[8,128,128]{2,1,0:T(8,128)(2,1)}), bf16[64,128,128]{2,1,0:T(8,128)(2,1)}) %all-gather.5.cloned.1.call-update) | async-done | bytes 2097168 | tf_op jit(solution)/shard_map/all_gather | solution.py:15
  487.5 49.9 %all-gather.7.cloned.1.call-done = bf16[64,128,128]{2,1,0:T(8,128)(2,1)} async-done(((bf16[8,128,128]{2,1,0:T(8,128)(2,1)}), bf16[64,128,128]{2,1,0:T(8,128)(2,1)}) %all-gather.7.cloned.1.call-update) | async-done | bytes 2097168 | tf_op jit(solution)/shard_map/all_gather | solution.py:15
  537.5 6.6 %fusion.17 = f32[8,8,128,128]{3,2,1,0:T(8,128)S(1)} fusion(f32[8,8,128,128]{3,2,1,0:T(8,128)} %get-tuple-element.89, f32[8,8,128,128]{3,2,1,0:T(8,128)} %get-tuple-element.93, f32[8]{0:T(128)S(1)} %convert_subtract_fusion, f32[8,128,128]{2,1,0:T(8,128)S(1)} %get-tuple-element.92), kind=kOutput, calls=%fused_computation.23 | convolution fusion | flops 1612709888 | bytes 13107232 | tf_op jit(solution)/shard_map/nhde,hef->nhdf/dot_general | solution.py:140
  544.1 4.2 fusion.40
  550.5 2.7 fusion.36
  555.2 5.3 all-to-all-start.5
  561.8 12.3 %all-to-all-done.5 = bf16[4,128,1024]{2,1,0:T(8,128)(2,1)S(1)} async-done(((bf16[4,128,1024]{2,1,0:T(8,128)(2,1)}), bf16[4,128,1024]{2,1,0:T(8,128)(2,1)S(1)}, u32[]{:S(2)}, u32[]{:S(2)}) %all-to-all-start.5) | async-done | bytes 1048608 | tf_op jit(solution)/shard_map/all_to_all | solution.py:144
  575.7 2.9 copy.126
  583.9 2.7 fusion.39
  (138 shorter events, 74.7 us)
Async XLA Ops:
  6.5 555.2 %copy-start = (f32[128]{0:T(128)S(1)}, f32[128]{0:T(128)}, u32[]{:S(2)}) copy-start(f32[128]{0:T(128)} %param.20) | copy-start | bytes 1540
  6.5 10.1 %copy-start.12 = (bf16[128,4096]{1,0:T(8,128)(2,1)S(1)}, bf16[128,4096]{1,0:T(8,128)(2,1)}, u32[]{:S(2)}) copy-start(bf16[128,4096]{1,0:T(8,128)(2,1)} %param.15) | copy-start | bytes 3145732
  7.9 9.8 %all-to-all-start.1 = ((bf16[128,4,8]{0,2,1:T(8,128)(2,1)}), bf16[128,4,8]{0,2,1:T(8,128)(2,1)S(1)}, u32[]{:S(2)}, u32[]{:S(2)}) async-start(bf16[128,4,8]{0,2,1:T(8,128)(2,1)} %convert_bitcast_fusion.2), calls=%async_computation.1 | async-start | bytes 16384 | tf_op jit(solution)/shard_map/all_to_all | solution.py:75
  14.3 6.8 %copy-start.15 = (f32[8]{0:T(128)S(1)}, f32[8]{0:T(128)}, u32[]{:S(2)}) copy-start(f32[8]{0:T(128)} %param.19) | copy-start | bytes 100
  17.8 10.0 %all-to-all-start = ((bf16[128,4,8]{0,2,1:T(8,128)(2,1)}), bf16[128,4,8]{0,2,1:T(8,128)(2,1)S(1)}, u32[]{:S(2)}, u32[]{:S(2)}) async-start(bf16[128,4,8]{0,2,1:T(8,128)(2,1)} %convert_bitcast_fusion.3), calls=%async_computation | async-start | bytes 16384 | tf_op jit(solution)/shard_map/all_to_all | solution.py:78
  27.8 17.1 %all-to-all-start.2 = ((bf16[128,4,1024]{2,0,1:T(8,128)(2,1)}), bf16[128,4,1024]{2,0,1:T(8,128)(2,1)S(1)}, u32[]{:S(2)}, u32[]{:S(2)}) async-start(bf16[128,4,1024]{2,0,1:T(8,128)(2,1)} %bitcast.126), calls=%async_computation.2 | async-start | bytes 2097152 | tf_op jit(solution)/shard_map/all_to_all | solution.py:71
  44.9 326.5 %all-to-all-start.3 = ((bf16[128,4,1024]{2,0,1:T(8,128)(2,1)}), bf16[128,4,1024]{2,0,1:T(8,128)(2,1)}, u32[]{:S(2)}, u32[]{:S(2)}) async-start(bf16[128,4,1024]{2,0,1:T(8,128)(2,1)} %bitcast.125), calls=%async_computation.3 | async-start | bytes 2097152 | tf_op jit(solution)/shard_map/all_to_all | solution.py:72
  50.0 437.5 %all-gather.5.cloned.1.call-start = ((), (), s32[]{:S(2)}) async-start(), calls=%async_computation.6 | async-start | bytes 2359296 | tf_op jit(solution)/shard_map/all_gather | solution.py:15
  53.8 1.0 copy-start.4
  373.3 1.6 copy-start.8
  373.3 2.2 copy-start.11
  375.5 4.2 copy-start.5
  379.7 8.9 %copy-start.1 = (f32[8,8,64,256]{3,2,1,0:T(8,128)}, f32[8,8,64,256]{3,2,1,0:T(8,128)S(1)}, u32[]{:S(2)}) copy-start(f32[8,8,64,256]{3,2,1,0:T(8,128)S(1)} %fusion.14) | copy-start | bytes 12582916
  436.8 1.6 copy-start.13
  437.6 99.8 %all-gather.7.cloned.1.call-start = ((), (), s32[]{:S(2)}) async-start(), calls=%async_computation.7 | async-start | bytes 2359296 | tf_op jit(solution)/shard_map/all_gather | solution.py:15
  439.5 17.3 %all-to-all-start.4 = ((bf16[128,4,1024]{2,0,1:T(8,128)(2,1)}), bf16[128,4,1024]{2,0,1:T(8,128)(2,1)S(1)}, u32[]{:S(2)}, u32[]{:S(2)}) async-start(bf16[128,4,1024]{2,0,1:T(8,128)(2,1)} %bitcast.153), calls=%async_computation.4 | async-start | bytes 2097152 | tf_op jit(solution)/shard_map/all_to_all | solution.py:70
  457.1 1.0 copy-start.9
  457.1 3.3 copy-start.2
  458.1 1.4 copy-start.6
  537.5 6.6 %copy-start.3 = (f32[8,8,64,256]{3,2,1,0:T(8,128)S(1)}, f32[8,8,64,256]{3,2,1,0:T(8,128)}, u32[]{:S(2)}) copy-start(f32[8,8,64,256]{3,2,1,0:T(8,128)} %copy-done.1) | copy-start | bytes 12582916
  544.1 4.2 copy-start.10
  548.3 2.2 copy-start.7
  553.9 6.6 %copy-start.14 = (bf16[128,4096]{1,0:T(8,128)(2,1)S(1)}, bf16[128,4096]{1,0:T(8,128)(2,1)}, u32[]{:S(2)}) copy-start(bf16[128,4096]{1,0:T(8,128)(2,1)} %param.16) | copy-start | bytes 3145732
  555.2 18.9 %all-to-all-start.5 = ((bf16[4,128,1024]{2,1,0:T(8,128)(2,1)}), bf16[4,128,1024]{2,1,0:T(8,128)(2,1)S(1)}, u32[]{:S(2)}, u32[]{:S(2)}) async-start(bf16[4,128,1024]{2,1,0:T(8,128)(2,1)} %convert_element_type.136), calls=%async_computation.5 | async-start | bytes 2097152 | tf_op jit(solution)/shard_map/all_to_all | solution.py:144
Sparse Core Ops, SparseCore 0:
  437.8 49.6 all-gather.4
  489.6 47.7 all-gather.6
where the time goes:
time: 608 us; the launch traced here: 596 us
  other arithmetic  349 us (57%)
  waiting for transfers between devices  114 us (19%)
  matrix products  71 us (12%)
  starting transfers between devices  25.1 us (4%)
  local copies, waits for them, and re-layouts  23 us (4%)
  between operations  14.3 us (2%)
    another operation x2, other arithmetic, body(): jax.scipy.linalg.solve_triangular(jnp.eye(C, dtype=jnp.float32) + lower_p...  315 us
    all_gather x2, waiting for transfers between devices, carried_in(): lax.all_gather(a.astype(kind), axis)  74.9 us
    dot_general x8, matrix products, extend(): jnp.einsum('hde,hef->hdf', step_matrix, carry[1], precision=PRECISE)  14.9 us
    dot_general x8, matrix products, extend(): jnp.einsum('hde,hef->hdf', step_matrix, carry[0], precision=PRECISE)  13.7 us
    all_to_all x1, waiting for transfers between devices, body(): lax.all_to_all(queries, 'head', split_axis=1, concat_axis=0, tiled=True)  13.6 us
    all_to_all x1, waiting for transfers between devices, body(): lax.all_to_all(key_input, 'head', split_axis=1, concat_axis=0, tiled=True)  12.8 us
    all_to_all x1, waiting for transfers between devices, body(): lax.all_to_all(core_rows, 'head', split_axis=0, concat_axis=1, tiled=True)  12.3 us
  transfers between devices with their start and end apart: 8, of which 5 were waited for; matrix products, arithmetic and copies ran while one was open for 57% of the time, Pallas kernels for 0%

commit v1 on v0

v1 whole, which is shorter than its diff:
```python
import functools

import jax
import jax.numpy as jnp
from jax import lax
from jax.experimental import pallas as pl
from jax.experimental.pallas import tpu as pltpu
from jax.sharding import PartitionSpec as P

C = 64
F32 = jnp.float32
BF16 = jnp.bfloat16
EXACT = lax.Precision.HIGHEST
VMEM_BYTES = 40 * 1024 * 1024
MASKED = -1e30


def params():
    return pltpu.CompilerParams(vmem_limit_bytes=VMEM_BYTES)


def cost(flops, moved):
    return pl.CostEstimate(flops=int(flops), bytes_accessed=int(moved), transcendentals=0)


def dot(a, b):
    return jnp.dot(a, b, preferred_element_type=F32)


def dot_t(a, b):
    return lax.dot_general(a, b, (((1,), (1,)), ((), ())), preferred_element_type=F32)


def gates_kernel(parts, width, decay_ref, beta_ref, resets_ref, resets_row_ref, *rest):
    bias_refs, (col_ref, row_ref, gap_ref) = rest[:-3], rest[-3:]
    bias = bias_refs[0][...]
    for ref in bias_refs[1:]:
        bias = bias + ref[...]
    tokens = decay_ref.shape[0]
    z = decay_ref[...] + bias
    log_decay = -(jnp.maximum(z, 0.0) + jnp.log1p(jnp.exp(-jnp.abs(z))))
    row = lax.broadcasted_iota(jnp.int32, (tokens, tokens), 0)
    column = lax.broadcasted_iota(jnp.int32, (tokens, tokens), 1)
    ones = jnp.where(row >= column, 1.0, 0.0).astype(F32)
    cum = jnp.dot(ones, log_decay, precision=EXACT, preferred_element_type=F32)
    beta = 1.0 / (1.0 + jnp.exp(-beta_ref[...]))
    resets = resets_ref[...]
    resets_row = resets_row_ref[...]
    gamma = jnp.exp(cum) * jnp.where(resets == 0.0, 1.0, 0.0)
    cum_row = jnp.transpose(cum)
    last = cum_row[:, tokens - 1 : tokens]
    final = resets_row[:, tokens - 1 : tokens]
    back = jnp.exp(last - cum_row) * jnp.where(resets_row == final, 1.0, 0.0)
    whole = jnp.broadcast_to(jnp.exp(last) * jnp.where(final == 0.0, 1.0, 0.0), cum_row.shape)
    for part in range(parts):
        span = slice(part * width, (part + 1) * width)
        for place, table in enumerate((cum, beta, beta * gamma, gamma)):
            col_ref[part, :, place * width : (place + 1) * width] = table[:, span]
        for place, table in enumerate((cum_row, back, whole)):
            row_ref[part, place * width : (place + 1) * width, :] = table[span, :]
    seen = jnp.logical_and(row >= column, resets == resets_row)
    gap_ref[...] = jnp.where(seen, 0.0, MASKED)


def gates(decay_logit, beta_logit, resets, biases, parts):
    tokens, heads = decay_logit.shape
    width = heads // parts
    return pl.pallas_call(
        functools.partial(gates_kernel, parts, width),
        out_shape=(
            jax.ShapeDtypeStruct((parts, tokens, 4 * width), F32),
            jax.ShapeDtypeStruct((parts, 3 * width, tokens), F32),
            jax.ShapeDtypeStruct((tokens, tokens), F32),
        ),
        compiler_params=params(),
        name="gates",
    )(decay_logit, beta_logit, resets[:, None], resets[None, :], *biases)


def local_kernel(width, half, head_bits, where_ref, col_ref, row_ref, gap_ref, q_ref, k_ref, v_ref, ab_ref, qo_ref):
    tokens = q_ref.shape[0]
    size = q_ref.shape[1] // width
    flip = where_ref[1]
    row = lax.broadcasted_iota(jnp.int32, (tokens, tokens), 0)
    column = lax.broadcasted_iota(jnp.int32, (tokens, tokens), 1)
    apart = jnp.bitwise_xor(row, column)
    eye = jnp.where(row == column, 1.0, 0.0)
    gap = gap_ref[...]
    steps = []
    block = 1
    while block < tokens:
        steps.append(jnp.logical_and(apart >= block, apart < 2 * block))
        block *= 2
    every = range(width)
    normed, lower, mix, inverse = [], [], [], []
    for j in every:
        span = slice(j * size, (j + 1) * size)
        keys = k_ref[:, span].astype(F32)
        keys = (keys * lax.rsqrt(jnp.sum(keys * keys, axis=-1, keepdims=True) + 1e-06)).astype(BF16)
        grams = dot_t(jnp.concatenate([keys, q_ref[:, span]], axis=0), keys)
        decay = jnp.exp(col_ref[0, :, j : j + 1] - row_ref[0, j : j + 1, :] + gap)
        low = col_ref[0, :, width + j : width + j + 1] * decay * grams[:tokens]
        normed.append(keys)
        mix.append((decay * grams[tokens:]).astype(BF16))
        inverse.append(eye - jnp.where(steps[0], low, 0.0))
        lower.append(low.astype(BF16))
    for step in steps[1:]:
        small = [inverse[j].astype(BF16) for j in every]
        inner = [
            dot(jnp.where(step, lower[j], jnp.zeros_like(lower[j])), small[j]).astype(BF16) for j in every
        ]
        inverse = [inverse[j] - dot(small[j], inner[j]) for j in every]
    solved = []
    for j in every:
        span = slice(j * size, (j + 1) * size)
        keys = col_ref[0, :, 2 * width + j : 2 * width + j + 1] * normed[j].astype(F32)
        values = col_ref[0, :, width + j : width + j + 1] * v_ref[:, span].astype(F32)
        right = jnp.concatenate([keys.astype(BF16), values.astype(BF16)], axis=1)
        solved.append(dot(inverse[j].astype(BF16), right).astype(BF16))
    for j in every:
        span = slice(j * size, (j + 1) * size)
        back = jnp.transpose(normed[j].astype(F32)) * row_ref[0, width + j : width + j + 1, :]
        both = dot(jnp.concatenate([back.astype(BF16), mix[j]], axis=0), solved[j])
        whole = eye * row_ref[0, 2 * width + j : 2 * width + j + 1, :]
        through = col_ref[0, :, 3 * width + j : 3 * width + j + 1] * q_ref[:, span].astype(F32)
        place = jnp.bitwise_xor(j // half, flip)
        ab_ref[0, place, j % half, :, :size] = (whole - both[:size, :size]).astype(BF16)
        ab_ref[0, place, j % half, :, size:] = both[:size, size:].astype(BF16)
        qo_ref[0, place, j % half, :, :size] = (through - both[size:, :size]).astype(BF16)
        qo_ref[0, place, j % half, :, size:] = both[size:, size:].astype(BF16)


def local(where, parts, col, rowt, gap, queries, keys, values):
    tokens = queries.shape[0]
    heads = queries.shape[1] // (rowt.shape[0] * rowt.shape[1] // 3)
    width = rowt.shape[1] // 3
    span = queries.shape[1] // rowt.shape[0]
    size = span // width
    half = width // 2
    first, stride = parts[0], parts[1] - parts[0] if len(parts) > 1 else 0
    del heads

    def part(i, where_ref):
        return jnp.bitwise_xor(where_ref[0], first + stride * i)

    strip = pl.BlockSpec((tokens, span), lambda i, w: (0, part(i, w)))
    result = jax.ShapeDtypeStruct((len(parts), 2, half, tokens, 2 * size), BF16)
    result_spec = pl.BlockSpec((1, 2, half, tokens, 2 * size), lambda i, w: (i, 0, 0, 0, 0))
    return pl.pallas_call(
        functools.partial(local_kernel, width, half, None),
        out_shape=(result, result),
        grid_spec=pltpu.PrefetchScalarGridSpec(
            num_scalar_prefetch=1,
            grid=(len(parts),),
            in_specs=[
                pl.BlockSpec((1,) + col.shape[1:], lambda i, w: (part(i, w), 0, 0)),
                pl.BlockSpec((1,) + rowt.shape[1:], lambda i, w: (part(i, w), 0, 0)),
                pl.BlockSpec(gap.shape, lambda i, w: (0, 0)),
                strip,
                strip,
                strip,
            ],
            out_specs=(result_spec, result_spec),
        ),
        compiler_params=params(),
        cost_estimate=cost(len(parts) * width * 6e7, len(parts) * 2**21),
        name="local_tokens",
    )(where, col, rowt, gap, queries, keys, values)


def pick(later, own, received):
    return jnp.where(later, received, own), jnp.where(later, own, received)


def joined(earlier, later):
    size = earlier.shape[0]
    product = dot(later[:, :size], earlier)
    return jnp.concatenate([product[:, :size], product[:, size:] + later[:, size:].astype(F32)], axis=1)


def compose_kernel(bit, where_ref, own_ref, received_ref, out_ref):
    later = where_ref[bit] == 1
    for j in range(own_ref.shape[0]):
        earlier_block, later_block = pick(later, own_ref[j], received_ref[j])
        out_ref[j] = joined(earlier_block, later_block).astype(BF16)


def compose(where, bit, own, received):
    return pl.pallas_call(
        functools.partial(compose_kernel, bit),
        out_shape=jax.ShapeDtypeStruct(own.shape, BF16),
        grid_spec=pltpu.PrefetchScalarGridSpec(
            num_scalar_prefetch=1,
            grid=(1,),
            in_specs=[pl.BlockSpec(own.shape, lambda i, w: (0, 0, 0))] * 2,
            out_specs=pl.BlockSpec(own.shape, lambda i, w: (0, 0, 0)),
        ),
        compiler_params=params(),
        cost_estimate=cost(own.size * 256, own.size * 6),
        name="compose",
    )(where, own, received)


def doubling_kernel(bit, first, where_ref, *refs):
    later = where_ref[bit] == 1
    own_ref, received_ref = refs[:2]
    total_ref, before_ref = refs[-2:]
    heads, size = own_ref.shape[:2]
    row = lax.broadcasted_iota(jnp.int32, (size, 2 * size), 0)
    column = lax.broadcasted_iota(jnp.int32, (size, 2 * size), 1)
    neutral = jnp.where(row == column, 1.0, 0.0).astype(BF16)
    for j in range(heads):
        earlier_block, later_block = pick(later, own_ref[j], received_ref[j])
        total_ref[j] = joined(earlier_block, later_block).astype(BF16)
        if first:
            before_ref[j] = jnp.where(later, received_ref[j], neutral)
        else:
            before = refs[2][j]
            before_ref[j] = jnp.where(later, joined(received_ref[j], before).astype(BF16), before)


def doubling(where, bit, own, received, before):
    first = before is None
    arrays = (own, received) if first else (own, received, before)
    spec = pl.BlockSpec(own.shape, lambda i, w: (0, 0, 0))
    return pl.pallas_call(
        functools.partial(doubling_kernel, bit, first),
        out_shape=(jax.ShapeDtypeStruct(own.shape, BF16),) * 2,
        grid_spec=pltpu.PrefetchScalarGridSpec(
            num_scalar_prefetch=1,
            grid=(1,),
            in_specs=[spec] * len(arrays),
            out_specs=(spec, spec),
        ),
        compiler_params=params(),
        cost_estimate=cost(own.size * 256, own.size * 8),
        name="doubling",
    )(where, *arrays)


def descend_kernel(bits, top, where_ref, *refs):
    count = len(bits)
    start = 2 if top is not None else 1
    blocks = refs[start : start + 2 * count]
    sends = refs[start + 2 * count : start + 3 * count]
    kept_ref = refs[-1]
    size = kept_ref.shape[-1]
    for j in range(kept_ref.shape[0]):
        if top is None:
            state = refs[0][j]
        else:
            before = refs[1][j]
            carried = dot(before[:, :size], refs[0][j]) + before[:, size:].astype(F32)
            state = jnp.where(where_ref[top] == 1, carried.astype(BF16), before[:, size:])
        for level, bit in enumerate(bits):
            later = where_ref[bit] == 1
            earlier = jnp.where(later, blocks[2 * level + 1][j], blocks[2 * level][j])
            after = (dot(earlier[:, :size], state) + earlier[:, size:].astype(F32)).astype(BF16)
            sends[level][j] = jnp.where(later, state, after)
            state = jnp.where(later, after, state)
        kept_ref[j] = state


def descend(where, bits, top, sources, blocks):
    arrays, specs = [], []
    heads, size = sources[0].shape[0], sources[0].shape[1]
    for array in sources:
        arrays.append(array)
        specs.append(pl.BlockSpec(array.shape, lambda i, w: (0, 0, 0)))
    for pair in blocks:
        for array, index in pair:
            arrays.append(array)
            lead = (None,) * len(index)
            specs.append(
                pl.BlockSpec(lead + array.shape[len(index) :], lambda i, w, index=index: index + (0, 0, 0))
            )
    spec = pl.BlockSpec((heads, size, size), lambda i, w: (0, 0, 0))
    outs = len(bits) + 1
    return pl.pallas_call(
        functools.partial(descend_kernel, bits, top),
        out_shape=(jax.ShapeDtypeStruct((heads, size, size), BF16),) * outs,
        grid_spec=pltpu.PrefetchScalarGridSpec(
            num_scalar_prefetch=1,
            grid=(1,),
            in_specs=specs,
            out_specs=(spec,) * outs,
        ),
        compiler_params=params(),
        cost_estimate=cost(outs * heads * 2 * size**3, outs * heads * 2**17),
        name="descend",
    )(where, *arrays)


def finish_kernel(has_previous, where_ref, state_ref, qo_ref, gate_ref, gain_ref, *rest):
    out_ref = rest[-1]
    size = state_ref.shape[-1]
    for j in range(state_ref.shape[0]):
        span = slice(j * size, (j + 1) * size)
        core = dot(qo_ref[j, :, :size], state_ref[j]) + qo_ref[j, :, size:].astype(F32)
        core = core.astype(BF16).astype(F32)
        scaled = core * lax.rsqrt(jnp.mean(core * core, axis=-1, keepdims=True) + 1e-06)
        gate = gate_ref[:, span].astype(F32)
        out_ref[:, span] = (scaled * gain_ref[...] * (gate / (1.0 + jnp.exp(-gate)))).astype(BF16)


def finish(where, part, turn, place, state, qo, gate, gain, previous):
    half, tokens, size = state.shape[0], gate.shape[0], state.shape[-1]

    def strip(i, w):
        return 0, 2 * jnp.bitwise_xor(w[0], part) + jnp.bitwise_xor(w[1], turn)

    specs = [
        pl.BlockSpec(state.shape, lambda i, w: (0, 0, 0)),
        pl.BlockSpec((None, None) + qo.shape[2:], lambda i, w: (place, turn, 0, 0, 0)),
        pl.BlockSpec((tokens, half * size), strip),
        pl.BlockSpec(gain.shape, lambda i, w: (0, 0)),
    ]
    arrays = [state, qo, gate, gain]
    aliases = {}
    if previous is not None:
        specs.append(pl.BlockSpec(memory_space=pl.ANY))
        arrays.append(previous)
        aliases = {len(arrays): 0}
    return pl.pallas_call(
        functools.partial(finish_kernel, previous is not None),
        out_shape=jax.ShapeDtypeStruct(gate.shape, BF16),
        grid_spec=pltpu.PrefetchScalarGridSpec(
            num_scalar_prefetch=1,
            grid=(1,),
            in_specs=specs,
            out_specs=pl.BlockSpec((tokens, half * size), strip),
        ),
        input_output_aliases=aliases,
        compiler_params=params(),
        cost_estimate=cost(half * 2 * tokens * size * size, half * 2**17),
        name="finish",
    )(where, *arrays)


def body(
    head_count,
    context_count,
    queries,
    key_input,
    value_input,
    gate_input,
    decay_logit,
    beta_logit,
    decay_bias,
    norm_gain,
    doc_start,
):
    place = lax.axis_index("head")
    block = lax.axis_index("context")
    tokens, heads = decay_logit.shape
    width = heads // head_count
    groups = tokens // C
    head_bits = head_count.bit_length() - 1
    context_bits = context_count.bit_length() - 1

    def swap(array, axis, distance):
        count = head_count if axis == "head" else context_count
        return lax.ppermute(array, axis, [(i, i ^ distance) for i in range(count)])

    where = jnp.stack(
        [place, block & 1]
        + [(place >> bit) & 1 for bit in range(head_bits)]
        + [(block >> bit) & 1 for bit in range(context_bits)]
    ).astype(jnp.int32)
    head_bit = [2 + bit for bit in range(head_bits)]
    context_bit = [2 + head_bits + bit for bit in range(context_bits)]

    mine = jnp.where(
        lax.broadcasted_iota(jnp.int32, (head_count, width), 0) == place, decay_bias[None, :], 0.0
    ).reshape(1, heads)
    biases = [mine] + [swap(mine, "head", other) for other in range(1, head_count)]
    starts = lax.dynamic_slice(doc_start, (place * groups,), (groups,)).astype(F32)
    resets = jnp.repeat(jnp.cumsum(starts), C)
    col, rowt, gap = gates(decay_logit, beta_logit, resets, biases, head_count)

    odd = list(range(head_count - 1, 0, -2))
    even = [part - 1 for part in odd]
    qo = {}
    ab_odd, qo_odd = local(where, odd, col, rowt, gap, queries, key_input, value_input)
    ab_even, qo_even = local(where, even, col, rowt, gap, queries, key_input, value_input)
    for index, part in enumerate(odd):
        qo[part] = (qo_odd, index)
    for index, part in enumerate(even):
        qo[part] = (qo_even, index)

    half, size = ab_even.shape[2], ab_even.shape[3]
    flat = lambda a: a.reshape((-1,) + a.shape[-2:])
    levels = []
    own = {part: (ab_even, (index,)) for index, part in enumerate(even)}
    received = swap(ab_odd, "head", 1)
    got = {part: (received, (index,)) for index, part in enumerate(even)}
    levels.append((own, got))
    blocks = compose(where, head_bit[0], flat(ab_even), flat(received)).reshape(ab_even.shape)
    current = {part: blocks[index] for index, part in enumerate(even)}
    for bit in range(1, head_bits):
        own, got = {}, {}
        following = {}
        for part in sorted(current):
            if part >> bit & 1:
                continue
            arrived = swap(current[part | 1 << bit], "head", 1 << bit)
            own[part] = (current[part], ())
            got[part] = (arrived, ())
            following[part] = compose(
                where, head_bit[bit], flat(current[part]), flat(arrived)
            ).reshape(arrived.shape)
        levels.append((own, got))
        current = following
    mine = current[0]
    arrived = swap(mine[1], "context", 1)
    x_pair = ((mine[0], ()), (arrived, ()))
    total = compose(where, context_bit[0], mine[0], arrived)
    before = None
    for bit in range(1, context_bits - 1):
        other = swap(total, "context", 1 << bit)
        total, before = doubling(where, context_bit[bit], total, other, before)
    top = context_bit[-1]
    other = swap(total[:, :, size:], "context", 1 << (context_bits - 1))

    def pair(bit, part, turn):
        own, got = levels[bit]
        (a, ai), (b, bi) = own[part], got[part]
        return (a, ai + (turn,)), (b, bi + (turn,))

    states = {}
    waiting = {}
    bits = [context_bit[0]] + [head_bit[bit] for bit in reversed(range(head_bits))]
    outs = descend(
        where,
        bits,
        top,
        (other, before),
        [x_pair] + [pair(bit, 0, 0) for bit in reversed(range(head_bits))],
    )
    states[0, 0] = outs[-1]
    waiting[0, 1] = (head_bits, swap(outs[0], "context", 1))
    for level, bit in enumerate(reversed(range(head_bits))):
        waiting[1 << bit, 0] = (bit, swap(outs[1 + level], "head", 1 << bit))
    while waiting:
        key = max(waiting, key=lambda entry: (waiting[entry][0], entry[1]))
        part, turn = key
        below, state = waiting.pop(key)
        if below == 0:
            states[key] = state
            continue
        bits = [head_bit[bit] for bit in reversed(range(below))]
        outs = descend(where, bits, None, (state,), [pair(bit, part, turn) for bit in reversed(range(below))])
        states[key] = outs[-1]
        for level, bit in enumerate(reversed(range(below))):
            waiting[part | 1 << bit, turn] = (bit, swap(outs[level], "head", 1 << bit))

    result = None
    gain = norm_gain[None, :]
    order = sorted(states, key=lambda entry: (bin(entry[0]).count("1") + entry[1], entry))
    for part, turn in order:
        source, index = qo[part]
        result = finish(where, part, turn, index, states[part, turn], source, gate_input, gain, result)
    return result


def solution(mesh):
    return jax.shard_map(
        functools.partial(body, mesh.shape["head"], mesh.shape["context"]),
        mesh=mesh,
        in_specs=(
            P(("context", "head"), None),
            P(("context", "head"), None),
            P(("context", "head"), None),
            P(("context", "head"), None),
            P(("context", "head"), None),
            P(("context", "head"), None),
            P("head"),
            P(),
            P("context"),
        ),
        out_specs=P(("context", "head"), None),
        check_vma=False,
    )
```

time: 608 us -> 91.2 us (0.15); the launches traced: 596 us -> 90.8 us
  other arithmetic: 349 us -> 0.33 us
  waiting for transfers between devices: 114 us -> 26.2 us
  matrix products: 71 us -> 0 us
  Pallas kernels: 0 us -> 33.7 us
  local copies, waits for them, and re-layouts: 23 us -> 7.62 us
  between operations: 14.3 us -> 0.18 us
    another operation x5 -> x2, other arithmetic: 322 us -> 0.25 us  [the longest x2 315 us: body(): jax.scipy.linalg.solve_triangular(jnp.eye(C, dtype=jnp.float32) + lower_p...]
    all_gather x2 -> x0, waiting for transfers between devices: 74.9 us -> none  [carried_in(): lax.all_gather(a.astype(kind), axis)]
    dot_general x25 -> x0, matrix products: 66.8 us -> none  [the longest x8 14.9 us: extend(): jnp.einsum('hde,hef->hdf', step_matrix, carry[1], precision=PRECISE)]
    all_to_all x6 -> x0, waiting for transfers between devices: 38.6 us -> none  [the longest x1 13.6 us: body(): lax.all_to_all(queries, 'head', split_axis=1, concat_axis=0, tiled=True)]
    pallas_call x0 -> x19, Pallas kernels: none -> 33.7 us  [the longest x2 13.3 us: local(): pl.pallas_call(functools.partial(local_kernel, width, half, None), out_sh...]
    ppermute x0 -> x15, waiting for transfers between devices: none -> 26.2 us  [swap(): return lax.ppermute(array, axis, [(i, i ^ distance) for i in range(count)])]
    all_to_all x6 -> x0, starting transfers between devices: 25.1 us -> none  [the longest x1 5.26 us: body(): lax.all_to_all(core_rows, 'head', split_axis=0, concat_axis=1, tiled=True)]
    ppermute x0 -> x15, starting transfers between devices: none -> 22.8 us  [swap(): return lax.ppermute(array, axis, [(i, i ^ distance) for i in range(count)])]
  transfers between devices with their start and end apart: 8 -> 15, of which waited for: 5 -> 5; matrix products, arithmetic and copies ran while one was open for 57% -> 1% of each run, Pallas kernels for 0% -> 22%
where the time goes in v1:
time: 91.2 us; the launch traced here: 90.8 us
  Pallas kernels  33.7 us (37%)
  waiting for transfers between devices  26.2 us (29%)
  starting transfers between devices  22.8 us (25%)
  local copies, waits for them, and re-layouts  7.62 us (8%)
    ppermute x15, waiting for transfers between devices, swap(): return lax.ppermute(array, axis, [(i, i ^ distance) for i in range(count)])  26.2 us
    ppermute x15, starting transfers between devices, swap(): return lax.ppermute(array, axis, [(i, i ^ distance) for i in range(count)])  22.8 us
    pallas_call x2, Pallas kernels, local(): pl.pallas_call(functools.partial(local_kernel, width, half, None), out_sh...  13.3 us
    pallas_call x8, Pallas kernels, finish(): pl.pallas_call(functools.partial(finish_kernel, previous is not None), ou...  12.1 us
    unnamed x20, local copies, waits for them, and re-layouts  7.01 us
    pallas_call x4, Pallas kernels, descend(): pl.pallas_call(functools.partial(descend_kernel, bits, top), out_shape=(j...  4.31 us
    pallas_call x3, Pallas kernels, compose(): pl.pallas_call(functools.partial(compose_kernel, bit), out_shape=jax.Shap...  2.6 us
  transfers between devices with their start and end apart: 15, of which 5 were waited for; matrix products, arithmetic and copies ran while one was open for 1% of the time, Pallas kernels for 22%

profile of v1, /device:TPU:1, one launch (start us, length us, event | category | flops | bytes accessed | tf_op | source)
XLA Modules:
  0.0 90.8 jit_solution(463569035485134913)
XLA Ops:
  0.8 2.6 %collective-permute-start.2 = (f32[1,32]{1,0:T(1,128)S(1)}, f32[1,32]{1,0:T(1,128)S(1)}, u32[]{:S(2)}, u32[]{:S(2)}) collective-permute-start(f32[1,32]{1,0:T(1,128)S(1)} %select_n.19.rest_0_), channel_id=1, source_target_pairs={{0,3},{1,2},{2,1},{3,0},{4,7},{5,6},{6,5},{7,4},{8,11},{9,10},{10,... | collective-permute-start | bytes 392 | tf_op jit(solution)/shard_map/ppermute | solution.py:363
  10.8 6.7 %local_tokens.3 = (bf16[2,2,4,128,256]{4,3,2,1,0:T(8,128)(2,1)S(1)}, bf16[2,2,4,128,256]{4,3,2,1,0:T(8,128)(2,1)S(1)}) custom-call(s32[7]{0:T(128)S(1)} %stack.31.where_ref, f32[4,128,32]{2,1,0:T(8,128)S(1)} %get-tuple-element.25.col_ref, f32[4,24,128]{2,1,0:T(8,128)S(1)} %get-tuple-element.26.row_ref, f32[128,128]{1,0:T(8,128)S(1)} %get-tuple-element.27.gap_ref, ...), custom_call_target="tpu_custom_call" | custom-call | flops 960000000 | bytes 4194304 | tf_op jit(solution)/shard_map/local_tokens/pallas_call | solution.py:149
  17.8 6.7 %local_tokens.2 = (bf16[2,2,4,128,256]{4,3,2,1,0:T(8,128)(2,1)S(1)}, bf16[2,2,4,128,256]{4,3,2,1,0:T(8,128)(2,1)S(1)}) custom-call(s32[7]{0:T(128)S(1)} %stack.31.where_ref, f32[4,128,32]{2,1,0:T(8,128)S(1)} %get-tuple-element.25.col_ref, f32[4,24,128]{2,1,0:T(8,128)S(1)} %get-tuple-element.26.row_ref, f32[128,128]{1,0:T(8,128)S(1)} %get-tuple-element.27.gap_ref, ...), custom_call_target="tpu_custom_call" | custom-call | flops 960000000 | bytes 4194304 | tf_op jit(solution)/shard_map/local_tokens/pallas_call | solution.py:149
  25.6 1.4 %collective-permute-start.4 = (bf16[2,4,128,256]{3,2,1,0:T(8,128)(2,1)S(1)}, bf16[2,4,128,256]{3,2,1,0:T(8,128)(2,1)S(1)}, u32[]{:S(2)}, u32[]{:S(2)}) collective-permute-start(bf16[2,4,128,256]{3,2,1,0:T(8,128)(2,1)S(1)} %bitcast.29), channel_id=1, source_target_pairs={{0,2},{1,3},{2,0},{3,1},{4,6},{5,7},{6,4},{7,5},{8,10},{9,11},{10,... | collective-permute-start | bytes 1572872 | tf_op jit(solution)/shard_map/ppermute | solution.py:363
  27.0 11.9 %collective-permute-done.4.refs_5_.refs_2_ = bf16[2,4,128,256]{3,2,1,0:T(8,128)(2,1)S(1)} collective-permute-done((bf16[2,4,128,256]{3,2,1,0:T(8,128)(2,1)S(1)}, bf16[2,4,128,256]{3,2,1,0:T(8,128)(2,1)S(1)}, u32[]{:S(2)}, u32[]{:S(2)}) %collective-permute-start.4) | collective-permute-done | bytes 524320 | tf_op jit(solution)/shard_map/ppermute | solution.py:363
  39.8 1.4 %collective-permute-start.5 = (bf16[4,128,256]{2,1,0:T(8,128)(2,1)S(1)}, bf16[4,128,256]{2,1,0:T(8,128)(2,1)S(1)}, u32[]{:S(2)}, u32[]{:S(2)}) collective-permute-start(bf16[4,128,256]{2,1,0:T(8,128)(2,1)S(1)} %get-tuple-element.47), channel_id=1, source_target_pairs={{0,4},{4,0},{8,12},{12,8},{16,20},{20,16},{24,28},{28,24},{1,5},{5... | collective-permute-start | bytes 786440 | tf_op jit(solution)/shard_map/ppermute | solution.py:363
  41.2 5.4 %collective-permute-done.5.received_ref.refs_3_ = bf16[4,128,256]{2,1,0:T(8,128)(2,1)S(1)} collective-permute-done((bf16[4,128,256]{2,1,0:T(8,128)(2,1)S(1)}, bf16[4,128,256]{2,1,0:T(8,128)(2,1)S(1)}, u32[]{:S(2)}, u32[]{:S(2)}) %collective-permute-start.5) | collective-permute-done | bytes 262176 | tf_op jit(solution)/shard_map/ppermute | solution.py:363
  47.3 1.6 %collective-permute-start.6 = (bf16[4,128,256]{2,1,0:T(8,128)(2,1)S(1)}, bf16[4,128,256]{2,1,0:T(8,128)(2,1)S(1)}, u32[]{:S(2)}, u32[]{:S(2)}) collective-permute-start(bf16[4,128,256]{2,1,0:T(8,128)(2,1)S(1)} %compose.5.refs_0_), channel_id=1, source_target_pairs={{0,8},{4,12},{8,0},{12,4},{16,24},{20,28},{24,16},{28,20},{1,9},{5... | collective-permute-start | bytes 786440 | tf_op jit(solution)/shard_map/ppermute | solution.py:363
  48.9 4.4 %collective-permute-done.6.refs_1_ = bf16[4,128,256]{2,1,0:T(8,128)(2,1)S(1)} collective-permute-done((bf16[4,128,256]{2,1,0:T(8,128)(2,1)S(1)}, bf16[4,128,256]{2,1,0:T(8,128)(2,1)S(1)}, u32[]{:S(2)}, u32[]{:S(2)}) %collective-permute-start.6) | collective-permute-done | bytes 262176 | tf_op jit(solution)/shard_map/ppermute | solution.py:363
  54.1 2.5 %collective-permute-start.7 = (bf16[4,128,128]{2,1,0:T(8,128)(2,1)S(1)}, bf16[4,128,128]{2,1,0:T(8,128)(2,1)S(1)}, u32[]{:S(2)}, u32[]{:S(2)}) collective-permute-start(bf16[4,128,128]{2,1,0:T(8,128)(2,1)S(1)} %slice.24), channel_id=1, source_target_pairs={{0,16},{4,20},{8,24},{12,28},{16,0},{20,4},{24,8},{28,12},{1,17},{... | collective-permute-start | bytes 393224 | tf_op jit(solution)/shard_map/ppermute | solution.py:363
  56.6 3.8 %collective-permute-done.7.refs_0_ = bf16[4,128,128]{2,1,0:T(8,128)(2,1)S(1)} collective-permute-done((bf16[4,128,128]{2,1,0:T(8,128)(2,1)S(1)}, bf16[4,128,128]{2,1,0:T(8,128)(2,1)S(1)}, u32[]{:S(2)}, u32[]{:S(2)}) %collective-permute-start.7) | collective-permute-done | bytes 131104 | tf_op jit(solution)/shard_map/ppermute | solution.py:363
  60.3 2.0 %descend.4 = (bf16[4,128,128]{2,1,0:T(8,128)(2,1)S(1)}, bf16[4,128,128]{2,1,0:T(8,128)(2,1)S(1)}, bf16[4,128,128]{2,1,0:T(8,128)(2,1)S(1)}, bf16[4,128,128]{2,1,0:T(8,128)(2,1)S(1)}) custom-call(s32[7]{0:T(128)S(1)} %stack.31.where_ref, bf16[4,128,128]{2,1,0:T(8,128)(2,1)S(1)} %collective-permute-done.7.refs_0_, ...), custom_call_target="tpu_custom_call" | custom-call | flops 67108864 | bytes 2097152 | tf_op jit(solution)/shard_map/descend/pallas_call | solution.py:279
  63.6 1.8 %collective-permute-start.11 = (bf16[4,128,128]{2,1,0:T(8,128)(2,1)S(1)}, bf16[4,128,128]{2,1,0:T(8,128)(2,1)S(1)}, u32[]{:S(2)}, u32[]{:S(2)}) collective-permute-start(bf16[4,128,128]{2,1,0:T(8,128)(2,1)S(1)} %get-tuple-element.36), channel_id=1, source_target_pairs={{0,2},{1,3},{2,0},{3,1},{4,6},{5,7},{6,4},{7,5},{8,10},{9,11},{10,... | collective-permute-start | bytes 393224 | tf_op jit(solution)/shard_map/ppermute | solution.py:363
  67.1 2.0 %collective-permute-start.9 = (bf16[4,128,128]{2,1,0:T(8,128)(2,1)S(1)}, bf16[4,128,128]{2,1,0:T(8,128)(2,1)S(1)}, u32[]{:S(2)}, u32[]{:S(2)}) collective-permute-start(bf16[4,128,128]{2,1,0:T(8,128)(2,1)S(1)} %get-tuple-element.33), channel_id=1, source_target_pairs={{0,2},{1,3},{2,0},{3,1},{4,6},{5,7},{6,4},{7,5},{8,10},{9,11},{10,... | collective-permute-start | bytes 393224 | tf_op jit(solution)/shard_map/ppermute | solution.py:363
  69.0 5.3 %collective-permute-start.14 = (bf16[4,128,128]{2,1,0:T(8,128)(2,1)S(1)}, bf16[4,128,128]{2,1,0:T(8,128)(2,1)S(1)}, u32[]{:S(2)}, u32[]{:S(2)}) collective-permute-start(bf16[4,128,128]{2,1,0:T(8,128)(2,1)S(1)} %get-tuple-element.42), channel_id=1, source_target_pairs={{0,1},{1,0},{2,3},{3,2},{4,5},{5,4},{6,7},{7,6},{8,9},{9,8},{10,11... | collective-permute-start | bytes 393224 | tf_op jit(solution)/shard_map/ppermute | solution.py:363
  76.4 1.7 %collective-permute-start.10 = (bf16[4,128,128]{2,1,0:T(8,128)(2,1)S(1)}, bf16[4,128,128]{2,1,0:T(8,128)(2,1)S(1)}, u32[]{:S(2)}, u32[]{:S(2)}) collective-permute-start(bf16[4,128,128]{2,1,0:T(8,128)(2,1)S(1)} %get-tuple-element.34), channel_id=1, source_target_pairs={{0,1},{1,0},{2,3},{3,2},{4,5},{5,4},{6,7},{7,6},{8,9},{9,8},{10,11... | collective-permute-start | bytes 393224 | tf_op jit(solution)/shard_map/ppermute | solution.py:363
  78.7 1.5 %finish.8.rest_0_ = bf16[128,4096]{1,0:T(8,128)(2,1)} custom-call(s32[7]{0:T(128)S(1)} %stack.31.where_ref, bf16[4,128,128]{2,1,0:T(8,128)(2,1)S(1)} %get-tuple-element.44.state_ref, bf16[2,2,4,128,256]{4,3,2,1,0:T(8,128)(2,1)S(1)} %get-tuple-element.39.qo_ref, bf16[128,4096]{1,0:T(8,128)(2,1)S(1)} %copy-done, f32[1,128]{1,0:T(1,128)S(1)} %bitcast.21), custom_call_target="tpu_custom_call" | custom-call | flops 16777216 | bytes 524288 | tf_op jit(solution)/shard_map/finish/pallas_call | solution.py:324
  80.2 1.5 %finish.9.rest_0_ = bf16[128,4096]{1,0:T(8,128)(2,1)} custom-call(s32[7]{0:T(128)S(1)} %stack.31.where_ref, bf16[4,128,128]{2,1,0:T(8,128)(2,1)S(1)} %get-tuple-element.43.state_ref, bf16[2,2,4,128,256]{4,3,2,1,0:T(8,128)(2,1)S(1)} %get-tuple-element.39.qo_ref, bf16[128,4096]{1,0:T(8,128)(2,1)S(1)} %copy-done, ...), custom_call_target="tpu_custom_call", output_to_operand_aliasing={{}: (5, {})} | custom-call | flops 16777216 | bytes 524288 | tf_op jit(solution)/shard_map/finish/pallas_call | solution.py:324
  81.7 1.5 %finish.10.rest_0_ = bf16[128,4096]{1,0:T(8,128)(2,1)} custom-call(s32[7]{0:T(128)S(1)} %stack.31.where_ref, bf16[4,128,128]{2,1,0:T(8,128)(2,1)S(1)} %collective-permute-done.14.state_ref, bf16[2,2,4,128,256]{4,3,2,1,0:T(8,128)(2,1)S(1)} %get-tuple-element.35.qo_ref, bf16[128,4096]{1,0:T(8,128)(2,1)S(1)} %copy-done, ...), custom_call_target="tpu_custom_call", output_to_operand_aliasing={{}: (5, {})} | custom-call | flops 16777216 | bytes 524288 | tf_op jit(solution)/shard_map/finish/pallas_call | solution.py:324
  83.3 1.5 %finish.11.rest_0_ = bf16[128,4096]{1,0:T(8,128)(2,1)} custom-call(s32[7]{0:T(128)S(1)} %stack.31.where_ref, bf16[4,128,128]{2,1,0:T(8,128)(2,1)S(1)} %get-tuple-element.41.state_ref, bf16[2,2,4,128,256]{4,3,2,1,0:T(8,128)(2,1)S(1)} %get-tuple-element.39.qo_ref, bf16[128,4096]{1,0:T(8,128)(2,1)S(1)} %copy-done, ...), custom_call_target="tpu_custom_call", output_to_operand_aliasing={{}: (5, {})} | custom-call | flops 16777216 | bytes 524288 | tf_op jit(solution)/shard_map/finish/pallas_call | solution.py:324
  84.8 1.5 %finish.12.rest_0_ = bf16[128,4096]{1,0:T(8,128)(2,1)} custom-call(s32[7]{0:T(128)S(1)} %stack.31.where_ref, bf16[4,128,128]{2,1,0:T(8,128)(2,1)S(1)} %collective-permute-done.13.state_ref, bf16[2,2,4,128,256]{4,3,2,1,0:T(8,128)(2,1)S(1)} %get-tuple-element.35.qo_ref, bf16[128,4096]{1,0:T(8,128)(2,1)S(1)} %copy-done, ...), custom_call_target="tpu_custom_call", output_to_operand_aliasing={{}: (5, {})} | custom-call | flops 16777216 | bytes 524288 | tf_op jit(solution)/shard_map/finish/pallas_call | solution.py:324
  86.3 1.5 %finish.13.rest_0_ = bf16[128,4096]{1,0:T(8,128)(2,1)} custom-call(s32[7]{0:T(128)S(1)} %stack.31.where_ref, bf16[4,128,128]{2,1,0:T(8,128)(2,1)S(1)} %get-tuple-element.38.state_ref, bf16[2,2,4,128,256]{4,3,2,1,0:T(8,128)(2,1)S(1)} %get-tuple-element.39.qo_ref, bf16[128,4096]{1,0:T(8,128)(2,1)S(1)} %copy-done, ...), custom_call_target="tpu_custom_call", output_to_operand_aliasing={{}: (5, {})} | custom-call | flops 16777216 | bytes 524288 | tf_op jit(solution)/shard_map/finish/pallas_call | solution.py:324
  87.8 1.5 %finish.14.rest_0_ = bf16[128,4096]{1,0:T(8,128)(2,1)} custom-call(s32[7]{0:T(128)S(1)} %stack.31.where_ref, bf16[4,128,128]{2,1,0:T(8,128)(2,1)S(1)} %collective-permute-done.12.state_ref, bf16[2,2,4,128,256]{4,3,2,1,0:T(8,128)(2,1)S(1)} %get-tuple-element.35.qo_ref, bf16[128,4096]{1,0:T(8,128)(2,1)S(1)} %copy-done, ...), custom_call_target="tpu_custom_call", output_to_operand_aliasing={{}: (5, {})} | custom-call | flops 16777216 | bytes 524288 | tf_op jit(solution)/shard_map/finish/pallas_call | solution.py:324
  89.3 1.5 %finish.15 = bf16[128,4096]{1,0:T(8,128)(2,1)} custom-call(s32[7]{0:T(128)S(1)} %stack.31.where_ref, bf16[4,128,128]{2,1,0:T(8,128)(2,1)S(1)} %collective-permute-done.10.state_ref, bf16[2,2,4,128,256]{4,3,2,1,0:T(8,128)(2,1)S(1)} %get-tuple-element.35.qo_ref, bf16[128,4096]{1,0:T(8,128)(2,1)S(1)} %copy-done, ...), custom_call_target="tpu_custom_call", output_to_operand_aliasing={{}: (5, {})} | custom-call | flops 16777216 | bytes 524288 | tf_op jit(solution)/shard_map/finish/pallas_call | solution.py:324
  (57 shorter events, 17.6 us)
Async XLA Ops:
  0.0 0.7 copy-start.7
  0.8 5.8 %collective-permute-start.2 = (f32[1,32]{1,0:T(1,128)S(1)}, f32[1,32]{1,0:T(1,128)S(1)}, u32[]{:S(2)}, u32[]{:S(2)}) collective-permute-start(f32[1,32]{1,0:T(1,128)S(1)} %select_n.19.rest_0_), channel_id=1, source_target_pairs={{0,3},{1,2},{2,1},{3,0},{4,7},{5,6},{6,5},{7,4},{8,11},{9,10},{10,... | collective-permute-start | bytes 392 | tf_op jit(solution)/shard_map/ppermute | solution.py:363
  3.4 3.2 %collective-permute-start.1 = (f32[1,32]{1,0:T(1,128)S(1)}, f32[1,32]{1,0:T(1,128)S(1)}, u32[]{:S(2)}, u32[]{:S(2)}) collective-permute-start(f32[1,32]{1,0:T(1,128)S(1)} %select_n.19.rest_0_), channel_id=1, source_target_pairs={{0,2},{1,3},{2,0},{3,1},{4,6},{5,7},{6,4},{7,5},{8,10},{9,11},{10,... | collective-permute-start | bytes 392 | tf_op jit(solution)/shard_map/ppermute | solution.py:363
  3.4 3.2 %collective-permute-start = (f32[1,32]{1,0:T(1,128)S(1)}, f32[1,32]{1,0:T(1,128)S(1)}, u32[]{:S(2)}, u32[]{:S(2)}) collective-permute-start(f32[1,32]{1,0:T(1,128)S(1)} %select_n.19.rest_0_), channel_id=1, source_target_pairs={{0,1},{1,0},{2,3},{3,2},{4,5},{5,4},{6,7},{7,6},{8,9},{9,8},{10,11... | collective-permute-start | bytes 392 | tf_op jit(solution)/shard_map/ppermute | solution.py:363
  3.9 0.7 copy-start.8
  5.0 0.7 copy-start.5
  5.7 0.7 copy-start.6
  7.2 1.2 %copy-start.2 = (bf16[128,4096]{1,0:T(8,128)(2,1)S(1)}, bf16[128,4096]{1,0:T(8,128)(2,1)}, u32[]{:S(2)}) copy-start(bf16[128,4096]{1,0:T(8,128)(2,1)} %q_ref.3) | copy-start | bytes 3145732
  8.4 1.2 %copy-start.3 = (bf16[128,4096]{1,0:T(8,128)(2,1)S(1)}, bf16[128,4096]{1,0:T(8,128)(2,1)}, u32[]{:S(2)}) copy-start(bf16[128,4096]{1,0:T(8,128)(2,1)} %k_ref.3) | copy-start | bytes 3145732
  9.6 1.2 %copy-start.4 = (bf16[128,4096]{1,0:T(8,128)(2,1)S(1)}, bf16[128,4096]{1,0:T(8,128)(2,1)}, u32[]{:S(2)}) copy-start(bf16[128,4096]{1,0:T(8,128)(2,1)} %v_ref.3) | copy-start | bytes 3145732
  17.5 7.0 %collective-permute-start.3 = (bf16[2,2,4,128,256]{4,3,2,1,0:T(8,128)(2,1)S(1)}, bf16[2,2,4,128,256]{4,3,2,1,0:T(8,128)(2,1)S(1)}, u32[]{:S(2)}, u32[]{:S(2)}) collective-permute-start(bf16[2,2,4,128,256]{4,3,2,1,0:T(8,128)(2,1)S(1)} %get-tuple-element.29), channel_id=1, source_target_pairs={{0,1},{1,0},{2,3},{3,2},{4,5},{5,4},{6,7},{7,6},{8,9},{9,8},{10,11... | collective-permute-start | bytes 3145736 | tf_op jit(solution)/shard_map/ppermute | solution.py:363
  25.6 13.3 %collective-permute-start.4 = (bf16[2,4,128,256]{3,2,1,0:T(8,128)(2,1)S(1)}, bf16[2,4,128,256]{3,2,1,0:T(8,128)(2,1)S(1)}, u32[]{:S(2)}, u32[]{:S(2)}) collective-permute-start(bf16[2,4,128,256]{3,2,1,0:T(8,128)(2,1)S(1)} %bitcast.29), channel_id=1, source_target_pairs={{0,2},{1,3},{2,0},{3,1},{4,6},{5,7},{6,4},{7,5},{8,10},{9,11},{10,... | collective-permute-start | bytes 1572872 | tf_op jit(solution)/shard_map/ppermute | solution.py:363
  39.8 6.8 %collective-permute-start.5 = (bf16[4,128,256]{2,1,0:T(8,128)(2,1)S(1)}, bf16[4,128,256]{2,1,0:T(8,128)(2,1)S(1)}, u32[]{:S(2)}, u32[]{:S(2)}) collective-permute-start(bf16[4,128,256]{2,1,0:T(8,128)(2,1)S(1)} %get-tuple-element.47), channel_id=1, source_target_pairs={{0,4},{4,0},{8,12},{12,8},{16,20},{20,16},{24,28},{28,24},{1,5},{5... | collective-permute-start | bytes 786440 | tf_op jit(solution)/shard_map/ppermute | solution.py:363
  47.3 6.0 %collective-permute-start.6 = (bf16[4,128,256]{2,1,0:T(8,128)(2,1)S(1)}, bf16[4,128,256]{2,1,0:T(8,128)(2,1)S(1)}, u32[]{:S(2)}, u32[]{:S(2)}) collective-permute-start(bf16[4,128,256]{2,1,0:T(8,128)(2,1)S(1)} %compose.5.refs_0_), channel_id=1, source_target_pairs={{0,8},{4,12},{8,0},{12,4},{16,24},{20,28},{24,16},{28,20},{1,9},{5... | collective-permute-start | bytes 786440 | tf_op jit(solution)/shard_map/ppermute | solution.py:363
  54.1 6.2 %collective-permute-start.7 = (bf16[4,128,128]{2,1,0:T(8,128)(2,1)S(1)}, bf16[4,128,128]{2,1,0:T(8,128)(2,1)S(1)}, u32[]{:S(2)}, u32[]{:S(2)}) collective-permute-start(bf16[4,128,128]{2,1,0:T(8,128)(2,1)S(1)} %slice.24), channel_id=1, source_target_pairs={{0,16},{4,20},{8,24},{12,28},{16,0},{20,4},{24,8},{28,12},{1,17},{... | collective-permute-start | bytes 393224 | tf_op jit(solution)/shard_map/ppermute | solution.py:363
  62.3 3.9 %collective-permute-start.8 = (bf16[4,128,128]{2,1,0:T(8,128)(2,1)S(1)}, bf16[4,128,128]{2,1,0:T(8,128)(2,1)S(1)}, u32[]{:S(2)}, u32[]{:S(2)}) collective-permute-start(bf16[4,128,128]{2,1,0:T(8,128)(2,1)S(1)} %get-tuple-element.32), channel_id=1, source_target_pairs={{0,4},{4,0},{8,12},{12,8},{16,20},{20,16},{24,28},{28,24},{1,5},{5... | collective-permute-start | bytes 393224 | tf_op jit(solution)/shard_map/ppermute | solution.py:363
  63.6 10.7 %collective-permute-start.11 = (bf16[4,128,128]{2,1,0:T(8,128)(2,1)S(1)}, bf16[4,128,128]{2,1,0:T(8,128)(2,1)S(1)}, u32[]{:S(2)}, u32[]{:S(2)}) collective-permute-start(bf16[4,128,128]{2,1,0:T(8,128)(2,1)S(1)} %get-tuple-element.36), channel_id=1, source_target_pairs={{0,2},{1,3},{2,0},{3,1},{4,6},{5,7},{6,4},{7,5},{8,10},{9,11},{10,... | collective-permute-start | bytes 393224 | tf_op jit(solution)/shard_map/ppermute | solution.py:363
  67.1 8.6 %collective-permute-start.9 = (bf16[4,128,128]{2,1,0:T(8,128)(2,1)S(1)}, bf16[4,128,128]{2,1,0:T(8,128)(2,1)S(1)}, u32[]{:S(2)}, u32[]{:S(2)}) collective-permute-start(bf16[4,128,128]{2,1,0:T(8,128)(2,1)S(1)} %get-tuple-element.33), channel_id=1, source_target_pairs={{0,2},{1,3},{2,0},{3,1},{4,6},{5,7},{6,4},{7,5},{8,10},{9,11},{10,... | collective-permute-start | bytes 393224 | tf_op jit(solution)/shard_map/ppermute | solution.py:363
  69.0 12.7 %collective-permute-start.14 = (bf16[4,128,128]{2,1,0:T(8,128)(2,1)S(1)}, bf16[4,128,128]{2,1,0:T(8,128)(2,1)S(1)}, u32[]{:S(2)}, u32[]{:S(2)}) collective-permute-start(bf16[4,128,128]{2,1,0:T(8,128)(2,1)S(1)} %get-tuple-element.42), channel_id=1, source_target_pairs={{0,1},{1,0},{2,3},{3,2},{4,5},{5,4},{6,7},{7,6},{8,9},{9,8},{10,11... | collective-permute-start | bytes 393224 | tf_op jit(solution)/shard_map/ppermute | solution.py:363
  74.3 10.5 %collective-permute-start.13 = (bf16[4,128,128]{2,1,0:T(8,128)(2,1)S(1)}, bf16[4,128,128]{2,1,0:T(8,128)(2,1)S(1)}, u32[]{:S(2)}, u32[]{:S(2)}) collective-permute-start(bf16[4,128,128]{2,1,0:T(8,128)(2,1)S(1)} %get-tuple-element.40), channel_id=1, source_target_pairs={{0,1},{1,0},{2,3},{3,2},{4,5},{5,4},{6,7},{7,6},{8,9},{9,8},{10,11... | collective-permute-start | bytes 393224 | tf_op jit(solution)/shard_map/ppermute | solution.py:363
  75.0 3.0 %copy-start = (bf16[128,4096]{1,0:T(8,128)(2,1)S(1)}, bf16[128,4096]{1,0:T(8,128)(2,1)}, u32[]{:S(2)}) copy-start(bf16[128,4096]{1,0:T(8,128)(2,1)} %gate_ref.15) | copy-start | bytes 3145732
  75.1 12.8 %collective-permute-start.12 = (bf16[4,128,128]{2,1,0:T(8,128)(2,1)S(1)}, bf16[4,128,128]{2,1,0:T(8,128)(2,1)S(1)}, u32[]{:S(2)}, u32[]{:S(2)}) collective-permute-start(bf16[4,128,128]{2,1,0:T(8,128)(2,1)S(1)} %get-tuple-element.37), channel_id=1, source_target_pairs={{0,1},{1,0},{2,3},{3,2},{4,5},{5,4},{6,7},{7,6},{8,9},{9,8},{10,11... | collective-permute-start | bytes 393224 | tf_op jit(solution)/shard_map/ppermute | solution.py:363
  76.4 13.0 %collective-permute-start.10 = (bf16[4,128,128]{2,1,0:T(8,128)(2,1)S(1)}, bf16[4,128,128]{2,1,0:T(8,128)(2,1)S(1)}, u32[]{:S(2)}, u32[]{:S(2)}) collective-permute-start(bf16[4,128,128]{2,1,0:T(8,128)(2,1)S(1)} %get-tuple-element.34), channel_id=1, source_target_pairs={{0,1},{1,0},{2,3},{3,2},{4,5},{5,4},{6,7},{7,6},{8,9},{9,8},{10,11... | collective-permute-start | bytes 393224 | tf_op jit(solution)/shard_map/ppermute | solution.py:363
  78.0 0.7 copy-start.1

commit v2 on v0

v2 whole, which is shorter than its diff:
```python
import functools

import jax
import jax.numpy as jnp
from jax import lax
from jax.experimental import pallas as pl
from jax.experimental.pallas import tpu as pltpu
from jax.sharding import PartitionSpec as P

C = 64
F32 = jnp.float32
BF16 = jnp.bfloat16
EXACT = lax.Precision.HIGHEST
VMEM_BYTES = 40 * 1024 * 1024
FETCH_BYTES = 51 * 1024 * 1024
REFETCH_BYTES = 47 * 1024 * 1024
MASKED = -1e30
BASE = 16


def params(limit=VMEM_BYTES):
    return pltpu.CompilerParams(vmem_limit_bytes=limit)


def cost():
    return pl.CostEstimate(flops=10**10, bytes_accessed=10**8, transcendentals=0)


def is_later(bit):
    axis, number = bit
    return jnp.bitwise_and(lax.shift_right_logical(lax.axis_index(axis), number), 1) == 1


def chunk_of(part):
    return jnp.bitwise_xor(lax.axis_index("head"), lax.axis_size("head") - 1 - part)


def parity():
    return jnp.bitwise_and(lax.axis_index("context"), 1)


def dot(a, b):
    return jnp.dot(a, b, preferred_element_type=F32)


def dot_t(a, b):
    return lax.dot_general(a, b, (((1,), (1,)), ((), ())), preferred_element_type=F32)


def whole_vmem():
    return pl.BlockSpec(memory_space=pltpu.VMEM)


def whole_smem():
    return pl.BlockSpec(memory_space=pltpu.SMEM)


def in_hbm():
    return pl.BlockSpec(memory_space=pltpu.HBM)


def masks(tokens):
    row = lax.broadcasted_iota(jnp.int32, (tokens, tokens), 0)
    column = lax.broadcasted_iota(jnp.int32, (tokens, tokens), 1)
    return row, column


def gates_kernel(parts, width, doc_ref, decay_ref, beta_ref, *rest):
    bias_refs, (col_ref, row_ref, gap_ref) = rest[:-3], rest[-3:]
    tokens = decay_ref.shape[1]
    half = width // 2
    row, column = masks(tokens)
    groups = tokens // C
    row_resets = jnp.zeros_like(row)
    column_resets = jnp.zeros_like(row)
    for group in range(groups):
        flag = doc_ref[lax.axis_index("head") * groups + group]
        row_resets = row_resets + jnp.where(row >= group * C, flag, 0)
        column_resets = column_resets + jnp.where(column >= group * C, flag, 0)
    gap_ref[...] = jnp.where(jnp.logical_and(row >= column, row_resets == column_resets), 0.0, MASKED)
    resets = column_resets[: parts * width]
    final = row_resets[tokens - 1 :]
    decay, beta = [], []
    for part in range(parts):
        rows = pl.ds(pl.multiple_of(chunk_of(part) * width, width), width)
        diagonal = row[:width, :width] == column[:width, :width]
        bias = jnp.sum(jnp.where(diagonal, bias_refs[part][...], 0.0), axis=1, keepdims=True)
        decay.append(decay_ref[rows, :] + bias)
        beta.append(beta_ref[rows, :])
    z = jnp.concatenate(decay, axis=0)
    beta = 1.0 / (1.0 + jnp.exp(-jnp.concatenate(beta, axis=0)))
    log_decay = -(jnp.maximum(z, 0.0) + jnp.log1p(jnp.exp(-jnp.abs(z))))
    upper = jnp.where(row <= column, 1.0, 0.0)
    cum = jnp.dot(log_decay, upper, precision=EXACT, preferred_element_type=F32)
    last = jnp.broadcast_to(cum[:, tokens - 1 :], cum.shape)
    gamma = jnp.where(resets == 0, jnp.exp(cum), 0.0)
    back = jnp.where(resets == final, jnp.exp(last - cum), 0.0)
    whole = jnp.where(final == 0, jnp.exp(last), 0.0)
    swapped = parity() == 1
    tall = []
    for part in range(parts):
        sides = [slice(part * width + side * half, part * width + (side + 1) * half) for side in range(2)]
        for turn in range(2):
            same, other = sides[turn], sides[1 - turn]
            for table in (cum, beta, beta * gamma, gamma):
                tall.append(jnp.where(swapped, table[other], table[same]))
            for place, table in enumerate((cum, back, whole)):
                row_ref[part, turn, place * half : (place + 1) * half, :] = jnp.where(
                    swapped, table[other], table[same]
                )
    col_ref[...] = jnp.transpose(jnp.concatenate(tall, axis=0))


def gates(doc_start, decay_rows, beta_rows, biases):
    heads, tokens = decay_rows.shape
    parts = len(biases)
    width = heads // parts
    half = width // 2
    return pl.pallas_call(
        functools.partial(gates_kernel, parts, width),
        out_shape=(
            jax.ShapeDtypeStruct((tokens, 4 * heads), F32),
            jax.ShapeDtypeStruct((parts, 2, 3 * half, tokens), F32),
            jax.ShapeDtypeStruct((tokens, tokens), F32),
        ),
        in_specs=[whole_smem()] + [whole_vmem()] * (2 + parts),
        out_specs=(whole_vmem(),) * 3,
        compiler_params=params(),
        cost_estimate=cost(),
        name="gates",
    )(doc_start, decay_rows, beta_rows, *biases)


def fetch_kernel(parts, half, q_hbm, k_hbm, v_hbm, *rest):
    normed_ref, turned_ref, q_ref, v_ref, k_ref, sems = rest[-6:]
    span = q_ref.shape[-1]
    size = span // half
    copies = {}
    for number, (source, target) in enumerate(((k_hbm, k_ref), (q_hbm, q_ref), (v_hbm, v_ref))):
        for turn in (1, 0):
            for place, part in enumerate(parts):
                at = 2 * chunk_of(part) + jnp.bitwise_xor(turn, parity())
                strip = pl.ds(pl.multiple_of(at * span, span), span)
                copy = pltpu.make_async_copy(
                    source.at[:, strip], target.at[place, turn], sems.at[number, place, turn]
                )
                copy.start()
                copies[number, place, turn] = copy
    for turn in (1, 0):
        for place in range(len(parts)):
            copies[0, place, turn].wait()
            for j in range(half):
                keys = k_ref[place, turn, :, j * size : (j + 1) * size].astype(F32)
                keys = (keys * lax.rsqrt(jnp.sum(keys * keys, axis=-1, keepdims=True) + 1e-06)).astype(BF16)
                normed_ref[place, turn, j] = keys
                turned_ref[place, turn, j] = jnp.transpose(keys)
    for number in (1, 2):
        for turn in (1, 0):
            for place in range(len(parts)):
                copies[number, place, turn].wait()


def fetch(parts, half, size, queries, keys, values, *after):
    tokens = queries.shape[0]
    count = len(parts)
    strips = jax.ShapeDtypeStruct((count, 2, tokens, half * size), BF16)
    return pl.pallas_call(
        functools.partial(fetch_kernel, parts, half),
        out_shape=(
            jax.ShapeDtypeStruct((count, 2, half, tokens, size), BF16),
            jax.ShapeDtypeStruct((count, 2, half, size, tokens), BF16),
            strips,
            strips,
        ),
        in_specs=[in_hbm()] * 3 + [whole_vmem()] * len(after),
        out_specs=(whole_vmem(),) * 4,
        scratch_shapes=[pltpu.VMEM(strips.shape, BF16), pltpu.SemaphoreType.DMA((3, count, 2))],
        compiler_params=params(REFETCH_BYTES if after else FETCH_BYTES),
        cost_estimate=cost(),
        name="fetch",
    )(queries, keys, values, *after)


def local_kernel(part, at, turn, *refs):
    normed_ref, turned_ref, q_ref, v_ref, col_ref, row_ref, gap_ref = refs[:7]
    ab_ref, qo_ref = refs[-2:]
    tokens = gap_ref.shape[0]
    half = ab_ref.shape[0]
    size = ab_ref.shape[1]
    row, column = masks(tokens)
    apart = jnp.bitwise_xor(row, column)
    eye = jnp.where(row == column, 1.0, 0.0)
    strict = row > column
    lane_block = lax.shift_right_logical(column[:BASE], BASE.bit_length() - 1)
    inside = jnp.bitwise_and(column[:BASE], BASE - 1)
    small_eye = jnp.where(row[:BASE] == inside, 1.0, 0.0)
    gap = gap_ref[...]
    every = range(half)

    def tall_of(table, j):
        at = ((2 * part + turn) * 4 + table) * half + j
        return col_ref[:, at : at + 1]

    def wide_of(table, j):
        return row_ref[part, turn, table * half + j : table * half + j + 1, :]

    lower, mix, inverse = [], [], []
    for j in every:
        decay = jnp.exp(tall_of(0, j) - wide_of(0, j) + gap)
        queries = q_ref[at, turn, :, j * size : (j + 1) * size]
        grams = dot(jnp.concatenate([normed_ref[at, turn, j], queries], axis=0), turned_ref[at, turn, j])
        low = jnp.where(strict, tall_of(1, j) * decay * grams[:tokens], 0.0)
        mix.append((decay * grams[tokens:]).astype(BF16))
        packed = jnp.zeros((BASE, tokens), F32)
        for top in range(0, tokens, BASE):
            packed = jnp.where(lane_block == top // BASE, low[top : top + BASE], packed)
        solution_rows = small_eye
        for k in range(BASE - 1):
            factor = jnp.take_along_axis(packed, column[:BASE] - inside + k, axis=1, mode="promise_in_bounds")
            solution_rows = solution_rows - factor * solution_rows[k : k + 1]
        inverse.append(
            jnp.concatenate(
                [jnp.where(lane_block == at_block, solution_rows, 0.0) for at_block in range(tokens // BASE)],
                axis=0,
            )
        )
        lower.append(low.astype(BF16))
    nothing = jnp.zeros((tokens, tokens), BF16)
    block = BASE
    while block < tokens:
        small = [inverse[j].astype(BF16) for j in every]
        step = jnp.logical_and(apart >= block, apart < 2 * block)
        masked = [jnp.where(step, lower[j], nothing) for j in every]
        spans = [slice(top, top + block) for top in range(block, tokens, 2 * block)]

        def odd(array):
            return jnp.concatenate([array[s] for s in spans], axis=0)

        def spread(array, evens):
            pieces = []
            for i, s in enumerate(spans):
                pieces.append(evens[s.start - block : s.start])
                pieces.append(array[i * block : (i + 1) * block])
            return jnp.concatenate(pieces, axis=0)

        inner = [spread(dot(odd(masked[j]), small[j]).astype(BF16), nothing) for j in every]
        inverse = [
            spread(odd(inverse[j]) - dot(odd(small[j]), inner[j]), inverse[j]) for j in every
        ]
        block *= 2
    solved = []
    for j in every:
        lanes = slice(j * size, (j + 1) * size)
        keys = tall_of(2, j) * normed_ref[at, turn, j].astype(F32)
        values = tall_of(1, j) * v_ref[at, turn, :, lanes].astype(F32)
        right = jnp.concatenate([keys.astype(BF16), values.astype(BF16)], axis=1)
        solved.append(dot(inverse[j].astype(BF16), right).astype(BF16))
    for j in every:
        lanes = slice(j * size, (j + 1) * size)
        after = turned_ref[at, turn, j].astype(F32) * wide_of(1, j)
        both = dot(jnp.concatenate([after.astype(BF16), mix[j]], axis=0), solved[j])
        through = tall_of(3, j) * q_ref[at, turn, :, lanes].astype(F32)
        ab_ref[j, :, :size] = (eye * wide_of(2, j) - both[:size, :size]).astype(BF16)
        ab_ref[j, :, size:] = both[:size, size:].astype(BF16)
        qo_ref[j, :, :size] = (through - both[size:, :size]).astype(BF16)
        qo_ref[j, :, size:] = both[size:, size:].astype(BF16)


def local(part, at, turn, prepared, tables, *after):
    half, tokens, size = prepared[0].shape[2:]
    result = jax.ShapeDtypeStruct((half, tokens, 2 * size), BF16)
    arrays = tuple(prepared) + tuple(tables) + after
    return pl.pallas_call(
        functools.partial(local_kernel, part, at, turn),
        out_shape=(result, result),
        in_specs=[whole_vmem()] * len(arrays),
        out_specs=(whole_vmem(), whole_vmem()),
        compiler_params=params(),
        cost_estimate=cost(),
        name="local_tokens",
    )(*arrays)


def joined(earlier, later):
    size = earlier.shape[0]
    product = dot(later[:, :size], earlier)
    return jnp.concatenate([product[:, :size], product[:, size:] + later[:, size:].astype(F32)], axis=1)


def pick(later, own, received):
    return jnp.where(later, received, own), jnp.where(later, own, received)


def compose_kernel(bit, own_ref, got_ref, out_ref):
    later = is_later(bit)
    for j in range(out_ref.shape[0]):
        earlier_block, later_block = pick(later, own_ref[j], got_ref[j])
        out_ref[j] = joined(earlier_block, later_block).astype(BF16)


def compose(bit, own, got):
    return pl.pallas_call(
        functools.partial(compose_kernel, bit),
        out_shape=jax.ShapeDtypeStruct(own.shape, BF16),
        in_specs=[whole_vmem(), whole_vmem()],
        out_specs=whole_vmem(),
        compiler_params=params(),
        cost_estimate=cost(),
        name="compose",
    )(own, got)


def doubling_kernel(bit, first, last, *refs):
    later = is_later(bit)
    own_ref, got_ref = refs[:2]
    total_ref, before_ref = refs[-2:]
    heads, size = own_ref.shape[:2]
    row = lax.broadcasted_iota(jnp.int32, (size, 2 * size), 0)
    column = lax.broadcasted_iota(jnp.int32, (size, 2 * size), 1)
    neutral = jnp.where(row == column, 1.0, 0.0).astype(BF16)
    for j in range(heads):
        earlier_block, later_block = pick(later, own_ref[j], got_ref[j])
        total = joined(earlier_block, later_block).astype(BF16)
        total_ref[j] = total[:, size:] if last else total
        if first:
            before_ref[j] = jnp.where(later, got_ref[j], neutral)
        else:
            before = refs[2][j]
            before_ref[j] = jnp.where(later, joined(got_ref[j], before).astype(BF16), before)


def doubling(bit, last, own, got, before):
    first = before is None
    arrays = (own, got) if first else (own, got, before)
    heads, size = own.shape[:2]
    total = jax.ShapeDtypeStruct((heads, size, size if last else 2 * size), BF16)
    return pl.pallas_call(
        functools.partial(doubling_kernel, bit, first, last),
        out_shape=(total, jax.ShapeDtypeStruct(own.shape, BF16)),
        in_specs=[whole_vmem()] * len(arrays),
        out_specs=(whole_vmem(), whole_vmem()),
        compiler_params=params(),
        cost_estimate=cost(),
        name="doubling",
    )(*arrays)


def descend_kernel(bits, top, threaded, *refs):
    count = len(bits)
    start = 2 if top is not None else 1
    blocks = refs[start : start + 2 * count]
    outs = refs[start + 2 * count + threaded :]
    sends, kept_ref = outs[:count], outs[count]
    size = kept_ref.shape[-1]
    for j in range(kept_ref.shape[0]):
        if top is None:
            state = refs[0][j]
        else:
            before = refs[1][j]
            carried = dot(before[:, :size], refs[0][j]) + before[:, size:].astype(F32)
            state = jnp.where(is_later(top), carried.astype(BF16), before[:, size:])
        for level, bit in enumerate(bits):
            later = is_later(bit)
            earlier = jnp.where(later, blocks[2 * level + 1][j], blocks[2 * level][j])
            after = (dot(earlier[:, :size], state) + earlier[:, size:].astype(F32)).astype(BF16)
            sends[level][j] = jnp.where(later, state, after)
            state = jnp.where(later, after, state)
        kept_ref[j] = state


def descend(bits, top, sources, blocks, thread):
    heads, size = sources[0].shape[0], sources[0].shape[1]
    arrays = list(sources) + [array for pair in blocks for array in pair]
    specs = [whole_vmem()] * len(arrays)
    outs = len(bits) + 1
    shapes = [jax.ShapeDtypeStruct((heads, size, size), BF16)] * outs
    out_specs = [whole_vmem()] * outs
    aliases = {}
    if thread is not None:
        arrays.append(thread)
        specs.append(in_hbm())
        shapes.append(jax.ShapeDtypeStruct(thread.shape, thread.dtype))
        out_specs.append(in_hbm())
        aliases = {len(arrays) - 1: outs}
    return pl.pallas_call(
        functools.partial(descend_kernel, bits, top, int(thread is not None)),
        out_shape=tuple(shapes),
        in_specs=specs,
        out_specs=tuple(out_specs),
        input_output_aliases=aliases,
        compiler_params=params(),
        cost_estimate=cost(),
        name="descend",
    )(*arrays)


def finish_kernel(part, turn, gain_ref, state_ref, qo_ref, gate_hbm, *rest):
    out_hbm, gate_ref, out_ref, sems = rest[-4:]
    half, size = state_ref.shape[0], state_ref.shape[-1]
    span = half * size
    at = 2 * chunk_of(part) + jnp.bitwise_xor(parity(), turn)
    strip = pl.ds(pl.multiple_of(at * span, span), span)
    fetch = pltpu.make_async_copy(gate_hbm.at[:, strip], gate_ref, sems.at[0])
    fetch.start()
    scaled = []
    for j in range(half):
        core = dot(qo_ref[j, :, :size], state_ref[j]) + qo_ref[j, :, size:].astype(F32)
        core = core.astype(BF16).astype(F32)
        scaled.append(
            core * lax.rsqrt(jnp.mean(core * core, axis=-1, keepdims=True) + 1e-06) * gain_ref[...]
        )
    fetch.wait()
    stores = []
    for j in range(half):
        lanes = slice(j * size, (j + 1) * size)
        gate = gate_ref[:, lanes].astype(F32)
        out_ref[:, lanes] = (scaled[j] * (0.5 * gate) * (1.0 + jnp.tanh(0.5 * gate))).astype(BF16)
        there = pl.ds(pl.multiple_of(at * span + j * size, size), size)
        stores.append(pltpu.make_async_copy(out_ref.at[:, lanes], out_hbm.at[:, there], sems.at[1 + j]))
        stores[-1].start()
    for store in stores:
        store.wait()


def finish(part, turn, state, qo, gate, gain, previous):
    half, tokens, size = state.shape[0], gate.shape[0], state.shape[-1]
    specs = [whole_vmem()] * 3 + [in_hbm()]
    arrays = [gain, state, qo, gate]
    aliases = {}
    if previous is not None:
        specs.append(in_hbm())
        arrays.append(previous)
        aliases = {len(arrays) - 1: 0}
    return pl.pallas_call(
        functools.partial(finish_kernel, part, turn),
        out_shape=jax.ShapeDtypeStruct(gate.shape, BF16),
        in_specs=specs,
        out_specs=in_hbm(),
        scratch_shapes=[pltpu.VMEM((tokens, half * size), BF16)] * 2 + [pltpu.SemaphoreType.DMA((1 + half,))],
        input_output_aliases=aliases,
        compiler_params=params(),
        cost_estimate=cost(),
        name="finish",
    )(*arrays)


def body(
    head_count,
    context_count,
    queries,
    key_input,
    value_input,
    gate_input,
    decay_logit,
    beta_logit,
    decay_bias,
    norm_gain,
    doc_start,
):
    head_bits = head_count.bit_length() - 1
    context_bits = context_count.bit_length() - 1

    def swap(array, axis, distance):
        count = head_count if axis == "head" else context_count
        return lax.ppermute(array, axis, [(i, i ^ distance) for i in range(count)])

    head_bit = [("head", bit) for bit in range(head_bits)]
    context_bit = [("context", bit) for bit in range(context_bits)]
    own_bias = decay_bias[None, :]
    biases = [swap(own_bias, "head", head_count - 1 - part) for part in range(head_count - 1)] + [own_bias]
    half, size = decay_bias.shape[0] // 2, norm_gain.shape[0]
    inputs = (queries, key_input, value_input)

    qo = {}
    levels = [{} for _ in range(head_bits)]
    far_parts = list(reversed(range(head_count // 2, head_count)))
    near_parts = [part - head_count // 2 for part in far_parts]
    prepared = {}
    for at, part in enumerate(far_parts):
        if at == 0:
            fetched = fetch(far_parts, half, size, *inputs)
        prepared[part] = (at, fetched)
    tables = gates(doc_start, decay_logit.T, beta_logit.T, biases)

    def climb(part, turn, bit, *after):
        if bit == 0:
            at, fetched = prepared[part]
            block, qo[part, turn] = local(part, at, turn, fetched, tables, *after)
            return block
        far = climb(part | 1 << (bit - 1), turn, bit - 1, *after)
        got = swap(far, "head", 1 << (bit - 1))
        near = climb(part, turn, bit - 1, far)
        levels[bit - 1][part, turn] = (near, got)
        return compose(head_bit[bit - 1], near, got)

    under = head_bits - 1
    far, got, near = {}, {}, {}
    far[1] = climb(1 << under, 1, under)
    got[1] = swap(far[1], "head", 1 << under)
    far[0] = climb(1 << under, 0, under, far[1])
    got[0] = swap(far[0], "head", 1 << under)
    fetched = fetch(near_parts, half, size, *inputs, far[1], far[0])
    for at, part in enumerate(near_parts):
        prepared[part] = (at, fetched)
    near[1] = climb(0, 1, under)
    chip = {1: compose(head_bit[under], near[1], got[1])}
    across = swap(chip[1], "context", 1)
    near[0] = climb(0, 0, under, chip[1])
    chip[0] = compose(head_bit[under], near[0], got[0])
    for turn in (1, 0):
        levels[under][0, turn] = (near[turn], got[turn])

    x_pair = (chip[0], across)
    total = compose(context_bit[0], *x_pair)
    before = None
    for bit in range(1, context_bits - 1):
        other = swap(total, "context", 1 << bit)
        total, before = doubling(context_bit[bit], bit == context_bits - 2, total, other, before)
    other = swap(total, "context", 1 << (context_bits - 1))

    gain = norm_gain[None, :]
    states = {}
    result = None
    descending = list(reversed(range(head_bits)))
    outs = descend(
        [context_bit[0]] + [head_bit[bit] for bit in descending],
        context_bit[-1],
        (other, before),
        [x_pair] + [levels[bit][0, 0] for bit in descending],
        None,
    )
    states[0, 0] = outs[-1]
    arriving = [(0, 1, head_bits, swap(outs[0], "context", 1))]
    for level, bit in enumerate(descending):
        arriving.append((1 << bit, 0, bit, swap(outs[1 + level], "head", 1 << bit)))
    ready = [(0, 0)]
    while arriving or ready:
        for part, turn in ready:
            result = finish(part, turn, states[part, turn], qo[part, turn], gate_input, gain, result)
        ready = []
        leaves = [entry for entry in arriving if entry[2] == 0]
        inner = [entry for entry in arriving if entry[2] > 0]
        arriving = []
        for part, turn, _, state in leaves:
            result = finish(part, turn, state, qo[part, turn], gate_input, gain, result)
        for part, turn, below, state in inner:
            under = list(reversed(range(below)))
            outs = descend(
                        [head_bit[bit] for bit in under],
                None,
                (state,),
                [levels[bit][part, turn] for bit in under],
                result,
            )
            states[part, turn] = outs[below]
            result = outs[-1]
            ready.append((part, turn))
            for level, bit in enumerate(under):
                arriving.append((part | 1 << bit, turn, bit, swap(outs[level], "head", 1 << bit)))
    return result


def solution(mesh):
    return jax.shard_map(
        functools.partial(body, mesh.shape["head"], mesh.shape["context"]),
        mesh=mesh,
        in_specs=(
            P(("context", "head"), None),
            P(("context", "head"), None),
            P(("context", "head"), None),
            P(("context", "head"), None),
            P(("context", "head"), None),
            P(("context", "head"), None),
            P("head"),
            P(),
            P("context"),
        ),
        out_specs=P(("context", "head"), None),
        check_vma=False,
    )
```

time: 608 us -> 66.3 us (0.11); the launches traced: 596 us -> 66 us
  other arithmetic: 349 us -> 0 us
  waiting for transfers between devices: 114 us -> 12.6 us
  matrix products: 71 us -> 0 us
  Pallas kernels: 0 us -> 30.9 us
  local copies, waits for them, and re-layouts: 23 us -> 3.4 us
  between operations: 14.3 us -> 0.6 us
  starting transfers between devices: 25.1 us -> 18.5 us
    another operation x5 -> x0, other arithmetic: 322 us -> none  [the longest x2 315 us: body(): jax.scipy.linalg.solve_triangular(jnp.eye(C, dtype=jnp.float32) + lower_p...]
    all_gather x2 -> x0, waiting for transfers between devices: 74.9 us -> none  [carried_in(): lax.all_gather(a.astype(kind), axis)]
    dot_general x25 -> x0, matrix products: 66.8 us -> none  [the longest x8 14.9 us: extend(): jnp.einsum('hde,hef->hdf', step_matrix, carry[1], precision=PRECISE)]
    all_to_all x6 -> x0, waiting for transfers between devices: 38.6 us -> none  [the longest x1 13.6 us: body(): lax.all_to_all(queries, 'head', split_axis=1, concat_axis=0, tiled=True)]
    pallas_call x0 -> x31, Pallas kernels: none -> 30.9 us  [the longest x8 14.6 us: local(): pl.pallas_call(functools.partial(local_kernel, part, at, turn), out_shape...]
    all_to_all x6 -> x0, starting transfers between devices: 25.1 us -> none  [the longest x1 5.26 us: body(): lax.all_to_all(core_rows, 'head', split_axis=0, concat_axis=1, tiled=True)]
    ppermute x0 -> x19, starting transfers between devices: none -> 18.5 us  [swap(): return lax.ppermute(array, axis, [(i, i ^ distance) for i in range(count)])]
    ppermute x0 -> x19, waiting for transfers between devices: none -> 12.6 us  [swap(): return lax.ppermute(array, axis, [(i, i ^ distance) for i in range(count)])]
  transfers between devices with their start and end apart: 8 -> 19, of which waited for: 5 -> 5; matrix products, arithmetic and copies ran while one was open for 57% -> 0% of each run, Pallas kernels for 0% -> 38%
where the time goes in v2:
time: 66.3 us; the launch traced here: 66 us
  Pallas kernels  30.9 us (47%)
  starting transfers between devices  18.5 us (28%)
  waiting for transfers between devices  12.6 us (19%)
  local copies, waits for them, and re-layouts  3.4 us (5%)
    ppermute x19, starting transfers between devices, swap(): return lax.ppermute(array, axis, [(i, i ^ distance) for i in range(count)])  18.5 us
    pallas_call x8, Pallas kernels, local(): pl.pallas_call(functools.partial(local_kernel, part, at, turn), out_shape...  14.6 us
    ppermute x19, waiting for transfers between devices, swap(): return lax.ppermute(array, axis, [(i, i ^ distance) for i in range(count)])  12.6 us
    pallas_call x8, Pallas kernels, finish(): pl.pallas_call(functools.partial(finish_kernel, part, turn), out_shape=ja...  8.42 us
    unnamed x34, local copies, waits for them, and re-layouts  3.4 us
    pallas_call x2, Pallas kernels, fetch(): pl.pallas_call(functools.partial(fetch_kernel, parts, half), out_shape=(j...  3.04 us
    pallas_call x4, Pallas kernels, descend(): pl.pallas_call(functools.partial(descend_kernel, bits, top, int(thread is...  2.16 us
    pallas_call x7, Pallas kernels, compose(): pl.pallas_call(functools.partial(compose_kernel, bit), out_shape=jax.Shap...  1.55 us
  transfers between devices with their start and end apart: 19, of which 5 were waited for; matrix products, arithmetic and copies ran while one was open for 0% of the time, Pallas kernels for 38%

profile of v2, /device:TPU:1, one launch (start us, length us, event | category | flops | bytes accessed | tf_op | source)
XLA Modules:
  0.0 66.0 jit_solution(7348602365158705630)
XLA Ops:
  0.7 2.7 %collective-permute-start.1 = (f32[1,8]{1,0:T(1,128)S(1)}, f32[1,8]{1,0:T(1,128)S(1)}, u32[]{:S(2)}, u32[]{:S(2)}) collective-permute-start(f32[1,8]{1,0:T(1,128)S(1)} %bitcast.7), channel_id=1, source_target_pairs={{0,2},{1,3},{2,0},{3,1},{4,6},{5,7},{6,4},{7,5},{8,10},{9,11},{10,... | collective-permute-start | bytes 104 | tf_op jit(solution)/shard_map/ppermute | solution.py:465
  3.4 1.9 %fetch.2 = (bf16[2,2,4,128,128]{4,3,2,1,0:T(8,128)(2,1)S(1)}, bf16[2,2,4,128,128]{4,3,2,1,0:T(8,128)(2,1)S(1)}, bf16[2,2,128,512]{3,2,1,0:T(8,128)(2,1)S(1)}, bf16[2,2,128,512]{3,2,1,0:T(8,128)(2,1)S(1)}) custom-call(bf16[128,4096]{1,0:T(8,128)(2,1)} %q_hbm.3, bf16[128,4096]{1,0:T(8,128)(2,1)} %k_hbm.3, bf16[128,4096]{1,0:T(8,128)(2,1)} %v_hbm.3), custom_call_target="tpu_custom_call" | custom-call | flops 10000000000 | bytes 100000000 | tf_op jit(solution)/shard_map/fetch/pallas_call | solution.py:167
  5.3 1.1 %collective-permute-done.rest_0_ = f32[1,8]{1,0:T(1,128)S(1)} collective-permute-done((f32[1,8]{1,0:T(1,128)S(1)}, f32[1,8]{1,0:T(1,128)S(1)}, u32[]{:S(2)}, u32[]{:S(2)}) %collective-permute-start) | collective-permute-done | bytes 64 | tf_op jit(solution)/shard_map/ppermute | solution.py:465
  8.0 1.8 %local_tokens.8 = (bf16[4,128,256]{2,1,0:T(8,128)(2,1)S(1)}, bf16[4,128,256]{2,1,0:T(8,128)(2,1)S(1)}) custom-call(bf16[2,2,4,128,128]{4,3,2,1,0:T(8,128)(2,1)S(1)} %get-tuple-element.48.refs_0_, bf16[2,2,4,128,128]{4,3,2,1,0:T(8,128)(2,1)S(1)} %get-tuple-element.49.refs_1_, bf16[2,2,128,512]{3,2,1,0:T(8,128)(2,1)S(1)} %get-tuple-element.50.refs_2_, ...), custom_call_target="tpu_custom_call" | custom-call | flops 10000000000 | bytes 100000000 | tf_op jit(solution)/shard_map/local_tokens/pallas_call | solution.py:273
  10.1 1.8 %local_tokens.9 = (bf16[4,128,256]{2,1,0:T(8,128)(2,1)S(1)}, bf16[4,128,256]{2,1,0:T(8,128)(2,1)S(1)}) custom-call(bf16[2,2,4,128,128]{4,3,2,1,0:T(8,128)(2,1)S(1)} %get-tuple-element.48.refs_0_, bf16[2,2,4,128,128]{4,3,2,1,0:T(8,128)(2,1)S(1)} %get-tuple-element.49.refs_1_, bf16[2,2,128,512]{3,2,1,0:T(8,128)(2,1)S(1)} %get-tuple-element.50.refs_2_, ...), custom_call_target="tpu_custom_call" | custom-call | flops 10000000000 | bytes 100000000 | tf_op jit(solution)/shard_map/local_tokens/pallas_call | solution.py:273
  13.3 1.8 %local_tokens.10 = (bf16[4,128,256]{2,1,0:T(8,128)(2,1)S(1)}, bf16[4,128,256]{2,1,0:T(8,128)(2,1)S(1)}) custom-call(bf16[2,2,4,128,128]{4,3,2,1,0:T(8,128)(2,1)S(1)} %get-tuple-element.48.refs_0_, bf16[2,2,4,128,128]{4,3,2,1,0:T(8,128)(2,1)S(1)} %get-tuple-element.49.refs_1_, bf16[2,2,128,512]{3,2,1,0:T(8,128)(2,1)S(1)} %get-tuple-element.50.refs_2_, ...), custom_call_target="tpu_custom_call" | custom-call | flops 10000000000 | bytes 100000000 | tf_op jit(solution)/shard_map/local_tokens/pallas_call | solution.py:273
  15.7 1.8 %local_tokens.11 = (bf16[4,128,256]{2,1,0:T(8,128)(2,1)S(1)}, bf16[4,128,256]{2,1,0:T(8,128)(2,1)S(1)}) custom-call(bf16[2,2,4,128,128]{4,3,2,1,0:T(8,128)(2,1)S(1)} %get-tuple-element.48.refs_0_, bf16[2,2,4,128,128]{4,3,2,1,0:T(8,128)(2,1)S(1)} %get-tuple-element.49.refs_1_, bf16[2,2,128,512]{3,2,1,0:T(8,128)(2,1)S(1)} %get-tuple-element.50.refs_2_, ...), custom_call_target="tpu_custom_call" | custom-call | flops 10000000000 | bytes 100000000 | tf_op jit(solution)/shard_map/local_tokens/pallas_call | solution.py:273
  19.6 1.2 %fetch.3 = (bf16[2,2,4,128,128]{4,3,2,1,0:T(8,128)(2,1)S(1)}, bf16[2,2,4,128,128]{4,3,2,1,0:T(8,128)(2,1)S(1)}, bf16[2,2,128,512]{3,2,1,0:T(8,128)(2,1)S(1)}, bf16[2,2,128,512]{3,2,1,0:T(8,128)(2,1)S(1)}) custom-call(bf16[128,4096]{1,0:T(8,128)(2,1)S(1)} %copy-done, bf16[128,4096]{1,0:T(8,128)(2,1)S(1)} %copy-done.1, bf16[128,4096]{1,0:T(8,128)(2,1)S(1)} %copy-done.2, ...), custom_call_target="tpu_custom_call" | custom-call | flops 10000000000 | bytes 100000000 | tf_op jit(solution)/shard_map/fetch/pallas_call | solution.py:167
  20.8 1.8 %local_tokens.12 = (bf16[4,128,256]{2,1,0:T(8,128)(2,1)S(1)}, bf16[4,128,256]{2,1,0:T(8,128)(2,1)S(1)}) custom-call(bf16[2,2,4,128,128]{4,3,2,1,0:T(8,128)(2,1)S(1)} %get-tuple-element.59.refs_0_, bf16[2,2,4,128,128]{4,3,2,1,0:T(8,128)(2,1)S(1)} %get-tuple-element.60.refs_1_, bf16[2,2,128,512]{3,2,1,0:T(8,128)(2,1)S(1)} %get-tuple-element.61.refs_2_, ...), custom_call_target="tpu_custom_call" | custom-call | flops 10000000000 | bytes 100000000 | tf_op jit(solution)/shard_map/local_tokens/pallas_call | solution.py:273
  22.9 1.8 %local_tokens.13 = (bf16[4,128,256]{2,1,0:T(8,128)(2,1)S(1)}, bf16[4,128,256]{2,1,0:T(8,128)(2,1)S(1)}) custom-call(bf16[2,2,4,128,128]{4,3,2,1,0:T(8,128)(2,1)S(1)} %get-tuple-element.59.refs_0_, bf16[2,2,4,128,128]{4,3,2,1,0:T(8,128)(2,1)S(1)} %get-tuple-element.60.refs_1_, bf16[2,2,128,512]{3,2,1,0:T(8,128)(2,1)S(1)} %get-tuple-element.61.refs_2_, ...), custom_call_target="tpu_custom_call" | custom-call | flops 10000000000 | bytes 100000000 | tf_op jit(solution)/shard_map/local_tokens/pallas_call | solution.py:273
  25.2 1.3 %collective-permute-start.9 = (bf16[4,128,256]{2,1,0:T(8,128)(2,1)S(1)}, bf16[4,128,256]{2,1,0:T(8,128)(2,1)S(1)}, u32[]{:S(2)}, u32[]{:S(2)}) collective-permute-start(bf16[4,128,256]{2,1,0:T(8,128)(2,1)S(1)} %compose.10.refs_7_), channel_id=1, source_target_pairs={{0,4},{4,0},{8,12},{12,8},{16,20},{20,16},{24,28},{28,24},{1,5},{5... | collective-permute-start | bytes 786440 | tf_op jit(solution)/shard_map/ppermute | solution.py:465
  26.5 1.8 %local_tokens.14 = (bf16[4,128,256]{2,1,0:T(8,128)(2,1)S(1)}, bf16[4,128,256]{2,1,0:T(8,128)(2,1)S(1)}) custom-call(bf16[2,2,4,128,128]{4,3,2,1,0:T(8,128)(2,1)S(1)} %get-tuple-element.59.refs_0_, bf16[2,2,4,128,128]{4,3,2,1,0:T(8,128)(2,1)S(1)} %get-tuple-element.60.refs_1_, bf16[2,2,128,512]{3,2,1,0:T(8,128)(2,1)S(1)} %get-tuple-element.61.refs_2_, ...), custom_call_target="tpu_custom_call" | custom-call | flops 10000000000 | bytes 100000000 | tf_op jit(solution)/shard_map/local_tokens/pallas_call | solution.py:273
  29.0 1.8 %local_tokens.15 = (bf16[4,128,256]{2,1,0:T(8,128)(2,1)S(1)}, bf16[4,128,256]{2,1,0:T(8,128)(2,1)S(1)}) custom-call(bf16[2,2,4,128,128]{4,3,2,1,0:T(8,128)(2,1)S(1)} %get-tuple-element.59.refs_0_, bf16[2,2,4,128,128]{4,3,2,1,0:T(8,128)(2,1)S(1)} %get-tuple-element.60.refs_1_, bf16[2,2,128,512]{3,2,1,0:T(8,128)(2,1)S(1)} %get-tuple-element.61.refs_2_, ...), custom_call_target="tpu_custom_call" | custom-call | flops 10000000000 | bytes 100000000 | tf_op jit(solution)/shard_map/local_tokens/pallas_call | solution.py:273
  31.3 1.5 %collective-permute-done.9.got_ref.refs_3_ = bf16[4,128,256]{2,1,0:T(8,128)(2,1)S(1)} collective-permute-done((bf16[4,128,256]{2,1,0:T(8,128)(2,1)S(1)}, bf16[4,128,256]{2,1,0:T(8,128)(2,1)S(1)}, u32[]{:S(2)}, u32[]{:S(2)}) %collective-permute-start.9) | collective-permute-done | bytes 262176 | tf_op jit(solution)/shard_map/ppermute | solution.py:465
  33.0 1.3 %collective-permute-start.10 = (bf16[4,128,256]{2,1,0:T(8,128)(2,1)S(1)}, bf16[4,128,256]{2,1,0:T(8,128)(2,1)S(1)}, u32[]{:S(2)}, u32[]{:S(2)}) collective-permute-start(bf16[4,128,256]{2,1,0:T(8,128)(2,1)S(1)} %compose.13.refs_0_), channel_id=1, source_target_pairs={{0,8},{4,12},{8,0},{12,4},{16,24},{20,28},{24,16},{28,20},{1,9},{5... | collective-permute-start | bytes 786440 | tf_op jit(solution)/shard_map/ppermute | solution.py:465
  34.4 5.4 %collective-permute-done.10.refs_1_ = bf16[4,128,256]{2,1,0:T(8,128)(2,1)S(1)} collective-permute-done((bf16[4,128,256]{2,1,0:T(8,128)(2,1)S(1)}, bf16[4,128,256]{2,1,0:T(8,128)(2,1)S(1)}, u32[]{:S(2)}, u32[]{:S(2)}) %collective-permute-start.10) | collective-permute-done | bytes 262176 | tf_op jit(solution)/shard_map/ppermute | solution.py:465
  40.0 2.3 %collective-permute-start.11 = (bf16[4,128,128]{2,1,0:T(8,128)(2,1)S(1)}, bf16[4,128,128]{2,1,0:T(8,128)(2,1)S(1)}, u32[]{:S(2)}, u32[]{:S(2)}) collective-permute-start(bf16[4,128,128]{2,1,0:T(8,128)(2,1)S(1)} %get-tuple-element.67), channel_id=1, source_target_pairs={{0,16},{4,20},{8,24},{12,28},{16,0},{20,4},{24,8},{28,12},{1,17},{... | collective-permute-start | bytes 393224 | tf_op jit(solution)/shard_map/ppermute | solution.py:465
  42.3 4.4 %collective-permute-done.11.refs_0_ = bf16[4,128,128]{2,1,0:T(8,128)(2,1)S(1)} collective-permute-done((bf16[4,128,128]{2,1,0:T(8,128)(2,1)S(1)}, bf16[4,128,128]{2,1,0:T(8,128)(2,1)S(1)}, u32[]{:S(2)}, u32[]{:S(2)}) %collective-permute-start.11) | collective-permute-done | bytes 131104 | tf_op jit(solution)/shard_map/ppermute | solution.py:465
  46.6 1.4 %descend.4 = (bf16[4,128,128]{2,1,0:T(8,128)(2,1)S(1)}, bf16[4,128,128]{2,1,0:T(8,128)(2,1)S(1)}, bf16[4,128,128]{2,1,0:T(8,128)(2,1)S(1)}, bf16[4,128,128]{2,1,0:T(8,128)(2,1)S(1)}) custom-call(bf16[4,128,128]{2,1,0:T(8,128)(2,1)S(1)} %collective-permute-done.11.refs_0_, bf16[4,128,256]{2,1,0:T(8,128)(2,1)S(1)} %get-tuple-element.68.refs_1_, ...), custom_call_target="tpu_custom_call" | custom-call | flops 10000000000 | bytes 100000000 | tf_op jit(solution)/shard_map/descend/pallas_call | solution.py:385
  48.1 1.2 %collective-permute-start.12 = (bf16[4,128,128]{2,1,0:T(8,128)(2,1)S(1)}, bf16[4,128,128]{2,1,0:T(8,128)(2,1)S(1)}, u32[]{:S(2)}, u32[]{:S(2)}) collective-permute-start(bf16[4,128,128]{2,1,0:T(8,128)(2,1)S(1)} %get-tuple-element.69), channel_id=1, source_target_pairs={{0,4},{4,0},{8,12},{12,8},{16,20},{20,16},{24,28},{28,24},{1,5},{5... | collective-permute-start | bytes 393224 | tf_op jit(solution)/shard_map/ppermute | solution.py:465
  49.3 3.3 %collective-permute-start.13 = (bf16[4,128,128]{2,1,0:T(8,128)(2,1)S(1)}, bf16[4,128,128]{2,1,0:T(8,128)(2,1)S(1)}, u32[]{:S(2)}, u32[]{:S(2)}) collective-permute-start(bf16[4,128,128]{2,1,0:T(8,128)(2,1)S(1)} %get-tuple-element.70), channel_id=1, source_target_pairs={{0,1},{1,0},{2,3},{3,2},{4,5},{5,4},{6,7},{7,6},{8,9},{9,8},{10,11... | collective-permute-start | bytes 393224 | tf_op jit(solution)/shard_map/ppermute | solution.py:465
  56.2 1.1 %collective-permute-start.14 = (bf16[4,128,128]{2,1,0:T(8,128)(2,1)S(1)}, bf16[4,128,128]{2,1,0:T(8,128)(2,1)S(1)}, u32[]{:S(2)}, u32[]{:S(2)}) collective-permute-start(bf16[4,128,128]{2,1,0:T(8,128)(2,1)S(1)} %get-tuple-element.74), channel_id=1, source_target_pairs={{0,2},{1,3},{2,0},{3,1},{4,6},{5,7},{6,4},{7,5},{8,10},{9,11},{10,... | collective-permute-start | bytes 393224 | tf_op jit(solution)/shard_map/ppermute | solution.py:465
  59.8 1.1 %finish.11.rest_0_ = bf16[128,4096]{1,0:T(8,128)(2,1)} custom-call(f32[1,128]{1,0:T(1,128)S(1)} %bitcast.13, bf16[4,128,128]{2,1,0:T(8,128)(2,1)S(1)} %get-tuple-element.81.state_ref, bf16[4,128,256]{2,1,0:T(8,128)(2,1)S(1)} %get-tuple-element.82.qo_ref, bf16[128,4096]{1,0:T(8,128)(2,1)S(1)} %copy-done.3, ...), custom_call_target="tpu_custom_call", output_to_operand_aliasing={{}: (4, {})} | custom-call | flops 10000000000 | bytes 100000000 | tf_op jit(solution)/shard_map/finish/pallas_call | solution.py:434
  62.0 1.1 %finish.13.refs_3_ = bf16[128,4096]{1,0:T(8,128)(2,1)} custom-call(f32[1,128]{1,0:T(1,128)S(1)} %bitcast.15, bf16[4,128,128]{2,1,0:T(8,128)(2,1)S(1)} %collective-permute-done.16.state_ref, bf16[4,128,256]{2,1,0:T(8,128)(2,1)S(1)} %get-tuple-element.78.qo_ref, bf16[128,4096]{1,0:T(8,128)(2,1)S(1)} %copy-done.3, ...), custom_call_target="tpu_custom_call", output_to_operand_aliasing={{}: (4, {})} | custom-call | flops 10000000000 | bytes 100000000 | tf_op jit(solution)/shard_map/finish/pallas_call | solution.py:434
  (79 shorter events, 18.7 us)
Async XLA Ops:
  0.7 5.7 %copy-start.8 = (f32[128,32]{0,1:T(8,128)S(1)}, f32[128,32]{0,1:T(8,128)}, u32[]{:S(2)}) copy-start(f32[128,32]{0,1:T(8,128)} %param.13) | copy-start | bytes 49156
  0.7 5.7 %copy-start.9 = (f32[128,32]{0,1:T(8,128)S(1)}, f32[128,32]{0,1:T(8,128)}, u32[]{:S(2)}) copy-start(f32[128,32]{0,1:T(8,128)} %param.14) | copy-start | bytes 49156
  0.7 4.6 %collective-permute-start.2 = (f32[1,8]{1,0:T(1,128)S(1)}, f32[1,8]{1,0:T(1,128)S(1)}, u32[]{:S(2)}, u32[]{:S(2)}) collective-permute-start(f32[1,8]{1,0:T(1,128)S(1)} %bitcast.6), channel_id=1, source_target_pairs={{0,1},{1,0},{2,3},{3,2},{4,5},{5,4},{6,7},{7,6},{8,9},{9,8},{10,11... | collective-permute-start | bytes 104 | tf_op jit(solution)/shard_map/ppermute | solution.py:465
  0.7 4.6 %collective-permute-start.1 = (f32[1,8]{1,0:T(1,128)S(1)}, f32[1,8]{1,0:T(1,128)S(1)}, u32[]{:S(2)}, u32[]{:S(2)}) collective-permute-start(f32[1,8]{1,0:T(1,128)S(1)} %bitcast.7), channel_id=1, source_target_pairs={{0,2},{1,3},{2,0},{3,1},{4,6},{5,7},{6,4},{7,5},{8,10},{9,11},{10,... | collective-permute-start | bytes 104 | tf_op jit(solution)/shard_map/ppermute | solution.py:465
  3.4 3.0 %collective-permute-start = (f32[1,8]{1,0:T(1,128)S(1)}, f32[1,8]{1,0:T(1,128)S(1)}, u32[]{:S(2)}, u32[]{:S(2)}) collective-permute-start(f32[1,8]{1,0:T(1,128)S(1)} %bitcast.8), channel_id=1, source_target_pairs={{0,3},{1,2},{2,1},{3,0},{4,7},{5,6},{6,5},{7,4},{8,11},{9,10},{10,... | collective-permute-start | bytes 104 | tf_op jit(solution)/shard_map/ppermute | solution.py:465
  9.8 2.2 %collective-permute-start.3 = (bf16[4,128,256]{2,1,0:T(8,128)(2,1)S(1)}, bf16[4,128,256]{2,1,0:T(8,128)(2,1)S(1)}, u32[]{:S(2)}, u32[]{:S(2)}) collective-permute-start(bf16[4,128,256]{2,1,0:T(8,128)(2,1)S(1)} %get-tuple-element.55.refs_7_), channel_id=1, source_target_pairs={{0,1},{1,0},{2,3},{3,2},{4,5},{5,4},{6,7},{7,6},{8,9},{9,8},{10,11... | collective-permute-start | bytes 786440 | tf_op jit(solution)/shard_map/ppermute | solution.py:465
  12.8 12.2 %collective-permute-start.6 = (bf16[4,128,256]{2,1,0:T(8,128)(2,1)S(1)}, bf16[4,128,256]{2,1,0:T(8,128)(2,1)S(1)}, u32[]{:S(2)}, u32[]{:S(2)}) collective-permute-start(bf16[4,128,256]{2,1,0:T(8,128)(2,1)S(1)} %compose.7.refs_7_.rest_0_), channel_id=1, source_target_pairs={{0,2},{1,3},{2,0},{3,1},{4,6},{5,7},{6,4},{7,5},{8,10},{9,11},{10,... | collective-permute-start | bytes 786440 | tf_op jit(solution)/shard_map/ppermute | solution.py:465
  15.1 2.5 %collective-permute-start.4 = (bf16[4,128,256]{2,1,0:T(8,128)(2,1)S(1)}, bf16[4,128,256]{2,1,0:T(8,128)(2,1)S(1)}, u32[]{:S(2)}, u32[]{:S(2)}) collective-permute-start(bf16[4,128,256]{2,1,0:T(8,128)(2,1)S(1)} %get-tuple-element.57.refs_7_), channel_id=1, source_target_pairs={{0,1},{1,0},{2,3},{3,2},{4,5},{5,4},{6,7},{7,6},{8,9},{9,8},{10,11... | collective-permute-start | bytes 786440 | tf_op jit(solution)/shard_map/ppermute | solution.py:465
  18.4 12.7 %collective-permute-start.8 = (bf16[4,128,256]{2,1,0:T(8,128)(2,1)S(1)}, bf16[4,128,256]{2,1,0:T(8,128)(2,1)S(1)}, u32[]{:S(2)}, u32[]{:S(2)}) collective-permute-start(bf16[4,128,256]{2,1,0:T(8,128)(2,1)S(1)} %compose.8.rest_1_), channel_id=1, source_target_pairs={{0,2},{1,3},{2,0},{3,1},{4,6},{5,7},{6,4},{7,5},{8,10},{9,11},{10,... | collective-permute-start | bytes 786440 | tf_op jit(solution)/shard_map/ppermute | solution.py:465
  22.6 2.1 %collective-permute-start.5 = (bf16[4,128,256]{2,1,0:T(8,128)(2,1)S(1)}, bf16[4,128,256]{2,1,0:T(8,128)(2,1)S(1)}, u32[]{:S(2)}, u32[]{:S(2)}) collective-permute-start(bf16[4,128,256]{2,1,0:T(8,128)(2,1)S(1)} %get-tuple-element.63.refs_7_), channel_id=1, source_target_pairs={{0,1},{1,0},{2,3},{3,2},{4,5},{5,4},{6,7},{7,6},{8,9},{9,8},{10,11... | collective-permute-start | bytes 786440 | tf_op jit(solution)/shard_map/ppermute | solution.py:465
  25.2 7.6 %collective-permute-start.9 = (bf16[4,128,256]{2,1,0:T(8,128)(2,1)S(1)}, bf16[4,128,256]{2,1,0:T(8,128)(2,1)S(1)}, u32[]{:S(2)}, u32[]{:S(2)}) collective-permute-start(bf16[4,128,256]{2,1,0:T(8,128)(2,1)S(1)} %compose.10.refs_7_), channel_id=1, source_target_pairs={{0,4},{4,0},{8,12},{12,8},{16,20},{20,16},{24,28},{28,24},{1,5},{5... | collective-permute-start | bytes 786440 | tf_op jit(solution)/shard_map/ppermute | solution.py:465
  28.3 2.6 %collective-permute-start.7 = (bf16[4,128,256]{2,1,0:T(8,128)(2,1)S(1)}, bf16[4,128,256]{2,1,0:T(8,128)(2,1)S(1)}, u32[]{:S(2)}, u32[]{:S(2)}) collective-permute-start(bf16[4,128,256]{2,1,0:T(8,128)(2,1)S(1)} %get-tuple-element.65.refs_7_), channel_id=1, source_target_pairs={{0,1},{1,0},{2,3},{3,2},{4,5},{5,4},{6,7},{7,6},{8,9},{9,8},{10,11... | collective-permute-start | bytes 786440 | tf_op jit(solution)/shard_map/ppermute | solution.py:465
  33.0 6.7 %collective-permute-start.10 = (bf16[4,128,256]{2,1,0:T(8,128)(2,1)S(1)}, bf16[4,128,256]{2,1,0:T(8,128)(2,1)S(1)}, u32[]{:S(2)}, u32[]{:S(2)}) collective-permute-start(bf16[4,128,256]{2,1,0:T(8,128)(2,1)S(1)} %compose.13.refs_0_), channel_id=1, source_target_pairs={{0,8},{4,12},{8,0},{12,4},{16,24},{20,28},{24,16},{28,20},{1,9},{5... | collective-permute-start | bytes 786440 | tf_op jit(solution)/shard_map/ppermute | solution.py:465
  40.0 6.7 %collective-permute-start.11 = (bf16[4,128,128]{2,1,0:T(8,128)(2,1)S(1)}, bf16[4,128,128]{2,1,0:T(8,128)(2,1)S(1)}, u32[]{:S(2)}, u32[]{:S(2)}) collective-permute-start(bf16[4,128,128]{2,1,0:T(8,128)(2,1)S(1)} %get-tuple-element.67), channel_id=1, source_target_pairs={{0,16},{4,20},{8,24},{12,28},{16,0},{20,4},{24,8},{28,12},{1,17},{... | collective-permute-start | bytes 393224 | tf_op jit(solution)/shard_map/ppermute | solution.py:465
  46.6 6.4 %copy-start.3 = (bf16[128,4096]{1,0:T(8,128)(2,1)S(1)}, bf16[128,4096]{1,0:T(8,128)(2,1)}, u32[]{:S(2)}) copy-start(bf16[128,4096]{1,0:T(8,128)(2,1)} %gate_hbm.15) | copy-start | bytes 3145732
  48.1 7.8 %collective-permute-start.12 = (bf16[4,128,128]{2,1,0:T(8,128)(2,1)S(1)}, bf16[4,128,128]{2,1,0:T(8,128)(2,1)S(1)}, u32[]{:S(2)}, u32[]{:S(2)}) collective-permute-start(bf16[4,128,128]{2,1,0:T(8,128)(2,1)S(1)} %get-tuple-element.69), channel_id=1, source_target_pairs={{0,4},{4,0},{8,12},{12,8},{16,20},{20,16},{24,28},{28,24},{1,5},{5... | collective-permute-start | bytes 393224 | tf_op jit(solution)/shard_map/ppermute | solution.py:465
  49.3 5.5 %collective-permute-start.13 = (bf16[4,128,128]{2,1,0:T(8,128)(2,1)S(1)}, bf16[4,128,128]{2,1,0:T(8,128)(2,1)S(1)}, u32[]{:S(2)}, u32[]{:S(2)}) collective-permute-start(bf16[4,128,128]{2,1,0:T(8,128)(2,1)S(1)} %get-tuple-element.70), channel_id=1, source_target_pairs={{0,1},{1,0},{2,3},{3,2},{4,5},{5,4},{6,7},{7,6},{8,9},{9,8},{10,11... | collective-permute-start | bytes 393224 | tf_op jit(solution)/shard_map/ppermute | solution.py:465
  52.6 5.3 %collective-permute-start.15 = (bf16[4,128,128]{2,1,0:T(8,128)(2,1)S(1)}, bf16[4,128,128]{2,1,0:T(8,128)(2,1)S(1)}, u32[]{:S(2)}, u32[]{:S(2)}) collective-permute-start(bf16[4,128,128]{2,1,0:T(8,128)(2,1)S(1)} %get-tuple-element.75), channel_id=1, source_target_pairs={{0,2},{1,3},{2,0},{3,1},{4,6},{5,7},{6,4},{7,5},{8,10},{9,11},{10,... | collective-permute-start | bytes 393224 | tf_op jit(solution)/shard_map/ppermute | solution.py:465
  55.8 2.0 %copy-start.7 = (bf16[4,128,256]{2,1,0:T(8,128)(2,1)S(1)}, bf16[4,128,256]{2,1,0:T(8,128)(2,1)}, u32[]{:S(2)}) copy-start(bf16[4,128,256]{2,1,0:T(8,128)(2,1)} %copy-done.6) | copy-start | bytes 786436
  55.8 2.0 %copy-start.16 = (bf16[4,128,256]{2,1,0:T(8,128)(2,1)S(1)}, bf16[4,128,256]{2,1,0:T(8,128)(2,1)}, u32[]{:S(2)}) copy-start(bf16[4,128,256]{2,1,0:T(8,128)(2,1)} %copy-done.15) | copy-start | bytes 786436
  56.2 6.9 %collective-permute-start.14 = (bf16[4,128,128]{2,1,0:T(8,128)(2,1)S(1)}, bf16[4,128,128]{2,1,0:T(8,128)(2,1)S(1)}, u32[]{:S(2)}, u32[]{:S(2)}) collective-permute-start(bf16[4,128,128]{2,1,0:T(8,128)(2,1)S(1)} %get-tuple-element.74), channel_id=1, source_target_pairs={{0,2},{1,3},{2,0},{3,1},{4,6},{5,7},{6,4},{7,5},{8,10},{9,11},{10,... | collective-permute-start | bytes 393224 | tf_op jit(solution)/shard_map/ppermute | solution.py:465
  57.3 3.6 %collective-permute-start.17 = (bf16[4,128,128]{2,1,0:T(8,128)(2,1)S(1)}, bf16[4,128,128]{2,1,0:T(8,128)(2,1)S(1)}, u32[]{:S(2)}, u32[]{:S(2)}) collective-permute-start(bf16[4,128,128]{2,1,0:T(8,128)(2,1)S(1)} %get-tuple-element.79), channel_id=1, source_target_pairs={{0,1},{1,0},{2,3},{3,2},{4,5},{5,4},{6,7},{7,6},{8,9},{9,8},{10,11... | collective-permute-start | bytes 393224 | tf_op jit(solution)/shard_map/ppermute | solution.py:465
  58.1 3.9 %collective-permute-start.16 = (bf16[4,128,128]{2,1,0:T(8,128)(2,1)S(1)}, bf16[4,128,128]{2,1,0:T(8,128)(2,1)S(1)}, u32[]{:S(2)}, u32[]{:S(2)}) collective-permute-start(bf16[4,128,128]{2,1,0:T(8,128)(2,1)S(1)} %get-tuple-element.77), channel_id=1, source_target_pairs={{0,1},{1,0},{2,3},{3,2},{4,5},{5,4},{6,7},{7,6},{8,9},{9,8},{10,11... | collective-permute-start | bytes 393224 | tf_op jit(solution)/shard_map/ppermute | solution.py:465
  63.3 1.4 %collective-permute-start.18 = (bf16[4,128,128]{2,1,0:T(8,128)(2,1)S(1)}, bf16[4,128,128]{2,1,0:T(8,128)(2,1)S(1)}, u32[]{:S(2)}, u32[]{:S(2)}) collective-permute-start(bf16[4,128,128]{2,1,0:T(8,128)(2,1)S(1)} %get-tuple-element.86), channel_id=1, source_target_pairs={{0,1},{1,0},{2,3},{3,2},{4,5},{5,4},{6,7},{7,6},{8,9},{9,8},{10,11... | collective-permute-start | bytes 393224 | tf_op jit(solution)/shard_map/ppermute | solution.py:465
  (12 other events, 12.6 us)

commit v3 on v2

v3 whole, which is shorter than its diff:
```python
import functools

import jax
import jax.numpy as jnp
from jax import lax
from jax.experimental import pallas as pl
from jax.experimental.pallas import tpu as pltpu
from jax.sharding import PartitionSpec as P

C = 64
F32 = jnp.float32
BF16 = jnp.bfloat16
EXACT = lax.Precision.HIGHEST
VMEM_BYTES = 28 * 1024 * 1024
FETCH_BYTES = 52 * 1024 * 1024
REFETCH_BYTES = 47 * 1024 * 1024
MASKED = -1e30
BASE = 16


def params(limit=VMEM_BYTES):
    return pltpu.CompilerParams(vmem_limit_bytes=limit)


def cost(long=True):
    return pl.CostEstimate(flops=10**10 if long else 10**7, bytes_accessed=10**8 if long else 10**5, transcendentals=0)


def is_later(bit):
    axis, number = bit
    return jnp.bitwise_and(lax.shift_right_logical(lax.axis_index(axis), number), 1) == 1


def chunk_of(part):
    return jnp.bitwise_xor(lax.axis_index("head"), lax.axis_size("head") - 1 - part)


def parity():
    return jnp.bitwise_and(lax.axis_index("context"), 1)


def dot(a, b):
    return jnp.dot(a, b, preferred_element_type=F32)


def dot_t(a, b):
    return lax.dot_general(a, b, (((1,), (1,)), ((), ())), preferred_element_type=F32)


def whole_vmem():
    return pl.BlockSpec(memory_space=pltpu.VMEM)


def whole_smem():
    return pl.BlockSpec(memory_space=pltpu.SMEM)


def in_hbm():
    return pl.BlockSpec(memory_space=pltpu.HBM)


def masks(tokens):
    row = lax.broadcasted_iota(jnp.int32, (tokens, tokens), 0)
    column = lax.broadcasted_iota(jnp.int32, (tokens, tokens), 1)
    return row, column


def gates_kernel(parts, bias_rows, width, decay_ref, beta_ref, flag_ref, *rest):
    bias_refs, (col_ref, row_ref) = rest[: len(parts)], rest[-2:]
    tokens = decay_ref.shape[1]
    half = width // 2
    row, column = masks(tokens)
    decay, beta = [], []
    for place, part in enumerate(parts):
        rows = pl.ds(pl.multiple_of(chunk_of(part) * width, width), width)
        diagonal = row[:width, :width] == column[:width, :width]
        bias = bias_refs[place][bias_rows[place] : bias_rows[place] + 1, :width]
        bias = jnp.sum(jnp.where(diagonal, bias, 0.0), axis=1, keepdims=True)
        decay.append(decay_ref[rows, :] + bias)
        beta.append(beta_ref[rows, :])
    z = jnp.concatenate(decay, axis=0)
    beta = 1.0 / (1.0 + jnp.exp(-jnp.concatenate(beta, axis=0)))
    log_decay = -(jnp.maximum(z, 0.0) + jnp.log1p(jnp.exp(-jnp.abs(z))))
    upper = jnp.where(row <= column, 1.0, 0.0)
    cum = jnp.dot(log_decay, upper, precision=EXACT, preferred_element_type=F32)
    last = jnp.broadcast_to(cum[:, tokens - 1 :], cum.shape)
    gamma = jnp.exp(cum) * flag_ref[0, :1]
    back = jnp.exp(last - cum) * flag_ref[1, :1]
    whole = jnp.exp(last) * flag_ref[2, :1]
    swapped = parity() == 1
    tall = []
    for part in range(len(parts)):
        sides = [slice(part * width + side * half, part * width + (side + 1) * half) for side in range(2)]
        for turn in range(2):
            same, other = sides[turn], sides[1 - turn]
            for table in (cum, beta, beta * gamma, gamma):
                tall.append(jnp.where(swapped, table[other], table[same]))
            for place, table in enumerate((cum, back, whole)):
                row_ref[part, turn, place * half : (place + 1) * half, :] = jnp.where(
                    swapped, table[other], table[same]
                )
    col_ref[...] = jnp.transpose(jnp.concatenate(tall, axis=0))


def gates(parts, decay_rows, beta_rows, flags, biases, *after):
    heads, tokens = decay_rows.shape
    bias_rows = [row for _, row in biases]
    width = heads // lax.axis_size("head")
    half = width // 2
    count = len(parts)
    arrays = (decay_rows, beta_rows, flags) + tuple(array for array, _ in biases) + after
    return pl.pallas_call(
        functools.partial(gates_kernel, parts, bias_rows, width),
        out_shape=(
            jax.ShapeDtypeStruct((tokens, 4 * count * width), F32),
            jax.ShapeDtypeStruct((count, 2, 3 * half, tokens), F32),
        ),
        in_specs=[whole_vmem()] * len(arrays),
        out_specs=(whole_vmem(),) * 2,
        compiler_params=params(),
        cost_estimate=cost(),
        name="gates",
    )(*arrays)


def fetch_kernel(parts, half, with_resets, *refs):
    if with_resets:
        doc_ref, refs = refs[0], refs[1:]
    k_hbm, v_hbm = refs[:2]
    k_ref, sems = refs[-2:]
    normed_ref, turned_ref, v_ref = refs[-7:-4] if with_resets else refs[-5:-2]
    span = v_ref.shape[-1]
    size = span // half
    copies = {}
    for number, (source, target) in enumerate(((k_hbm, k_ref), (v_hbm, v_ref))):
        for turn in (1, 0):
            for place, part in enumerate(parts):
                at = 2 * chunk_of(part) + jnp.bitwise_xor(turn, parity())
                strip = pl.ds(pl.multiple_of(at * span, span), span)
                copy = pltpu.make_async_copy(
                    source.at[:, strip], target.at[place, turn], sems.at[number, place, turn]
                )
                copy.start()
                copies[number, place, turn] = copy
    if with_resets:
        gap_ref, flag_ref = refs[-4:-2]
        tokens = gap_ref.shape[0]
        row, column = masks(tokens)
        groups = tokens // C
        row_resets = jnp.zeros_like(row)
        column_resets = jnp.zeros_like(row)
        for group in range(groups):
            flag = doc_ref[lax.axis_index("head") * groups + group]
            row_resets = row_resets + jnp.where(row >= group * C, flag, 0)
            column_resets = column_resets + jnp.where(column >= group * C, flag, 0)
        gap_ref[...] = jnp.where(jnp.logical_and(row >= column, row_resets == column_resets), 0.0, MASKED)
        resets = column_resets[:8]
        final = row_resets[tokens - 8 :]
        flag_ref[0] = jnp.where(resets == 0, 1.0, 0.0)
        flag_ref[1] = jnp.where(resets == final, 1.0, 0.0)
        flag_ref[2] = jnp.where(final == 0, 1.0, 0.0)
    for turn in (1, 0):
        for place in range(len(parts)):
            copies[0, place, turn].wait()
            for j in range(half):
                keys = k_ref[place, turn, :, j * size : (j + 1) * size].astype(F32)
                keys = (keys * lax.rsqrt(jnp.sum(keys * keys, axis=-1, keepdims=True) + 1e-06)).astype(BF16)
                normed_ref[place, turn, j] = keys
                turned_ref[place, turn, j] = jnp.transpose(keys)
    for turn in (1, 0):
        for place in range(len(parts)):
            copies[1, place, turn].wait()


def fetch(parts, half, size, doc_start, keys, values, *after):
    tokens = keys.shape[0]
    count = len(parts)
    strips = jax.ShapeDtypeStruct((count, 2, tokens, half * size), BF16)
    outs = [
        jax.ShapeDtypeStruct((count, 2, half, tokens, size), BF16),
        jax.ShapeDtypeStruct((count, 2, half, size, tokens), BF16),
        strips,
    ]
    specs = [in_hbm()] * 2 + [whole_vmem()] * len(after)
    arrays = [keys, values, *after]
    if doc_start is not None:
        outs += [jax.ShapeDtypeStruct((tokens, tokens), F32), jax.ShapeDtypeStruct((3, 8, tokens), F32)]
        specs = [whole_smem()] + specs
        arrays = [doc_start] + arrays
    return pl.pallas_call(
        functools.partial(fetch_kernel, parts, half, doc_start is not None),
        out_shape=tuple(outs),
        in_specs=specs,
        out_specs=(whole_vmem(),) * len(outs),
        scratch_shapes=[pltpu.VMEM(strips.shape, BF16), pltpu.SemaphoreType.DMA((2, count, 2))],
        compiler_params=params(REFETCH_BYTES if after else FETCH_BYTES),
        cost_estimate=cost(),
        name="fetch",
    )(*arrays)


def local_kernel(units, *refs):
    normed_ref, turned_ref, v_ref, gap_ref, col_ref, row_ref = refs[:6]
    outs = refs[-2 * len(units) :]
    tokens = gap_ref.shape[0]
    half, size = outs[0].shape[:2]
    row, column = masks(tokens)
    apart = jnp.bitwise_xor(row, column)
    eye = jnp.where(row == column, 1.0, 0.0)
    strict = row > column
    lane_block = lax.shift_right_logical(column[:BASE], BASE.bit_length() - 1)
    inside = jnp.bitwise_and(column[:BASE], BASE - 1)
    small_eye = jnp.where(row[:BASE] == inside, 1.0, 0.0)
    gap = gap_ref[...]
    every = range(len(units) * half)

    def unit_of(i):
        return units[i // half] + (i % half,)

    def tall_of(table, i):
        at, turn, j = unit_of(i)
        at = ((2 * at + turn) * 4 + table) * half + j
        return col_ref[:, at : at + 1]

    def wide_of(table, i):
        at, turn, j = unit_of(i)
        return row_ref[at, turn, table * half + j : table * half + j + 1, :]

    lower, inverse = [], []
    for i in every:
        at, turn, j = unit_of(i)
        decay = jnp.exp(tall_of(0, i) - wide_of(0, i) + gap)
        gram = dot(normed_ref[at, turn, j], turned_ref[at, turn, j])
        low = jnp.where(strict, tall_of(1, i) * decay * gram, 0.0)
        packed = jnp.zeros((BASE, tokens), F32)
        for top in range(0, tokens, BASE):
            packed = jnp.where(lane_block == top // BASE, low[top : top + BASE], packed)
        solution_rows = small_eye
        for k in range(BASE - 1):
            factor = jnp.take_along_axis(packed, column[:BASE] - inside + k, axis=1, mode="promise_in_bounds")
            solution_rows = solution_rows - factor * solution_rows[k : k + 1]
        inverse.append(
            jnp.concatenate(
                [jnp.where(lane_block == at_block, solution_rows, 0.0) for at_block in range(tokens // BASE)],
                axis=0,
            )
        )
        lower.append(low.astype(BF16))
    nothing = jnp.zeros((tokens, tokens), BF16)
    block = BASE
    while block < tokens:
        small = [inverse[j].astype(BF16) for j in every]
        step = jnp.logical_and(apart >= block, apart < 2 * block)
        masked = [jnp.where(step, lower[j], nothing) for j in every]
        spans = [slice(top, top + block) for top in range(block, tokens, 2 * block)]

        def odd(array):
            return jnp.concatenate([array[s] for s in spans], axis=0)

        def spread(array, evens):
            pieces = []
            for i, s in enumerate(spans):
                pieces.append(evens[s.start - block : s.start])
                pieces.append(array[i * block : (i + 1) * block])
            return jnp.concatenate(pieces, axis=0)

        inner = [spread(dot(odd(masked[j]), small[j]).astype(BF16), nothing) for j in every]
        inverse = [
            spread(odd(inverse[j]) - dot(odd(small[j]), inner[j]), inverse[j]) for j in every
        ]
        block *= 2
    solved = []
    for i in every:
        at, turn, j = unit_of(i)
        lanes = slice(j * size, (j + 1) * size)
        keys = tall_of(2, i) * normed_ref[at, turn, j].astype(F32)
        values = tall_of(1, i) * v_ref[at, turn, :, lanes].astype(F32)
        right = jnp.concatenate([keys.astype(BF16), values.astype(BF16)], axis=1)
        solved.append(dot(inverse[i].astype(BF16), right).astype(BF16))
    for i in every:
        at, turn, j = unit_of(i)
        ab_ref, solved_ref = outs[2 * (i // half) : 2 * (i // half) + 2]
        solved_ref[j] = solved[i]
        after = turned_ref[at, turn, j].astype(F32) * wide_of(1, i)
        both = dot(after.astype(BF16), solved[i])
        ab_ref[j, :, :size] = (eye * wide_of(2, i) - both[:, :size]).astype(BF16)
        ab_ref[j, :, size:] = both[:, size:].astype(BF16)


def local(units, fetched, gap, tables, *after):
    half, tokens, size = fetched[0].shape[2:]
    result = jax.ShapeDtypeStruct((half, tokens, 2 * size), BF16)
    arrays = tuple(fetched) + (gap,) + tuple(tables) + after
    outs = pl.pallas_call(
        functools.partial(local_kernel, units),
        out_shape=(result,) * (2 * len(units)),
        in_specs=[whole_vmem()] * len(arrays),
        out_specs=(whole_vmem(),) * (2 * len(units)),
        compiler_params=params(),
        cost_estimate=cost(),
        name="local_tokens",
    )(*arrays)
    return [(outs[2 * i], outs[2 * i + 1]) for i in range(len(units))]


def outlook_kernel(at, part, q_hbm, turned_ref, gap_ref, col_ref, row_ref, *refs):
    solved_refs = refs[:2]
    qo_refs = refs[-4:-2]
    q_ref, sems = refs[-2:]
    half, tokens = solved_refs[0].shape[:2]
    size = solved_refs[0].shape[2] // 2
    span = half * size
    copies = []
    for turn in range(2):
        start = (2 * chunk_of(part) + jnp.bitwise_xor(turn, parity())) * span
        strip = pl.ds(pl.multiple_of(start, span), span)
        copies.append(pltpu.make_async_copy(q_hbm.at[:, strip], q_ref.at[turn], sems.at[turn]))
        copies[-1].start()
    gap = gap_ref[...]
    every = [(turn, j) for turn in range(2) for j in range(half)]

    def tall_of(table, turn, j):
        place = ((2 * at + turn) * 4 + table) * half + j
        return col_ref[:, place : place + 1]

    decay = {}
    for turn, j in every:
        decay[turn, j] = jnp.exp(tall_of(0, turn, j) - row_ref[at, turn, j : j + 1, :] + gap)
    for copy in copies:
        copy.wait()
    mix = {}
    for turn, j in every:
        gram = dot(q_ref[turn, :, j * size : (j + 1) * size], turned_ref[at, turn, j])
        mix[turn, j] = (decay[turn, j] * gram).astype(BF16)
    for turn, j in every:
        both = dot(mix[turn, j], solved_refs[turn][j])
        through = tall_of(3, turn, j) * q_ref[turn, :, j * size : (j + 1) * size].astype(F32)
        qo_refs[turn][j, :, :size] = (through - both[:, :size]).astype(BF16)
        qo_refs[turn][j, :, size:] = both[:, size:].astype(BF16)


def outlook(at, part, queries, turned, gap, tables, solved, *after):
    half, tokens, wide = solved[0].shape
    arrays = (queries, turned, gap) + tuple(tables) + tuple(solved) + after
    return pl.pallas_call(
        functools.partial(outlook_kernel, at, part),
        out_shape=(jax.ShapeDtypeStruct(solved[0].shape, BF16),) * 2,
        in_specs=[in_hbm()] + [whole_vmem()] * (len(arrays) - 1),
        out_specs=(whole_vmem(),) * 2,
        scratch_shapes=[pltpu.VMEM((2, tokens, half * wide // 2), BF16), pltpu.SemaphoreType.DMA((2,))],
        compiler_params=params(),
        cost_estimate=cost(),
        name="outlook",
    )(*arrays)


def joined(earlier, later):
    size = earlier.shape[0]
    product = dot(later[:, :size], earlier)
    return jnp.concatenate([product[:, :size], product[:, size:] + later[:, size:].astype(F32)], axis=1)


def pick(later, own, received):
    return jnp.where(later, received, own), jnp.where(later, own, received)


def compose_kernel(bit, with_token, carried, own_ref, got_ref, *rest):
    out_ref = rest[-1]
    if with_token:
        out_ref, token_ref = rest[-2:]
        token_ref[...] = jnp.zeros_like(token_ref)
        for row in range(carried):
            token_ref[row : row + 1, : rest[row].shape[1]] = rest[row][...]
    later = is_later(bit)
    for j in range(out_ref.shape[0]):
        earlier_block, later_block = pick(later, own_ref[j], got_ref[j])
        out_ref[j] = joined(earlier_block, later_block).astype(BF16)


def compose(bit, own, got, *after, with_token=False, carried=0):
    outs = (jax.ShapeDtypeStruct(own.shape, BF16),)
    if with_token:
        outs += (jax.ShapeDtypeStruct((8, 128), F32),)
    done = pl.pallas_call(
        functools.partial(compose_kernel, bit, with_token, carried),
        out_shape=outs,
        in_specs=[whole_vmem()] * (2 + len(after)),
        out_specs=(whole_vmem(),) * len(outs),
        compiler_params=params(),
        cost_estimate=cost(),
        name="compose",
    )(own, got, *after)
    return done if with_token else done[0]


def doubling_kernel(bit, first, last, *refs):
    later = is_later(bit)
    own_ref, got_ref = refs[:2]
    total_ref, before_ref = refs[-2:]
    heads, size = own_ref.shape[:2]
    row = lax.broadcasted_iota(jnp.int32, (size, 2 * size), 0)
    column = lax.broadcasted_iota(jnp.int32, (size, 2 * size), 1)
    neutral = jnp.where(row == column, 1.0, 0.0).astype(BF16)
    for j in range(heads):
        earlier_block, later_block = pick(later, own_ref[j], got_ref[j])
        total = joined(earlier_block, later_block).astype(BF16)
        total_ref[j] = total[:, size:] if last else total
        if first:
            before_ref[j] = jnp.where(later, got_ref[j], neutral)
        else:
            before = refs[2][j]
            before_ref[j] = jnp.where(later, joined(got_ref[j], before).astype(BF16), before)


def doubling(bit, last, own, got, before, *after):
    first = before is None
    arrays = (own, got) if first else (own, got, before)
    arrays += after
    heads, size = own.shape[:2]
    total = jax.ShapeDtypeStruct((heads, size, size if last else 2 * size), BF16)
    return pl.pallas_call(
        functools.partial(doubling_kernel, bit, first, last),
        out_shape=(total, jax.ShapeDtypeStruct(own.shape, BF16)),
        in_specs=[whole_vmem()] * len(arrays),
        out_specs=(whole_vmem(), whole_vmem()),
        compiler_params=params(),
        cost_estimate=cost(),
        name="doubling",
    )(*arrays)


def descend_kernel(bits, top, threaded, with_token, *refs):
    count = len(bits)
    start = 2 if top is not None else 1
    blocks = refs[start : start + 2 * count]
    outs = refs[start + 2 * count + threaded :]
    sends, kept_ref = outs[:count], outs[count]
    if with_token:
        outs[-1][...] = jnp.zeros_like(outs[-1])
    size = kept_ref.shape[-1]
    every = range(kept_ref.shape[0])
    if top is None:
        state = [refs[0][j] for j in every]
    else:
        carried = [dot(refs[1][j, :, :size], refs[0][j]) + refs[1][j, :, size:].astype(F32) for j in every]
        state = [jnp.where(is_later(top), carried[j].astype(BF16), refs[1][j, :, size:]) for j in every]
    for level, bit in enumerate(bits):
        later = is_later(bit)
        own_ref, got_ref = blocks[2 * level : 2 * level + 2]
        earlier = [jnp.where(later, got_ref[j], own_ref[j]) for j in every]
        after = [
            (dot(earlier[j][:, :size], state[j]) + earlier[j][:, size:].astype(F32)).astype(BF16) for j in every
        ]
        for j in every:
            sends[level][j] = jnp.where(later, state[j], after[j])
        state = [jnp.where(later, after[j], state[j]) for j in every]
    for j in every:
        kept_ref[j] = state[j]


def descend(bits, top, sources, blocks, thread, *after, with_token=False):
    heads, size = sources[0].shape[0], sources[0].shape[1]
    arrays = list(sources) + [array for pair in blocks for array in pair]
    specs = [whole_vmem()] * len(arrays)
    outs = len(bits) + 1
    shapes = [jax.ShapeDtypeStruct((heads, size, size), BF16)] * outs
    out_specs = [whole_vmem()] * outs
    aliases = {}
    if thread is not None:
        arrays.append(thread)
        specs.append(whole_vmem())
        shapes.append(jax.ShapeDtypeStruct(thread.shape, thread.dtype))
        out_specs.append(whole_vmem())
        aliases = {len(arrays) - 1: outs}
    if with_token:
        shapes.append(jax.ShapeDtypeStruct((8, 128), F32))
        out_specs.append(whole_vmem())
    arrays += after
    specs += [whole_vmem()] * len(after)
    return pl.pallas_call(
        functools.partial(descend_kernel, bits, top, int(thread is not None) + len(after), with_token),
        out_shape=tuple(shapes),
        in_specs=specs,
        out_specs=tuple(out_specs),
        input_output_aliases=aliases,
        compiler_params=params(),
        cost_estimate=cost(),
        name="descend",
    )(*arrays)


def finish_kernel(unit, earlier_unit, is_last, gain_ref, state_ref, qo_ref, gate_ref, *rest):
    sems = rest[-1]
    strip_ref = rest[-2]
    out_hbm = rest[-3]
    half, size = state_ref.shape[0], state_ref.shape[-1]
    span = half * size

    def start_of(part, turn):
        return (2 * chunk_of(part) + jnp.bitwise_xor(turn, parity())) * span

    stores = []
    if earlier_unit is not None:
        there = pl.ds(pl.multiple_of(start_of(*earlier_unit), span), span)
        stores.append(pltpu.make_async_copy(rest[0], out_hbm.at[:, there], sems.at[half]))
        stores[-1].start()
    cores = []
    for j in range(half):
        core = dot(qo_ref[j, :, :size], state_ref[j]) + qo_ref[j, :, size:].astype(F32)
        cores.append(core.astype(BF16).astype(F32))
    for j in range(half):
        core = cores[j]
        scaled = core * lax.rsqrt(jnp.mean(core * core, axis=-1, keepdims=True) + 1e-06) * gain_ref[...]
        there = pl.ds(pl.multiple_of(start_of(*unit) + j * size, size), size)
        gate = gate_ref[:, there].astype(F32)
        lanes = slice(j * size, (j + 1) * size)
        strip_ref[:, lanes] = (scaled * (0.5 * gate) * (1.0 + jnp.tanh(0.5 * gate))).astype(BF16)
        if is_last:
            stores.append(pltpu.make_async_copy(strip_ref.at[:, lanes], out_hbm.at[:, there], sems.at[j]))
            stores[-1].start()
    for store in stores:
        store.wait()


def finish(unit, is_last, state, qo, gate, gain, previous):
    half, tokens, size = state.shape[0], gate.shape[0], state.shape[-1]
    specs = [whole_vmem()] * 4
    arrays = [gain, state, qo, gate]
    aliases = {}
    earlier_unit = None
    if previous is not None:
        result, strip, earlier_unit = previous
        specs += [whole_vmem()]
        arrays += [strip]
        if result is not None:
            specs += [in_hbm()]
            arrays += [result]
            aliases = {len(arrays) - 1: 0}
    strip_shape = (tokens, half * size)
    outs = (jax.ShapeDtypeStruct(gate.shape, BF16),)
    out_specs = (in_hbm(),)
    scratch = [pltpu.SemaphoreType.DMA((1 + half,))]
    if is_last:
        scratch = [pltpu.VMEM(strip_shape, BF16)] + scratch
    else:
        outs += (jax.ShapeDtypeStruct(strip_shape, BF16),)
        out_specs += (whole_vmem(),)
    done = pl.pallas_call(
        functools.partial(finish_kernel, unit, earlier_unit, is_last),
        out_shape=outs,
        in_specs=specs,
        out_specs=out_specs,
        scratch_shapes=scratch,
        input_output_aliases=aliases,
        compiler_params=params(),
        cost_estimate=cost(),
        name="finish",
    )(*arrays)
    return done[0] if is_last else (done[0], done[1], unit)


def body(
    head_count,
    context_count,
    queries,
    key_input,
    value_input,
    gate_input,
    decay_logit,
    beta_logit,
    decay_bias,
    norm_gain,
    doc_start,
):
    head_bits = head_count.bit_length() - 1
    context_bits = context_count.bit_length() - 1

    def swap(array, axis, distance):
        count = head_count if axis == "head" else context_count
        return lax.ppermute(array, axis, [(i, i ^ distance) for i in range(count)])

    head_bit = [("head", bit) for bit in range(head_bits)]
    context_bit = [("context", bit) for bit in range(context_bits)]
    own_bias = decay_bias[None, :]
    far_biases = [own_bias] + [swap(own_bias, "head", other) for other in range(1, head_count // 2)]
    half, size = decay_bias.shape[0] // 2, norm_gain.shape[0]
    inputs = (key_input, value_input)
    decay_rows, beta_rows = decay_logit.T, beta_logit.T

    ab, solved, qo = {}, {}, {}
    levels = [{} for _ in range(head_bits)]
    far_parts = list(reversed(range(head_count // 2, head_count)))
    near_parts = [part - head_count // 2 for part in far_parts]

    def work(parts, turn, fetched, gap, tables, *after):
        names = far_parts if parts[0] in far_parts else near_parts
        units = [(names.index(part), turn) for part in parts]
        for part, (block, out) in zip(parts, local(units, fetched, gap, tables, *after)):
            ab[part, turn], solved[part, turn] = block, out

    def fold(part, turn, bit, *after, **options):
        if bit == 0:
            return ab[part, turn]
        got = swap(fold(part | 1 << (bit - 1), turn, bit - 1), "head", 1 << (bit - 1))
        near = fold(part, turn, bit - 1)
        levels[bit - 1][part, turn] = (near, got)
        return compose(head_bit[bit - 1], near, got, *after, **options)

    under = head_bits - 1
    *fetched, gap, flags = fetch(far_parts, half, size, doc_start, *inputs)
    tables = gates(far_parts, decay_rows, beta_rows, flags, [(array, 0) for array in far_biases])
    work(far_parts, 1, fetched, gap, tables)
    far, got, near, chip = {}, {}, {}, {}
    first_done = ab[far_parts[-1], 1]
    fetched_near = fetch(near_parts, half, size, None, *inputs, first_done)
    far[1], token = fold(
        1 << under, 1, under, *far_biases, fetched_near[0], with_token=True, carried=len(far_biases)
    )
    near_bias = swap(token, "head", 1 << under)
    got[1] = swap(far[1], "head", 1 << under)
    work(far_parts, 0, fetched, gap, tables, swap(token, "head", 1))
    near_biases = [(near_bias, row) for row in range(len(near_parts))]
    near_tables = gates(near_parts, decay_rows, beta_rows, flags, near_biases, ab[far_parts[-1], 0])
    work(near_parts, 1, fetched_near, gap, near_tables)
    far[0] = fold(1 << under, 0, under)
    got[0] = swap(far[0], "head", 1 << under)
    near[1] = fold(0, 1, under, far[0])
    chip[1], token = compose(head_bit[under], near[1], got[1], with_token=True)
    across = swap(chip[1], "context", 1)
    work(near_parts, 0, fetched_near, gap, near_tables, swap(token, "head", 1))

    def look(part, *after):
        names, data, known = (
            (far_parts, fetched, tables) if part in far_parts else (near_parts, fetched_near, near_tables)
        )
        qo[part, 0], qo[part, 1] = outlook(
            names.index(part), part, queries, data[1], gap, known, (solved[part, 0], solved[part, 1]), *after
        )

    every_part = far_parts + near_parts
    look(every_part[0], ab[near_parts[-1], 0])
    near[0] = fold(0, 0, under, qo[every_part[0], 0])
    chip[0] = compose(head_bit[under], near[0], got[0])
    for turn in (1, 0):
        levels[under][0, turn] = (near[turn], got[turn])

    x_pair = (chip[0], across)
    total = compose(context_bit[0], *x_pair)
    before = None
    for part in every_part[1:]:
        look(part, chip[0])
    for bit in range(1, context_bits - 1):
        other = swap(total, "context", 1 << bit)
        done_by = tuple(qo[part, 0] for part in every_part[1:]) if bit == 1 else ()
        total, before = doubling(context_bit[bit], bit == context_bits - 2, total, other, before, *done_by)
    other = swap(total, "context", 1 << (context_bits - 1))

    gain = norm_gain[None, :]
    states = {}
    result = None
    descending = list(reversed(range(head_bits)))
    first = descend([context_bit[0]], context_bit[-1], (other, before), [x_pair], None, with_token=True)
    arriving = [(0, 1, head_bits, swap(first[0], "context", 1))]
    outs = descend(
        [head_bit[bit] for bit in descending],
        None,
        (first[1],),
        [levels[bit][0, 0] for bit in descending],
        None,
        swap(first[-1], "head", 1),
    )
    states[0, 0] = outs[-1]
    for level, bit in enumerate(descending):
        arriving.append((1 << bit, 0, bit, swap(outs[level], "head", 1 << bit)))
    ready = [(0, 0)]
    total_units = 2 * head_count

    def write(part, turn, result):
        done.append((part, turn))
        return finish(
            (part, turn),
            len(done) == total_units,
            states[part, turn],
            qo[part, turn],
            gate_input,
            gain,
            result,
        )

    done = []
    while arriving or ready:
        for part, turn in ready:
            result = write(part, turn, result)
        ready = []
        leaves = [entry for entry in arriving if entry[2] == 0]
        inner = [entry for entry in arriving if entry[2] > 0]
        arriving = []
        for part, turn, _, state in leaves:
            states[part, turn] = state
            result = write(part, turn, result)
        tokens = ()
        for number, (part, turn, below, state) in enumerate(inner):
            down = list(reversed(range(below)))
            more = number + 1 < len(inner)
            outs = descend(
                [head_bit[bit] for bit in down],
                None,
                (state,),
                [levels[bit][part, turn] for bit in down],
                result[1],
                *tokens,
                with_token=more,
            )
            states[part, turn] = outs[below]
            result = (result[0], outs[below + 1], result[2])
            ready.append((part, turn))
            for level, bit in enumerate(down):
                arriving.append((part | 1 << bit, turn, bit, swap(outs[level], "head", 1 << bit)))
            tokens = (swap(outs[-1], "head", 1),) if more else ()
    return result


def solution(mesh):
    return jax.shard_map(
        functools.partial(body, mesh.shape["head"], mesh.shape["context"]),
        mesh=mesh,
        in_specs=(
            P(("context", "head"), None),
            P(("context", "head"), None),
            P(("context", "head"), None),
            P(("context", "head"), None),
            P(("context", "head"), None),
            P(("context", "head"), None),
            P("head"),
            P(),
            P("context"),
        ),
        out_specs=P(("context", "head"), None),
        check_vma=False,
    )
```

time: 66.3 us -> 60 us (0.905)
  Pallas kernels: 30.9 us -> 26.5 us
  waiting for transfers between devices: 12.6 us -> 9.98 us
  starting transfers between devices: 18.5 us -> 20.7 us
  local copies, waits for them, and re-layouts: 3.4 us -> 1.87 us
    pallas_call x26 -> x27, Pallas kernels: 28.5 us -> 24.8 us  [the longest x4 9.09 us: local(): pl.pallas_call(functools.partial(local_kernel, units), out_shape=(result,...]
    ppermute x19 -> x22, waiting for transfers between devices: 12.6 us -> 9.98 us  [swap(): return lax.ppermute(array, axis, [(i, i ^ distance) for i in range(count)])]
    ppermute x19 -> x22, starting transfers between devices: 18.5 us -> 20.7 us  [swap(): return lax.ppermute(array, axis, [(i, i ^ distance) for i in range(count)])]
    unnamed x34 -> x30, local copies, waits for them, and re-layouts: 3.4 us -> 1.87 us
    pallas_call x4 -> x5, Pallas kernels: 2.16 us -> 1.43 us  [descend(): pl.pallas_call(functools.partial(descend_kernel, bits, top, int(thread is...]
  transfers between devices with their start and end apart: 19 -> 22, of which waited for: 5 -> 8; matrix products, arithmetic and copies ran while one was open for 0% -> 0% of each run, Pallas kernels for 38% -> 36%
where the time goes in v3:
time: 60 us; the launch traced here: 59.6 us
  Pallas kernels  26.5 us (44%)
  starting transfers between devices  20.7 us (34%)
  waiting for transfers between devices  9.98 us (17%)
  local copies, waits for them, and re-layouts  1.87 us (3%)
    ppermute x22, starting transfers between devices, swap(): return lax.ppermute(array, axis, [(i, i ^ distance) for i in range(count)])  20.7 us
    ppermute x22, waiting for transfers between devices, swap(): return lax.ppermute(array, axis, [(i, i ^ distance) for i in range(count)])  9.98 us
    pallas_call x4, Pallas kernels, local(): pl.pallas_call(functools.partial(local_kernel, units), out_shape=(result,...  9.09 us
    pallas_call x8, Pallas kernels, finish(): pl.pallas_call(functools.partial(finish_kernel, unit, earlier_unit, is_la...  6.87 us
    pallas_call x2, Pallas kernels, fetch(): pl.pallas_call(functools.partial(fetch_kernel, parts, half, doc_start is...  3.44 us
    pallas_call x4, Pallas kernels, outlook(): pl.pallas_call(functools.partial(outlook_kernel, at, part), out_shape=(ja...  3.11 us
    unnamed x30, local copies, waits for them, and re-layouts  1.87 us
    pallas_call x7, Pallas kernels, compose(): pl.pallas_call(functools.partial(compose_kernel, bit, with_token, carried...  1.55 us
  transfers between devices with their start and end apart: 22, of which 8 were waited for; matrix products, arithmetic and copies ran while one was open for 0% of the time, Pallas kernels for 36%

profile of v3, /device:TPU:1, one launch (start us, length us, event | category | flops | bytes accessed | tf_op | source)
XLA Modules:
  0.0 59.6 jit_solution(15839960338549348354)
XLA Ops:
  0.7 2.4 %fetch.2 = (bf16[2,2,4,128,128]{4,3,2,1,0:T(8,128)(2,1)S(1)}, bf16[2,2,4,128,128]{4,3,2,1,0:T(8,128)(2,1)S(1)}, bf16[2,2,128,512]{3,2,1,0:T(8,128)(2,1)S(1)}, f32[128,128]{1,0:T(8,128)S(1)}, f32[3,8,128]{2,1,0:T(8,128)S(1)}) custom-call(s32[8]{0:T(128)S(1)} %copy-done.8, bf16[128,4096]{1,0:T(8,128)(2,1)} %refs_0_.3, bf16[128,4096]{1,0:T(8,128)(2,1)} %refs_1_.3), custom_call_target="tpu_custom_call" | custom-call | flops 10000000000 | bytes 100000000 | tf_op jit(solution)/shard_map/fetch/pallas_call | solution.py:190
  3.5 2.3 %local_tokens.4 = (bf16[4,128,256]{2,1,0:T(8,128)(2,1)S(1)}, bf16[4,128,256]{2,1,0:T(8,128)(2,1)S(1)}, bf16[4,128,256]{2,1,0:T(8,128)(2,1)S(1)}, bf16[4,128,256]{2,1,0:T(8,128)(2,1)S(1)}) custom-call(bf16[2,2,4,128,128]{4,3,2,1,0:T(8,128)(2,1)S(1)} %get-tuple-element.78.refs_0_, bf16[2,2,4,128,128]{4,3,2,1,0:T(8,128)(2,1)S(1)} %get-tuple-element.79.refs_1_.turned_ref, ...), custom_call_target="tpu_custom_call" | custom-call | flops 10000000000 | bytes 100000000 | tf_op jit(solution)/shard_map/local_tokens/pallas_call | solution.py:294
  6.3 1.1 %fetch.3 = (bf16[2,2,4,128,128]{4,3,2,1,0:T(8,128)(2,1)S(1)}, bf16[2,2,4,128,128]{4,3,2,1,0:T(8,128)(2,1)S(1)}, bf16[2,2,128,512]{3,2,1,0:T(8,128)(2,1)S(1)}) custom-call(bf16[128,4096]{1,0:T(8,128)(2,1)S(1)} %copy-done, bf16[128,4096]{1,0:T(8,128)(2,1)S(1)} %copy-done.1, bf16[4,128,256]{2,1,0:T(8,128)(2,1)S(1)} %get-tuple-element.85.refs_2_.own_ref.refs_1_), custom_call_target="tpu_custom_call" | custom-call | flops 10000000000 | bytes 100000000 | tf_op jit(solution)/shard_map/fetch/pallas_call | solution.py:190
  8.1 2.4 %collective-permute-start.2 = (f32[8,128]{1,0:T(8,128)S(1)}, f32[8,128]{1,0:T(8,128)S(1)}, u32[]{:S(2)}, u32[]{:S(2)}) collective-permute-start(f32[8,128]{1,0:T(8,128)S(1)} %get-tuple-element.90), channel_id=1, source_target_pairs={{0,2},{1,3},{2,0},{3,1},{4,6},{5,7},{6,4},{7,5},{8,10},{9,11},{10,... | collective-permute-start | bytes 12296 | tf_op jit(solution)/shard_map/ppermute | solution.py:580
  10.6 2.3 %local_tokens.5 = (bf16[4,128,256]{2,1,0:T(8,128)(2,1)S(1)}, bf16[4,128,256]{2,1,0:T(8,128)(2,1)S(1)}, bf16[4,128,256]{2,1,0:T(8,128)(2,1)S(1)}, bf16[4,128,256]{2,1,0:T(8,128)(2,1)S(1)}) custom-call(bf16[2,2,4,128,128]{4,3,2,1,0:T(8,128)(2,1)S(1)} %get-tuple-element.78.refs_0_, bf16[2,2,4,128,128]{4,3,2,1,0:T(8,128)(2,1)S(1)} %get-tuple-element.79.refs_1_.turned_ref, ...), custom_call_target="tpu_custom_call" | custom-call | flops 10000000000 | bytes 100000000 | tf_op jit(solution)/shard_map/local_tokens/pallas_call | solution.py:294
  13.9 2.3 %local_tokens.6 = (bf16[4,128,256]{2,1,0:T(8,128)(2,1)S(1)}, bf16[4,128,256]{2,1,0:T(8,128)(2,1)S(1)}, bf16[4,128,256]{2,1,0:T(8,128)(2,1)S(1)}, bf16[4,128,256]{2,1,0:T(8,128)(2,1)S(1)}) custom-call(bf16[2,2,4,128,128]{4,3,2,1,0:T(8,128)(2,1)S(1)} %get-tuple-element.86.rest_2_.refs_0_, ...), custom_call_target="tpu_custom_call" | custom-call | flops 10000000000 | bytes 100000000 | tf_op jit(solution)/shard_map/local_tokens/pallas_call | solution.py:294
  18.3 1.3 %collective-permute-start.7 = (f32[8,128]{1,0:T(8,128)S(1)}, f32[8,128]{1,0:T(8,128)S(1)}, u32[]{:S(2)}, u32[]{:S(2)}) collective-permute-start(f32[8,128]{1,0:T(8,128)S(1)} %get-tuple-element.98), channel_id=1, source_target_pairs={{0,1},{1,0},{2,3},{3,2},{4,5},{5,4},{6,7},{7,6},{8,9},{9,8},{10,11... | collective-permute-start | bytes 12296 | tf_op jit(solution)/shard_map/ppermute | solution.py:580
  20.2 1.2 %collective-permute-start.10 = (bf16[4,128,256]{2,1,0:T(8,128)(2,1)S(1)}, bf16[4,128,256]{2,1,0:T(8,128)(2,1)S(1)}, u32[]{:S(2)}, u32[]{:S(2)}) collective-permute-start(bf16[4,128,256]{2,1,0:T(8,128)(2,1)S(1)} %get-tuple-element.104), channel_id=1, source_target_pairs={{0,4},{4,0},{8,12},{12,8},{16,20},{20,16},{24,28},{28,24},{1,5},{5... | collective-permute-start | bytes 786440 | tf_op jit(solution)/shard_map/ppermute | solution.py:580
  21.4 2.3 %local_tokens.7 = (bf16[4,128,256]{2,1,0:T(8,128)(2,1)S(1)}, bf16[4,128,256]{2,1,0:T(8,128)(2,1)S(1)}, bf16[4,128,256]{2,1,0:T(8,128)(2,1)S(1)}, bf16[4,128,256]{2,1,0:T(8,128)(2,1)S(1)}) custom-call(bf16[2,2,4,128,128]{4,3,2,1,0:T(8,128)(2,1)S(1)} %get-tuple-element.86.rest_2_.refs_0_, ...), custom_call_target="tpu_custom_call" | custom-call | flops 10000000000 | bytes 100000000 | tf_op jit(solution)/shard_map/local_tokens/pallas_call | solution.py:294
  23.7 1.0 %collective-permute-start.8 = (bf16[4,128,256]{2,1,0:T(8,128)(2,1)S(1)}, bf16[4,128,256]{2,1,0:T(8,128)(2,1)S(1)}, u32[]{:S(2)}, u32[]{:S(2)}) collective-permute-start(bf16[4,128,256]{2,1,0:T(8,128)(2,1)S(1)} %get-tuple-element.100), channel_id=1, source_target_pairs={{0,1},{1,0},{2,3},{3,2},{4,5},{5,4},{6,7},{7,6},{8,9},{9,8},{10,11... | collective-permute-start | bytes 786440 | tf_op jit(solution)/shard_map/ppermute | solution.py:580
  26.1 1.3 %collective-permute-done.9.got_ref.refs_2_ = bf16[4,128,256]{2,1,0:T(8,128)(2,1)S(1)} collective-permute-done((bf16[4,128,256]{2,1,0:T(8,128)(2,1)S(1)}, bf16[4,128,256]{2,1,0:T(8,128)(2,1)S(1)}, u32[]{:S(2)}, u32[]{:S(2)}) %collective-permute-start.9) | collective-permute-done | bytes 262176 | tf_op jit(solution)/shard_map/ppermute | solution.py:580
  27.9 1.4 %collective-permute-start.11 = (bf16[4,128,256]{2,1,0:T(8,128)(2,1)S(1)}, bf16[4,128,256]{2,1,0:T(8,128)(2,1)S(1)}, u32[]{:S(2)}, u32[]{:S(2)}) collective-permute-start(bf16[4,128,256]{2,1,0:T(8,128)(2,1)S(1)} %compose.13.refs_0_), channel_id=1, source_target_pairs={{0,8},{4,12},{8,0},{12,4},{16,24},{20,28},{24,16},{28,20},{1,9},{5... | collective-permute-start | bytes 786440 | tf_op jit(solution)/shard_map/ppermute | solution.py:580
  30.7 1.0 %outlook.6 = (bf16[4,128,256]{2,1,0:T(8,128)(2,1)S(1)}, bf16[4,128,256]{2,1,0:T(8,128)(2,1)S(1)}) custom-call(bf16[128,4096]{1,0:T(8,128)(2,1)S(1)} %copy-done.2, bf16[2,2,4,128,128]{4,3,2,1,0:T(8,128)(2,1)S(1)} %get-tuple-element.87.refs_1_.turned_ref, f32[128,128]{1,0:T(8,128)S(1)} %get-tuple-element.81.refs_3_.gap_ref, ...), custom_call_target="tpu_custom_call" | custom-call | flops 10000000000 | bytes 100000000 | tf_op jit(solution)/shard_map/outlook/pallas_call | solution.py:345
  31.7 2.8 %collective-permute-done.11.refs_1_ = bf16[4,128,256]{2,1,0:T(8,128)(2,1)S(1)} collective-permute-done((bf16[4,128,256]{2,1,0:T(8,128)(2,1)S(1)}, bf16[4,128,256]{2,1,0:T(8,128)(2,1)S(1)}, u32[]{:S(2)}, u32[]{:S(2)}) %collective-permute-start.11) | collective-permute-done | bytes 262176 | tf_op jit(solution)/shard_map/ppermute | solution.py:580
  34.8 2.4 %collective-permute-start.12 = (bf16[4,128,128]{2,1,0:T(8,128)(2,1)S(1)}, bf16[4,128,128]{2,1,0:T(8,128)(2,1)S(1)}, u32[]{:S(2)}, u32[]{:S(2)}) collective-permute-start(bf16[4,128,128]{2,1,0:T(8,128)(2,1)S(1)} %get-tuple-element.114), channel_id=1, source_target_pairs={{0,16},{4,20},{8,24},{12,28},{16,0},{20,4},{24,8},{28,12},{1,17},{... | collective-permute-start | bytes 393224 | tf_op jit(solution)/shard_map/ppermute | solution.py:580
  37.1 4.2 %collective-permute-done.12.refs_0_ = bf16[4,128,128]{2,1,0:T(8,128)(2,1)S(1)} collective-permute-done((bf16[4,128,128]{2,1,0:T(8,128)(2,1)S(1)}, bf16[4,128,128]{2,1,0:T(8,128)(2,1)S(1)}, u32[]{:S(2)}, u32[]{:S(2)}) %collective-permute-start.12) | collective-permute-done | bytes 131104 | tf_op jit(solution)/shard_map/ppermute | solution.py:580
  41.7 3.2 %collective-permute-start.14 = (f32[8,128]{1,0:T(8,128)S(1)}, f32[8,128]{1,0:T(8,128)S(1)}, u32[]{:S(2)}, u32[]{:S(2)}) collective-permute-start(f32[8,128]{1,0:T(8,128)S(1)} %get-tuple-element.118), channel_id=1, source_target_pairs={{0,1},{1,0},{2,3},{3,2},{4,5},{5,4},{6,7},{7,6},{8,9},{9,8},{10,11... | collective-permute-start | bytes 12296 | tf_op jit(solution)/shard_map/ppermute | solution.py:580
  44.8 1.2 %collective-permute-start.13 = (bf16[4,128,128]{2,1,0:T(8,128)(2,1)S(1)}, bf16[4,128,128]{2,1,0:T(8,128)(2,1)S(1)}, u32[]{:S(2)}, u32[]{:S(2)}) collective-permute-start(bf16[4,128,128]{2,1,0:T(8,128)(2,1)S(1)} %get-tuple-element.116), channel_id=1, source_target_pairs={{0,4},{4,0},{8,12},{12,8},{16,20},{20,16},{24,28},{28,24},{1,5},{5... | collective-permute-start | bytes 393224 | tf_op jit(solution)/shard_map/ppermute | solution.py:580
  46.8 1.0 %collective-permute-start.17 = (bf16[4,128,128]{2,1,0:T(8,128)(2,1)S(1)}, bf16[4,128,128]{2,1,0:T(8,128)(2,1)S(1)}, u32[]{:S(2)}, u32[]{:S(2)}) collective-permute-start(bf16[4,128,128]{2,1,0:T(8,128)(2,1)S(1)} %get-tuple-element.125), channel_id=1, source_target_pairs={{0,2},{1,3},{2,0},{3,1},{4,6},{5,7},{6,4},{7,5},{8,10},{9,11},{10,... | collective-permute-start | bytes 393224 | tf_op jit(solution)/shard_map/ppermute | solution.py:580
  48.9 0.9 %finish.9 = (bf16[128,4096]{1,0:T(8,128)(2,1)}, bf16[128,512]{1,0:T(8,128)(2,1)S(1)}) custom-call(f32[1,128]{1,0:T(1,128)S(1)} %bitcast.12, bf16[4,128,128]{2,1,0:T(8,128)(2,1)S(1)} %collective-permute-done.15.state_ref, bf16[4,128,256]{2,1,0:T(8,128)(2,1)S(1)} %get-tuple-element.110.refs_3_.qo_ref, ...), custom_call_target="tpu_custom_call", output_to_operand_aliasing={{0}: (5, {})} | custom-call | flops 10000000000 | bytes 100000000 | tf_op jit(solution)/shard_map/finish/pallas_call | solution.py:548
  51.2 1.0 %collective-permute-start.16 = (bf16[4,128,128]{2,1,0:T(8,128)(2,1)S(1)}, bf16[4,128,128]{2,1,0:T(8,128)(2,1)S(1)}, u32[]{:S(2)}, u32[]{:S(2)}) collective-permute-start(bf16[4,128,128]{2,1,0:T(8,128)(2,1)S(1)} %get-tuple-element.124), channel_id=1, source_target_pairs={{0,2},{1,3},{2,0},{3,1},{4,6},{5,7},{6,4},{7,5},{8,10},{9,11},{10,... | collective-permute-start | bytes 393224 | tf_op jit(solution)/shard_map/ppermute | solution.py:580
  54.9 0.9 %finish.12 = (bf16[128,4096]{1,0:T(8,128)(2,1)}, bf16[128,512]{1,0:T(8,128)(2,1)S(1)}) custom-call(f32[1,128]{1,0:T(1,128)S(1)} %bitcast.15, bf16[4,128,128]{2,1,0:T(8,128)(2,1)S(1)} %collective-permute-done.20.state_ref, bf16[4,128,256]{2,1,0:T(8,128)(2,1)S(1)} %get-tuple-element.130.qo_ref, ...), custom_call_target="tpu_custom_call", output_to_operand_aliasing={{0}: (5, {})} | custom-call | flops 10000000000 | bytes 100000000 | tf_op jit(solution)/shard_map/finish/pallas_call | solution.py:548
  55.9 0.9 %finish.13 = (bf16[128,4096]{1,0:T(8,128)(2,1)}, bf16[128,512]{1,0:T(8,128)(2,1)S(1)}) custom-call(f32[1,128]{1,0:T(1,128)S(1)} %bitcast.16, bf16[4,128,128]{2,1,0:T(8,128)(2,1)S(1)} %collective-permute-done.19.state_ref, bf16[4,128,256]{2,1,0:T(8,128)(2,1)S(1)} %copy-done.12, bf16[128,4096]{1,0:T(8,128)(2,1)S(1)} %copy-done.3, ...), custom_call_target="tpu_custom_call", output_to_operand_aliasing={{0}: (5, {})} | custom-call | flops 10000000000 | bytes 100000000 | tf_op jit(solution)/shard_map/finish/pallas_call | solution.py:548
  58.4 1.0 %finish.15 = bf16[128,4096]{1,0:T(8,128)(2,1)} custom-call(f32[1,128]{1,0:T(1,128)S(1)} %bitcast.18, bf16[4,128,128]{2,1,0:T(8,128)(2,1)S(1)} %collective-permute-done.21.state_ref, bf16[4,128,256]{2,1,0:T(8,128)(2,1)S(1)} %get-tuple-element.144.qo_ref, bf16[128,4096]{1,0:T(8,128)(2,1)S(1)} %copy-done.3, ...), custom_call_target="tpu_custom_call", output_to_operand_aliasing={{}: (5, {})} | custom-call | flops 10000000000 | bytes 100000000 | tf_op jit(solution)/shard_map/finish/pallas_call | solution.py:548
  (83 shorter events, 17.5 us)
Async XLA Ops:
  0.7 2.4 %collective-permute-start = (f32[1,8]{1,0:T(1,128)S(1)}, f32[1,8]{1,0:T(1,128)S(1)}, u32[]{:S(2)}, u32[]{:S(2)}) collective-permute-start(f32[1,8]{1,0:T(1,128)S(1)} %bitcast.8), channel_id=1, source_target_pairs={{0,1},{1,0},{2,3},{3,2},{4,5},{5,4},{6,7},{7,6},{8,9},{9,8},{10,11... | collective-permute-start | bytes 104 | tf_op jit(solution)/shard_map/ppermute | solution.py:580
  5.8 1.7 %collective-permute-start.1 = (bf16[4,128,256]{2,1,0:T(8,128)(2,1)S(1)}, bf16[4,128,256]{2,1,0:T(8,128)(2,1)S(1)}, u32[]{:S(2)}, u32[]{:S(2)}) collective-permute-start(bf16[4,128,256]{2,1,0:T(8,128)(2,1)S(1)} %get-tuple-element.89), channel_id=1, source_target_pairs={{0,1},{1,0},{2,3},{3,2},{4,5},{5,4},{6,7},{7,6},{8,9},{9,8},{10,11... | collective-permute-start | bytes 786440 | tf_op jit(solution)/shard_map/ppermute | solution.py:580
  7.7 2.9 %collective-permute-start.3 = (f32[8,128]{1,0:T(8,128)S(1)}, f32[8,128]{1,0:T(8,128)S(1)}, u32[]{:S(2)}, u32[]{:S(2)}) collective-permute-start(f32[8,128]{1,0:T(8,128)S(1)} %get-tuple-element.90), channel_id=1, source_target_pairs={{0,1},{1,0},{2,3},{3,2},{4,5},{5,4},{6,7},{7,6},{8,9},{9,8},{10,11... | collective-permute-start | bytes 12296 | tf_op jit(solution)/shard_map/ppermute | solution.py:580
  8.1 5.4 %collective-permute-start.2 = (f32[8,128]{1,0:T(8,128)S(1)}, f32[8,128]{1,0:T(8,128)S(1)}, u32[]{:S(2)}, u32[]{:S(2)}) collective-permute-start(f32[8,128]{1,0:T(8,128)S(1)} %get-tuple-element.90), channel_id=1, source_target_pairs={{0,2},{1,3},{2,0},{3,1},{4,6},{5,7},{6,4},{7,5},{8,10},{9,11},{10,... | collective-permute-start | bytes 12296 | tf_op jit(solution)/shard_map/ppermute | solution.py:580
  10.5 7.5 %collective-permute-start.6 = (bf16[4,128,256]{2,1,0:T(8,128)(2,1)S(1)}, bf16[4,128,256]{2,1,0:T(8,128)(2,1)S(1)}, u32[]{:S(2)}, u32[]{:S(2)}) collective-permute-start(bf16[4,128,256]{2,1,0:T(8,128)(2,1)S(1)} %get-tuple-element.97), channel_id=1, source_target_pairs={{0,2},{1,3},{2,0},{3,1},{4,6},{5,7},{6,4},{7,5},{8,10},{9,11},{10,... | collective-permute-start | bytes 786440 | tf_op jit(solution)/shard_map/ppermute | solution.py:580
  12.8 3.5 %copy-start.13 = (bf16[4,128,256]{2,1,0:T(8,128)(2,1)}, bf16[4,128,256]{2,1,0:T(8,128)(2,1)S(1)}, u32[]{:S(2)}) copy-start(bf16[4,128,256]{2,1,0:T(8,128)(2,1)S(1)} %get-tuple-element.91.rest_2_.own_ref.refs_1_) | copy-start | bytes 786436
  12.9 3.4 %collective-permute-start.5 = (bf16[4,128,256]{2,1,0:T(8,128)(2,1)S(1)}, bf16[4,128,256]{2,1,0:T(8,128)(2,1)S(1)}, u32[]{:S(2)}, u32[]{:S(2)}) collective-permute-start(bf16[4,128,256]{2,1,0:T(8,128)(2,1)S(1)} %get-tuple-element.96), channel_id=1, source_target_pairs={{0,1},{1,0},{2,3},{3,2},{4,5},{5,4},{6,7},{7,6},{8,9},{9,8},{10,11... | collective-permute-start | bytes 786440 | tf_op jit(solution)/shard_map/ppermute | solution.py:580
  16.2 1.6 %collective-permute-start.4 = (bf16[4,128,256]{2,1,0:T(8,128)(2,1)S(1)}, bf16[4,128,256]{2,1,0:T(8,128)(2,1)S(1)}, u32[]{:S(2)}, u32[]{:S(2)}) collective-permute-start(bf16[4,128,256]{2,1,0:T(8,128)(2,1)S(1)} %get-tuple-element.95), channel_id=1, source_target_pairs={{0,1},{1,0},{2,3},{3,2},{4,5},{5,4},{6,7},{7,6},{8,9},{9,8},{10,11... | collective-permute-start | bytes 786440 | tf_op jit(solution)/shard_map/ppermute | solution.py:580
  18.3 3.1 %collective-permute-start.7 = (f32[8,128]{1,0:T(8,128)S(1)}, f32[8,128]{1,0:T(8,128)S(1)}, u32[]{:S(2)}, u32[]{:S(2)}) collective-permute-start(f32[8,128]{1,0:T(8,128)S(1)} %get-tuple-element.98), channel_id=1, source_target_pairs={{0,1},{1,0},{2,3},{3,2},{4,5},{5,4},{6,7},{7,6},{8,9},{9,8},{10,11... | collective-permute-start | bytes 12296 | tf_op jit(solution)/shard_map/ppermute | solution.py:580
  19.5 7.9 %collective-permute-start.9 = (bf16[4,128,256]{2,1,0:T(8,128)(2,1)S(1)}, bf16[4,128,256]{2,1,0:T(8,128)(2,1)S(1)}, u32[]{:S(2)}, u32[]{:S(2)}) collective-permute-start(bf16[4,128,256]{2,1,0:T(8,128)(2,1)S(1)} %compose.8.rest_0_), channel_id=1, source_target_pairs={{0,2},{1,3},{2,0},{3,1},{4,6},{5,7},{6,4},{7,5},{8,10},{9,11},{10,... | collective-permute-start | bytes 786440 | tf_op jit(solution)/shard_map/ppermute | solution.py:580
  20.2 4.5 %copy-start.2 = (bf16[128,4096]{1,0:T(8,128)(2,1)S(1)}, bf16[128,4096]{1,0:T(8,128)(2,1)}, u32[]{:S(2)}) copy-start(bf16[128,4096]{1,0:T(8,128)(2,1)} %q_hbm.7) | copy-start | bytes 3145732
  20.2 7.5 %collective-permute-start.10 = (bf16[4,128,256]{2,1,0:T(8,128)(2,1)S(1)}, bf16[4,128,256]{2,1,0:T(8,128)(2,1)S(1)}, u32[]{:S(2)}, u32[]{:S(2)}) collective-permute-start(bf16[4,128,256]{2,1,0:T(8,128)(2,1)S(1)} %get-tuple-element.104), channel_id=1, source_target_pairs={{0,4},{4,0},{8,12},{12,8},{16,20},{20,16},{24,28},{28,24},{1,5},{5... | collective-permute-start | bytes 786440 | tf_op jit(solution)/shard_map/ppermute | solution.py:580
  23.7 2.2 %collective-permute-start.8 = (bf16[4,128,256]{2,1,0:T(8,128)(2,1)S(1)}, bf16[4,128,256]{2,1,0:T(8,128)(2,1)S(1)}, u32[]{:S(2)}, u32[]{:S(2)}) collective-permute-start(bf16[4,128,256]{2,1,0:T(8,128)(2,1)S(1)} %get-tuple-element.100), channel_id=1, source_target_pairs={{0,1},{1,0},{2,3},{3,2},{4,5},{5,4},{6,7},{7,6},{8,9},{9,8},{10,11... | collective-permute-start | bytes 786440 | tf_op jit(solution)/shard_map/ppermute | solution.py:580
  27.9 6.6 %collective-permute-start.11 = (bf16[4,128,256]{2,1,0:T(8,128)(2,1)S(1)}, bf16[4,128,256]{2,1,0:T(8,128)(2,1)S(1)}, u32[]{:S(2)}, u32[]{:S(2)}) collective-permute-start(bf16[4,128,256]{2,1,0:T(8,128)(2,1)S(1)} %compose.13.refs_0_), channel_id=1, source_target_pairs={{0,8},{4,12},{8,0},{12,4},{16,24},{20,28},{24,16},{28,20},{1,9},{5... | collective-permute-start | bytes 786440 | tf_op jit(solution)/shard_map/ppermute | solution.py:580
  34.8 6.6 %collective-permute-start.12 = (bf16[4,128,128]{2,1,0:T(8,128)(2,1)S(1)}, bf16[4,128,128]{2,1,0:T(8,128)(2,1)S(1)}, u32[]{:S(2)}, u32[]{:S(2)}) collective-permute-start(bf16[4,128,128]{2,1,0:T(8,128)(2,1)S(1)} %get-tuple-element.114), channel_id=1, source_target_pairs={{0,16},{4,20},{8,24},{12,28},{16,0},{20,4},{24,8},{28,12},{1,17},{... | collective-permute-start | bytes 393224 | tf_op jit(solution)/shard_map/ppermute | solution.py:580
  41.7 4.4 %collective-permute-start.14 = (f32[8,128]{1,0:T(8,128)S(1)}, f32[8,128]{1,0:T(8,128)S(1)}, u32[]{:S(2)}, u32[]{:S(2)}) collective-permute-start(f32[8,128]{1,0:T(8,128)S(1)} %get-tuple-element.118), channel_id=1, source_target_pairs={{0,1},{1,0},{2,3},{3,2},{4,5},{5,4},{6,7},{7,6},{8,9},{9,8},{10,11... | collective-permute-start | bytes 12296 | tf_op jit(solution)/shard_map/ppermute | solution.py:580
  44.8 5.1 %collective-permute-start.13 = (bf16[4,128,128]{2,1,0:T(8,128)(2,1)S(1)}, bf16[4,128,128]{2,1,0:T(8,128)(2,1)S(1)}, u32[]{:S(2)}, u32[]{:S(2)}) collective-permute-start(bf16[4,128,128]{2,1,0:T(8,128)(2,1)S(1)} %get-tuple-element.116), channel_id=1, source_target_pairs={{0,4},{4,0},{8,12},{12,8},{16,20},{20,16},{24,28},{28,24},{1,5},{5... | collective-permute-start | bytes 393224 | tf_op jit(solution)/shard_map/ppermute | solution.py:580
  46.4 2.4 %collective-permute-start.15 = (bf16[4,128,128]{2,1,0:T(8,128)(2,1)S(1)}, bf16[4,128,128]{2,1,0:T(8,128)(2,1)S(1)}, u32[]{:S(2)}, u32[]{:S(2)}) collective-permute-start(bf16[4,128,128]{2,1,0:T(8,128)(2,1)S(1)} %get-tuple-element.119), channel_id=1, source_target_pairs={{0,1},{1,0},{2,3},{3,2},{4,5},{5,4},{6,7},{7,6},{8,9},{9,8},{10,11... | collective-permute-start | bytes 393224 | tf_op jit(solution)/shard_map/ppermute | solution.py:580
  46.8 5.7 %collective-permute-start.17 = (bf16[4,128,128]{2,1,0:T(8,128)(2,1)S(1)}, bf16[4,128,128]{2,1,0:T(8,128)(2,1)S(1)}, u32[]{:S(2)}, u32[]{:S(2)}) collective-permute-start(bf16[4,128,128]{2,1,0:T(8,128)(2,1)S(1)} %get-tuple-element.125), channel_id=1, source_target_pairs={{0,2},{1,3},{2,0},{3,1},{4,6},{5,7},{6,4},{7,5},{8,10},{9,11},{10,... | collective-permute-start | bytes 393224 | tf_op jit(solution)/shard_map/ppermute | solution.py:580
  50.3 2.3 %collective-permute-start.18 = (f32[8,128]{1,0:T(8,128)S(1)}, f32[8,128]{1,0:T(8,128)S(1)}, u32[]{:S(2)}, u32[]{:S(2)}) collective-permute-start(f32[8,128]{1,0:T(8,128)S(1)} %get-tuple-element.127), channel_id=1, source_target_pairs={{0,1},{1,0},{2,3},{3,2},{4,5},{5,4},{6,7},{7,6},{8,9},{9,8},{10,11... | collective-permute-start | bytes 12296 | tf_op jit(solution)/shard_map/ppermute | solution.py:580
  51.2 5.6 %collective-permute-start.16 = (bf16[4,128,128]{2,1,0:T(8,128)(2,1)S(1)}, bf16[4,128,128]{2,1,0:T(8,128)(2,1)S(1)}, u32[]{:S(2)}, u32[]{:S(2)}) collective-permute-start(bf16[4,128,128]{2,1,0:T(8,128)(2,1)S(1)} %get-tuple-element.124), channel_id=1, source_target_pairs={{0,2},{1,3},{2,0},{3,1},{4,6},{5,7},{6,4},{7,5},{8,10},{9,11},{10,... | collective-permute-start | bytes 393224 | tf_op jit(solution)/shard_map/ppermute | solution.py:580
  52.2 2.7 %collective-permute-start.20 = (bf16[4,128,128]{2,1,0:T(8,128)(2,1)S(1)}, bf16[4,128,128]{2,1,0:T(8,128)(2,1)S(1)}, u32[]{:S(2)}, u32[]{:S(2)}) collective-permute-start(bf16[4,128,128]{2,1,0:T(8,128)(2,1)S(1)} %get-tuple-element.129), channel_id=1, source_target_pairs={{0,1},{1,0},{2,3},{3,2},{4,5},{5,4},{6,7},{7,6},{8,9},{9,8},{10,11... | collective-permute-start | bytes 393224 | tf_op jit(solution)/shard_map/ppermute | solution.py:580
  52.8 3.1 %collective-permute-start.19 = (bf16[4,128,128]{2,1,0:T(8,128)(2,1)S(1)}, bf16[4,128,128]{2,1,0:T(8,128)(2,1)S(1)}, u32[]{:S(2)}, u32[]{:S(2)}) collective-permute-start(bf16[4,128,128]{2,1,0:T(8,128)(2,1)S(1)} %get-tuple-element.128), channel_id=1, source_target_pairs={{0,1},{1,0},{2,3},{3,2},{4,5},{5,4},{6,7},{7,6},{8,9},{9,8},{10,11... | collective-permute-start | bytes 393224 | tf_op jit(solution)/shard_map/ppermute | solution.py:580
  57.0 1.4 %collective-permute-start.21 = (bf16[4,128,128]{2,1,0:T(8,128)(2,1)S(1)}, bf16[4,128,128]{2,1,0:T(8,128)(2,1)S(1)}, u32[]{:S(2)}, u32[]{:S(2)}) collective-permute-start(bf16[4,128,128]{2,1,0:T(8,128)(2,1)S(1)} %get-tuple-element.143), channel_id=1, source_target_pairs={{0,1},{1,0},{2,3},{3,2},{4,5},{5,4},{6,7},{7,6},{8,9},{9,8},{10,11... | collective-permute-start | bytes 393224 | tf_op jit(solution)/shard_map/ppermute | solution.py:580
  (13 other events, 21.9 us)

commit v4 on v3

--- a/solution.py
+++ b/solution.py
@@ -79,7 +79,9 @@
         decay.append(decay_ref[rows, :] + bias)
         beta.append(beta_ref[rows, :])
     z = jnp.concatenate(decay, axis=0)
-    beta = 1.0 / (1.0 + jnp.exp(-jnp.concatenate(beta, axis=0)))
+    logit = jnp.concatenate(beta, axis=0)
+    beta = 1.0 / (1.0 + jnp.exp(-logit))
+    log_beta = jnp.minimum(logit, 0.0) - jnp.log1p(jnp.exp(-jnp.abs(logit)))
     log_decay = -(jnp.maximum(z, 0.0) + jnp.log1p(jnp.exp(-jnp.abs(z))))
     upper = jnp.where(row <= column, 1.0, 0.0)
     cum = jnp.dot(log_decay, upper, precision=EXACT, preferred_element_type=F32)
@@ -93,9 +95,9 @@
         sides = [slice(part * width + side * half, part * width + (side + 1) * half) for side in range(2)]
         for turn in range(2):
             same, other = sides[turn], sides[1 - turn]
-            for table in (cum, beta, beta * gamma, gamma):
+            for table in (cum, cum + log_beta, gamma):
                 tall.append(jnp.where(swapped, table[other], table[same]))
-            for place, table in enumerate((cum, back, whole)):
+            for place, table in enumerate((cum, back, whole, beta, beta * gamma)):
                 row_ref[part, turn, place * half : (place + 1) * half, :] = jnp.where(
                     swapped, table[other], table[same]
                 )
@@ -112,8 +114,8 @@
     return pl.pallas_call(
         functools.partial(gates_kernel, parts, bias_rows, width),
         out_shape=(
-            jax.ShapeDtypeStruct((tokens, 4 * count * width), F32),
-            jax.ShapeDtypeStruct((count, 2, 3 * half, tokens), F32),
+            jax.ShapeDtypeStruct((tokens, 3 * count * width), F32),
+            jax.ShapeDtypeStruct((count, 2, 5 * half, tokens), F32),
         ),
         in_specs=[whole_vmem()] * len(arrays),
         out_specs=(whole_vmem(),) * 2,
@@ -207,11 +209,11 @@
     row, column = masks(tokens)
     apart = jnp.bitwise_xor(row, column)
     eye = jnp.where(row == column, 1.0, 0.0)
-    strict = row > column
     lane_block = lax.shift_right_logical(column[:BASE], BASE.bit_length() - 1)
     inside = jnp.bitwise_and(column[:BASE], BASE - 1)
     small_eye = jnp.where(row[:BASE] == inside, 1.0, 0.0)
-    gap = gap_ref[...]
+    first_lane = column[:BASE] - inside
+    gap = jnp.where(row > column, gap_ref[...], MASKED)
     every = range(len(units) * half)
 
     def unit_of(i):
@@ -219,33 +221,41 @@
 
     def tall_of(table, i):
         at, turn, j = unit_of(i)
-        at = ((2 * at + turn) * 4 + table) * half + j
+        at = ((2 * at + turn) * 3 + table) * half + j
         return col_ref[:, at : at + 1]
 
     def wide_of(table, i):
         at, turn, j = unit_of(i)
         return row_ref[at, turn, table * half + j : table * half + j + 1, :]
 
-    lower, inverse = [], []
+    lower, packed = [], []
     for i in every:
         at, turn, j = unit_of(i)
-        decay = jnp.exp(tall_of(0, i) - wide_of(0, i) + gap)
-        gram = dot(normed_ref[at, turn, j], turned_ref[at, turn, j])
-        low = jnp.where(strict, tall_of(1, i) * decay * gram, 0.0)
-        packed = jnp.zeros((BASE, tokens), F32)
+        decay = jnp.exp(tall_of(1, i) - wide_of(0, i) + gap)
+        low = decay * dot(normed_ref[at, turn, j], turned_ref[at, turn, j])
+        blocks = jnp.zeros((BASE, tokens), F32)
         for top in range(0, tokens, BASE):
-            packed = jnp.where(lane_block == top // BASE, low[top : top + BASE], packed)
-        solution_rows = small_eye
-        for k in range(BASE - 1):
-            factor = jnp.take_along_axis(packed, column[:BASE] - inside + k, axis=1, mode="promise_in_bounds")
-            solution_rows = solution_rows - factor * solution_rows[k : k + 1]
+            blocks = jnp.where(lane_block == top // BASE, low[top : top + BASE], blocks)
+        packed.append(blocks)
+        lower.append(low.astype(BF16))
+    rows = [[small_eye[top : top + 8] for top in range(0, BASE, 8)] for _ in every]
+    for k in range(BASE - 1):
+        for i in every:
+            pivot = rows[i][k // 8][k % 8 : k % 8 + 1]
+            for group in range((k + 1) // 8, BASE // 8):
+                block_rows = slice(group * 8, group * 8 + 8)
+                factor = jnp.take_along_axis(
+                    packed[i][block_rows], first_lane[block_rows] + k, axis=1, mode="promise_in_bounds"
+                )
+                rows[i][group] = rows[i][group] - factor * pivot
+    inverse = []
+    for i in every:
+        joint = jnp.concatenate(rows[i], axis=0)
         inverse.append(
             jnp.concatenate(
-                [jnp.where(lane_block == at_block, solution_rows, 0.0) for at_block in range(tokens // BASE)],
-                axis=0,
+                [jnp.where(lane_block == at_block, joint, 0.0) for at_block in range(tokens // BASE)], axis=0
             )
         )
-        lower.append(low.astype(BF16))
     nothing = jnp.zeros((tokens, tokens), BF16)
     block = BASE
     while block < tokens:
@@ -273,10 +283,9 @@
     for i in every:
         at, turn, j = unit_of(i)
         lanes = slice(j * size, (j + 1) * size)
-        keys = tall_of(2, i) * normed_ref[at, turn, j].astype(F32)
-        values = tall_of(1, i) * v_ref[at, turn, :, lanes].astype(F32)
-        right = jnp.concatenate([keys.astype(BF16), values.astype(BF16)], axis=1)
-        solved.append(dot(inverse[i].astype(BF16), right).astype(BF16))
+        keys = dot((inverse[i] * wide_of(4, i)).astype(BF16), normed_ref[at, turn, j])
+        values = dot((inverse[i] * wide_of(3, i)).astype(BF16), v_ref[at, turn, :, lanes])
+        solved.append(jnp.concatenate([keys.astype(BF16), values.astype(BF16)], axis=1))
     for i in every:
         at, turn, j = unit_of(i)
         ab_ref, solved_ref = outs[2 * (i // half) : 2 * (i // half) + 2]
@@ -303,9 +312,10 @@
     return [(outs[2 * i], outs[2 * i + 1]) for i in range(len(units))]
 
 
-def outlook_kernel(at, part, q_hbm, turned_ref, gap_ref, col_ref, row_ref, *refs):
+def outlook_kernel(at, part, q_hbm, turned_ref, gap_ref, col_ref, row_ref, gain_ref, *refs):
     solved_refs = refs[:2]
-    qo_refs = refs[-4:-2]
+    qo_refs = refs[-5:-3]
+    refs[-3][...] = gain_ref[...]
     q_ref, sems = refs[-2:]
     half, tokens = solved_refs[0].shape[:2]
     size = solved_refs[0].shape[2] // 2
@@ -320,7 +330,7 @@
     every = [(turn, j) for turn in range(2) for j in range(half)]
 
     def tall_of(table, turn, j):
-        place = ((2 * at + turn) * 4 + table) * half + j
+        place = ((2 * at + turn) * 3 + table) * half + j
         return col_ref[:, place : place + 1]
 
     decay = {}
@@ -334,19 +344,19 @@
         mix[turn, j] = (decay[turn, j] * gram).astype(BF16)
     for turn, j in every:
         both = dot(mix[turn, j], solved_refs[turn][j])
-        through = tall_of(3, turn, j) * q_ref[turn, :, j * size : (j + 1) * size].astype(F32)
+        through = tall_of(2, turn, j) * q_ref[turn, :, j * size : (j + 1) * size].astype(F32)
         qo_refs[turn][j, :, :size] = (through - both[:, :size]).astype(BF16)
         qo_refs[turn][j, :, size:] = both[:, size:].astype(BF16)
 
 
-def outlook(at, part, queries, turned, gap, tables, solved, *after):
+def outlook(at, part, queries, turned, gap, tables, gain, solved, *after):
     half, tokens, wide = solved[0].shape
-    arrays = (queries, turned, gap) + tuple(tables) + tuple(solved) + after
+    arrays = (queries, turned, gap) + tuple(tables) + (gain,) + tuple(solved) + after
     return pl.pallas_call(
         functools.partial(outlook_kernel, at, part),
-        out_shape=(jax.ShapeDtypeStruct(solved[0].shape, BF16),) * 2,
+        out_shape=(jax.ShapeDtypeStruct(solved[0].shape, BF16),) * 2 + (jax.ShapeDtypeStruct(gain.shape, F32),),
         in_specs=[in_hbm()] + [whole_vmem()] * (len(arrays) - 1),
-        out_specs=(whole_vmem(),) * 2,
+        out_specs=(whole_vmem(),) * 3,
         scratch_shapes=[pltpu.VMEM((2, tokens, half * wide // 2), BF16), pltpu.SemaphoreType.DMA((2,))],
         compiler_params=params(),
         cost_estimate=cost(),
@@ -489,20 +499,20 @@
     )(*arrays)
 
 
-def finish_kernel(unit, earlier_unit, is_last, gain_ref, state_ref, qo_ref, gate_ref, *rest):
-    sems = rest[-1]
-    strip_ref = rest[-2]
-    out_hbm = rest[-3]
+def finish_kernel(unit, stored, is_last, gain_ref, state_ref, qo_ref, gate_ref, *rest):
     half, size = state_ref.shape[0], state_ref.shape[-1]
     span = half * size
+    strip_ref = rest[-2] if is_last or stored else rest[-1]
 
     def start_of(part, turn):
         return (2 * chunk_of(part) + jnp.bitwise_xor(turn, parity())) * span
 
     stores = []
-    if earlier_unit is not None:
-        there = pl.ds(pl.multiple_of(start_of(*earlier_unit), span), span)
-        stores.append(pltpu.make_async_copy(rest[0], out_hbm.at[:, there], sems.at[half]))
+    if stored or is_last:
+        out_hbm, sems = rest[-3], rest[-1]
+    for number, earlier in enumerate(stored):
+        there = pl.ds(pl.multiple_of(start_of(*earlier), span), span)
+        stores.append(pltpu.make_async_copy(rest[number], out_hbm.at[:, there], sems.at[half + number]))
         stores[-1].start()
     cores = []
     for j in range(half):
@@ -522,41 +532,40 @@
         store.wait()
 
 
-def finish(unit, is_last, state, qo, gate, gain, previous):
+def finish(unit, is_last, state, qo, gate, gain, result, stored, *after):
     half, tokens, size = state.shape[0], gate.shape[0], state.shape[-1]
-    specs = [whole_vmem()] * 4
-    arrays = [gain, state, qo, gate]
+    arrays = [gain, state, qo, gate] + [strip for strip, _ in stored] + list(after)
+    specs = [whole_vmem()] * len(arrays)
     aliases = {}
-    earlier_unit = None
-    if previous is not None:
-        result, strip, earlier_unit = previous
-        specs += [whole_vmem()]
-        arrays += [strip]
-        if result is not None:
-            specs += [in_hbm()]
-            arrays += [result]
-            aliases = {len(arrays) - 1: 0}
-    strip_shape = (tokens, half * size)
-    outs = (jax.ShapeDtypeStruct(gate.shape, BF16),)
-    out_specs = (in_hbm(),)
-    scratch = [pltpu.SemaphoreType.DMA((1 + half,))]
+    if result is not None:
+        aliases = {len(arrays): 0}
+        arrays.append(result)
+        specs.append(in_hbm())
+    strip = jax.ShapeDtypeStruct((tokens, half * size), BF16)
+    outs, out_specs, scratch = [], [], []
+    if stored or is_last:
+        outs.append(jax.ShapeDtypeStruct(gate.shape, BF16))
+        out_specs.append(in_hbm())
+        scratch.append(pltpu.SemaphoreType.DMA((half + len(stored),)))
     if is_last:
-        scratch = [pltpu.VMEM(strip_shape, BF16)] + scratch
+        scratch = [pltpu.VMEM(strip.shape, BF16)] + scratch
     else:
-        outs += (jax.ShapeDtypeStruct(strip_shape, BF16),)
-        out_specs += (whole_vmem(),)
+        outs.append(strip)
+        out_specs.append(whole_vmem())
     done = pl.pallas_call(
-        functools.partial(finish_kernel, unit, earlier_unit, is_last),
-        out_shape=outs,
+        functools.partial(finish_kernel, unit, [earlier for _, earlier in stored], is_last),
+        out_shape=tuple(outs),
         in_specs=specs,
-        out_specs=out_specs,
+        out_specs=tuple(out_specs),
         scratch_shapes=scratch,
         input_output_aliases=aliases,
         compiler_params=params(),
         cost_estimate=cost(),
         name="finish",
     )(*arrays)
-    return done[0] if is_last else (done[0], done[1], unit)
+    if is_last:
+        return done[0], None
+    return (done[0], done[1]) if stored else (result, done[0])
 
 
 def body(
@@ -613,6 +622,7 @@
     far, got, near, chip = {}, {}, {}, {}
     first_done = ab[far_parts[-1], 1]
     fetched_near = fetch(near_parts, half, size, None, *inputs, first_done)
+    early = swap(flags, "head", 1)
     far[1], token = fold(
         1 << under, 1, under, *far_biases, fetched_near[0], with_token=True, carried=len(far_biases)
     )
@@ -625,17 +635,18 @@
     far[0] = fold(1 << under, 0, under)
     got[0] = swap(far[0], "head", 1 << under)
     near[1] = fold(0, 1, under, far[0])
-    chip[1], token = compose(head_bit[under], near[1], got[1], with_token=True)
+    chip[1] = compose(head_bit[under], near[1], got[1])
     across = swap(chip[1], "context", 1)
-    work(near_parts, 0, fetched_near, gap, near_tables, swap(token, "head", 1))
+    work(near_parts, 0, fetched_near, gap, near_tables, chip[1], early)
 
     def look(part, *after):
         names, data, known = (
             (far_parts, fetched, tables) if part in far_parts else (near_parts, fetched_near, near_tables)
         )
-        qo[part, 0], qo[part, 1] = outlook(
-            names.index(part), part, queries, data[1], gap, known, (solved[part, 0], solved[part, 1]), *after
+        qo[part, 0], qo[part, 1], gain = outlook(
+            names.index(part), part, queries, data[1], gap, known, norm_gain[None, :], (solved[part, 0], solved[part, 1]), *after
         )
+        return gain
 
     every_part = far_parts + near_parts
     look(every_part[0], ab[near_parts[-1], 0])
@@ -647,15 +658,15 @@
     x_pair = (chip[0], across)
     total = compose(context_bit[0], *x_pair)
     before = None
+    held = [array for level in levels[:under] for pair in level.values() for array in pair]
     for part in every_part[1:]:
-        look(part, chip[0])
+        gain = look(part, chip[0], *held)
     for bit in range(1, context_bits - 1):
         other = swap(total, "context", 1 << bit)
-        done_by = tuple(qo[part, 0] for part in every_part[1:]) if bit == 1 else ()
+        done_by = tuple(qo[part, turn] for part in every_part for turn in (0, 1)) + tuple(held) if bit == 1 else ()
         total, before = doubling(context_bit[bit], bit == context_bits - 2, total, other, before, *done_by)
     other = swap(total, "context", 1 << (context_bits - 1))
 
-    gain = norm_gain[None, :]
     states = {}
     result = None
     descending = list(reversed(range(head_bits)))
@@ -675,19 +686,26 @@
     ready = [(0, 0)]
     total_units = 2 * head_count
 
+    strips = []
+
     def write(part, turn, result):
-        done.append((part, turn))
-        return finish(
+        number = len(strips) + 1
+        stored = strips if number == total_units - 1 else strips[-1:] if number == total_units else []
+        chained = [strips[-1][0]] if strips and not stored else []
+        result, strip = finish(
             (part, turn),
-            len(done) == total_units,
+            number == total_units,
             states[part, turn],
             qo[part, turn],
             gate_input,
             gain,
             result,
+            list(stored),
+            *chained,
         )
-
-    done = []
+        strips.append((strip, (part, turn)))
+        return result
+
     while arriving or ready:
         for part, turn in ready:
             result = write(part, turn, result)
@@ -707,12 +725,12 @@
                 None,
                 (state,),
                 [levels[bit][part, turn] for bit in down],
-                result[1],
+                strips[-1][0],
                 *tokens,
                 with_token=more,
             )
             states[part, turn] = outs[below]
-            result = (result[0], outs[below + 1], result[2])
+            strips[-1] = (outs[below + 1], strips[-1][1])
             ready.append((part, turn))
             for level, bit in enumerate(down):
                 arriving.append((part | 1 << bit, turn, bit, swap(outs[level], "head", 1 << bit)))

time: 60 us -> 57.4 us (0.957)
  Pallas kernels: 26.5 us -> 23.3 us
  starting transfers between devices: 20.7 us -> 23.2 us
  waiting for transfers between devices: 9.98 us -> 8.91 us
    pallas_call x8, Pallas kernels: 6.87 us -> 4.03 us  [finish(): pl.pallas_call(functools.partial(finish_kernel, unit, [earlier for _, ear...]
    ppermute x22, starting transfers between devices: 20.7 us -> 23.2 us  [swap(): return lax.ppermute(array, axis, [(i, i ^ distance) for i in range(count)])]
    pallas_call x4, Pallas kernels: 9.09 us -> 7.68 us  [local(): pl.pallas_call(functools.partial(local_kernel, units), out_shape=(result,...]
    ppermute x22, waiting for transfers between devices: 9.98 us -> 8.91 us  [swap(): return lax.ppermute(array, axis, [(i, i ^ distance) for i in range(count)])]
    pallas_call x4, Pallas kernels: 3.11 us -> 4.11 us  [outlook(): pl.pallas_call(functools.partial(outlook_kernel, at, part), out_shape=(ja...]
    unnamed x30 -> x18, local copies, waits for them, and re-layouts: 1.87 us -> 1.34 us
  transfers between devices with their start and end apart: 22 -> 22, of which waited for: 8 -> 7; matrix products, arithmetic and copies ran while one was open for 0% -> 0% of each run, Pallas kernels for 36% -> 33%
where the time goes in v4:
time: 57.4 us; the launch traced here: 57.2 us
  Pallas kernels  23.3 us (41%)
  starting transfers between devices  23.2 us (40%)
  waiting for transfers between devices  8.91 us (16%)
  local copies, waits for them, and re-layouts  1.34 us (2%)
    ppermute x22, starting transfers between devices, swap(): return lax.ppermute(array, axis, [(i, i ^ distance) for i in range(count)])  23.2 us
    ppermute x22, waiting for transfers between devices, swap(): return lax.ppermute(array, axis, [(i, i ^ distance) for i in range(count)])  8.91 us
    pallas_call x4, Pallas kernels, local(): pl.pallas_call(functools.partial(local_kernel, units), out_shape=(result,...  7.68 us
    pallas_call x4, Pallas kernels, outlook(): pl.pallas_call(functools.partial(outlook_kernel, at, part), out_shape=(ja...  4.11 us
    pallas_call x8, Pallas kernels, finish(): pl.pallas_call(functools.partial(finish_kernel, unit, [earlier for _, ear...  4.03 us
    pallas_call x2, Pallas kernels, fetch(): pl.pallas_call(functools.partial(fetch_kernel, parts, half, doc_start is...  3.44 us
    pallas_call x7, Pallas kernels, compose(): pl.pallas_call(functools.partial(compose_kernel, bit, with_token, carried...  1.59 us
    pallas_call x5, Pallas kernels, descend(): pl.pallas_call(functools.partial(descend_kernel, bits, top, int(thread is...  1.47 us
  transfers between devices with their start and end apart: 22, of which 7 were waited for; matrix products, arithmetic and copies ran while one was open for 0% of the time, Pallas kernels for 33%

profile of v4, /device:TPU:1, one launch (start us, length us, event | category | flops | bytes accessed | tf_op | source)
XLA Modules:
  0.0 57.2 jit_solution(843536006387029330)
XLA Ops:
  0.7 2.4 %fetch.2 = (bf16[2,2,4,128,128]{4,3,2,1,0:T(8,128)(2,1)S(1)}, bf16[2,2,4,128,128]{4,3,2,1,0:T(8,128)(2,1)S(1)}, bf16[2,2,128,512]{3,2,1,0:T(8,128)(2,1)S(1)}, f32[128,128]{1,0:T(8,128)S(1)}, f32[3,8,128]{2,1,0:T(8,128)S(1)}) custom-call(s32[8]{0:T(128)S(1)} %copy-done.6, bf16[128,4096]{1,0:T(8,128)(2,1)} %refs_0_.3, bf16[128,4096]{1,0:T(8,128)(2,1)} %refs_1_.3), custom_call_target="tpu_custom_call" | custom-call | flops 10000000000 | bytes 100000000 | tf_op jit(solution)/shard_map/fetch/pallas_call | solution.py:192
  3.5 1.9 %local_tokens.4 = (bf16[4,128,256]{2,1,0:T(8,128)(2,1)S(1)}, bf16[4,128,256]{2,1,0:T(8,128)(2,1)S(1)}, bf16[4,128,256]{2,1,0:T(8,128)(2,1)S(1)}, bf16[4,128,256]{2,1,0:T(8,128)(2,1)S(1)}) custom-call(bf16[2,2,4,128,128]{4,3,2,1,0:T(8,128)(2,1)S(1)} %get-tuple-element.65.refs_0_, bf16[2,2,4,128,128]{4,3,2,1,0:T(8,128)(2,1)S(1)} %get-tuple-element.66.refs_1_.turned_ref, ...), custom_call_target="tpu_custom_call" | custom-call | flops 10000000000 | bytes 100000000 | tf_op jit(solution)/shard_map/local_tokens/pallas_call | solution.py:303
  6.0 1.1 %fetch.3 = (bf16[2,2,4,128,128]{4,3,2,1,0:T(8,128)(2,1)S(1)}, bf16[2,2,4,128,128]{4,3,2,1,0:T(8,128)(2,1)S(1)}, bf16[2,2,128,512]{3,2,1,0:T(8,128)(2,1)S(1)}) custom-call(bf16[128,4096]{1,0:T(8,128)(2,1)S(1)} %copy-done, bf16[128,4096]{1,0:T(8,128)(2,1)S(1)} %copy-done.1, bf16[4,128,256]{2,1,0:T(8,128)(2,1)S(1)} %get-tuple-element.72.refs_2_.own_ref.refs_3_.refs_10_.refs_1_), custom_call_target="tpu_custom_call" | custom-call | flops 10000000000 | bytes 100000000 | tf_op jit(solution)/shard_map/fetch/pallas_call | solution.py:192
  7.9 2.6 %collective-permute-start.2 = (f32[8,128]{1,0:T(8,128)S(1)}, f32[8,128]{1,0:T(8,128)S(1)}, u32[]{:S(2)}, u32[]{:S(2)}) collective-permute-start(f32[8,128]{1,0:T(8,128)S(1)} %get-tuple-element.76), channel_id=1, source_target_pairs={{0,2},{1,3},{2,0},{3,1},{4,6},{5,7},{6,4},{7,5},{8,10},{9,11},{10,... | collective-permute-start | bytes 12296 | tf_op jit(solution)/shard_map/ppermute | solution.py:589
  10.6 1.9 %local_tokens.5 = (bf16[4,128,256]{2,1,0:T(8,128)(2,1)S(1)}, bf16[4,128,256]{2,1,0:T(8,128)(2,1)S(1)}, bf16[4,128,256]{2,1,0:T(8,128)(2,1)S(1)}, bf16[4,128,256]{2,1,0:T(8,128)(2,1)S(1)}) custom-call(bf16[2,2,4,128,128]{4,3,2,1,0:T(8,128)(2,1)S(1)} %get-tuple-element.65.refs_0_, bf16[2,2,4,128,128]{4,3,2,1,0:T(8,128)(2,1)S(1)} %get-tuple-element.66.refs_1_.turned_ref, ...), custom_call_target="tpu_custom_call" | custom-call | flops 10000000000 | bytes 100000000 | tf_op jit(solution)/shard_map/local_tokens/pallas_call | solution.py:303
  13.4 1.9 %local_tokens.6 = (bf16[4,128,256]{2,1,0:T(8,128)(2,1)S(1)}, bf16[4,128,256]{2,1,0:T(8,128)(2,1)S(1)}, bf16[4,128,256]{2,1,0:T(8,128)(2,1)S(1)}, bf16[4,128,256]{2,1,0:T(8,128)(2,1)S(1)}) custom-call(bf16[2,2,4,128,128]{4,3,2,1,0:T(8,128)(2,1)S(1)} %get-tuple-element.75.rest_2_.refs_0_, ...), custom_call_target="tpu_custom_call" | custom-call | flops 10000000000 | bytes 100000000 | tf_op jit(solution)/shard_map/local_tokens/pallas_call | solution.py:303
  15.7 1.7 %collective-permute-start.9 = (bf16[4,128,256]{2,1,0:T(8,128)(2,1)S(1)}, bf16[4,128,256]{2,1,0:T(8,128)(2,1)S(1)}, u32[]{:S(2)}, u32[]{:S(2)}) collective-permute-start(bf16[4,128,256]{2,1,0:T(8,128)(2,1)S(1)} %compose.8.rest_0_), channel_id=1, source_target_pairs={{0,2},{1,3},{2,0},{3,1},{4,6},{5,7},{6,4},{7,5},{8,10},{9,11},{10,... | collective-permute-start | bytes 786440 | tf_op jit(solution)/shard_map/ppermute | solution.py:589
  18.2 1.3 %collective-permute-start.10 = (bf16[4,128,256]{2,1,0:T(8,128)(2,1)S(1)}, bf16[4,128,256]{2,1,0:T(8,128)(2,1)S(1)}, u32[]{:S(2)}, u32[]{:S(2)}) collective-permute-start(bf16[4,128,256]{2,1,0:T(8,128)(2,1)S(1)} %compose.10.refs_6_), channel_id=1, source_target_pairs={{0,4},{4,0},{8,12},{12,8},{16,20},{20,16},{24,28},{28,24},{1,5},{5... | collective-permute-start | bytes 786440 | tf_op jit(solution)/shard_map/ppermute | solution.py:589
  19.5 1.9 %local_tokens.7 = (bf16[4,128,256]{2,1,0:T(8,128)(2,1)S(1)}, bf16[4,128,256]{2,1,0:T(8,128)(2,1)S(1)}, bf16[4,128,256]{2,1,0:T(8,128)(2,1)S(1)}, bf16[4,128,256]{2,1,0:T(8,128)(2,1)S(1)}) custom-call(bf16[2,2,4,128,128]{4,3,2,1,0:T(8,128)(2,1)S(1)} %get-tuple-element.75.rest_2_.refs_0_, ...), custom_call_target="tpu_custom_call" | custom-call | flops 10000000000 | bytes 100000000 | tf_op jit(solution)/shard_map/local_tokens/pallas_call | solution.py:303
  21.4 1.6 %collective-permute-start.8 = (bf16[4,128,256]{2,1,0:T(8,128)(2,1)S(1)}, bf16[4,128,256]{2,1,0:T(8,128)(2,1)S(1)}, u32[]{:S(2)}, u32[]{:S(2)}) collective-permute-start(bf16[4,128,256]{2,1,0:T(8,128)(2,1)S(1)} %get-tuple-element.88), channel_id=1, source_target_pairs={{0,1},{1,0},{2,3},{3,2},{4,5},{5,4},{6,7},{7,6},{8,9},{9,8},{10,11... | collective-permute-start | bytes 786440 | tf_op jit(solution)/shard_map/ppermute | solution.py:589
  23.7 1.1 %outlook.4 = (bf16[4,128,256]{2,1,0:T(8,128)(2,1)S(1)}, bf16[4,128,256]{2,1,0:T(8,128)(2,1)S(1)}, f32[1,128]{1,0:T(1,128)}) custom-call(bf16[128,4096]{1,0:T(8,128)(2,1)S(1)} %copy-done.2, bf16[2,2,4,128,128]{4,3,2,1,0:T(8,128)(2,1)S(1)} %get-tuple-element.66.refs_1_.turned_ref, f32[128,128]{1,0:T(8,128)S(1)} %get-tuple-element.68.refs_3_.gap_ref, ...), custom_call_target="tpu_custom_call" | custom-call | flops 10000000000 | bytes 100000000 | tf_op jit(solution)/shard_map/outlook/pallas_call | solution.py:355
  25.5 1.4 %collective-permute-start.11 = (bf16[4,128,256]{2,1,0:T(8,128)(2,1)S(1)}, bf16[4,128,256]{2,1,0:T(8,128)(2,1)S(1)}, u32[]{:S(2)}, u32[]{:S(2)}) collective-permute-start(bf16[4,128,256]{2,1,0:T(8,128)(2,1)S(1)} %compose.13.refs_0_), channel_id=1, source_target_pairs={{0,8},{4,12},{8,0},{12,4},{16,24},{20,28},{24,16},{28,20},{1,9},{5... | collective-permute-start | bytes 786440 | tf_op jit(solution)/shard_map/ppermute | solution.py:589
  26.9 1.1 %outlook.6 = (bf16[4,128,256]{2,1,0:T(8,128)(2,1)S(1)}, bf16[4,128,256]{2,1,0:T(8,128)(2,1)S(1)}, f32[1,128]{1,0:T(1,128)}) custom-call(bf16[128,4096]{1,0:T(8,128)(2,1)S(1)} %copy-done.2, bf16[2,2,4,128,128]{4,3,2,1,0:T(8,128)(2,1)S(1)} %get-tuple-element.66.refs_1_.turned_ref, f32[128,128]{1,0:T(8,128)S(1)} %get-tuple-element.68.refs_3_.gap_ref, ...), custom_call_target="tpu_custom_call" | custom-call | flops 10000000000 | bytes 100000000 | tf_op jit(solution)/shard_map/outlook/pallas_call | solution.py:355
  28.7 1.3 %outlook.7 = (bf16[4,128,256]{2,1,0:T(8,128)(2,1)S(1)}, bf16[4,128,256]{2,1,0:T(8,128)(2,1)S(1)}, f32[1,128]{1,0:T(1,128)}) custom-call(bf16[128,4096]{1,0:T(8,128)(2,1)S(1)} %copy-done.2, bf16[2,2,4,128,128]{4,3,2,1,0:T(8,128)(2,1)S(1)} %get-tuple-element.73.refs_1_.turned_ref, f32[128,128]{1,0:T(8,128)S(1)} %get-tuple-element.68.refs_3_.gap_ref, ...), custom_call_target="tpu_custom_call" | custom-call | flops 10000000000 | bytes 100000000 | tf_op jit(solution)/shard_map/outlook/pallas_call | solution.py:355
  29.9 1.7 %collective-permute-done.11.refs_1_ = bf16[4,128,256]{2,1,0:T(8,128)(2,1)S(1)} collective-permute-done((bf16[4,128,256]{2,1,0:T(8,128)(2,1)S(1)}, bf16[4,128,256]{2,1,0:T(8,128)(2,1)S(1)}, u32[]{:S(2)}, u32[]{:S(2)}) %collective-permute-start.11) | collective-permute-done | bytes 262176 | tf_op jit(solution)/shard_map/ppermute | solution.py:589
  31.9 2.4 %collective-permute-start.12 = (bf16[4,128,128]{2,1,0:T(8,128)(2,1)S(1)}, bf16[4,128,128]{2,1,0:T(8,128)(2,1)S(1)}, u32[]{:S(2)}, u32[]{:S(2)}) collective-permute-start(bf16[4,128,128]{2,1,0:T(8,128)(2,1)S(1)} %get-tuple-element.104), channel_id=1, source_target_pairs={{0,16},{4,20},{8,24},{12,28},{16,0},{20,4},{24,8},{28,12},{1,17},{... | collective-permute-start | bytes 393224 | tf_op jit(solution)/shard_map/ppermute | solution.py:589
  34.2 3.8 %collective-permute-done.12.refs_0_ = bf16[4,128,128]{2,1,0:T(8,128)(2,1)S(1)} collective-permute-done((bf16[4,128,128]{2,1,0:T(8,128)(2,1)S(1)}, bf16[4,128,128]{2,1,0:T(8,128)(2,1)S(1)}, u32[]{:S(2)}, u32[]{:S(2)}) %collective-permute-start.12) | collective-permute-done | bytes 131104 | tf_op jit(solution)/shard_map/ppermute | solution.py:589
  38.4 3.9 %collective-permute-start.14 = (f32[8,128]{1,0:T(8,128)S(1)}, f32[8,128]{1,0:T(8,128)S(1)}, u32[]{:S(2)}, u32[]{:S(2)}) collective-permute-start(f32[8,128]{1,0:T(8,128)S(1)} %get-tuple-element.108), channel_id=1, source_target_pairs={{0,1},{1,0},{2,3},{3,2},{4,5},{5,4},{6,7},{7,6},{8,9},{9,8},{10,11... | collective-permute-start | bytes 12296 | tf_op jit(solution)/shard_map/ppermute | solution.py:589
  43.9 1.5 %collective-permute-start.17 = (bf16[4,128,128]{2,1,0:T(8,128)(2,1)S(1)}, bf16[4,128,128]{2,1,0:T(8,128)(2,1)S(1)}, u32[]{:S(2)}, u32[]{:S(2)}) collective-permute-start(bf16[4,128,128]{2,1,0:T(8,128)(2,1)S(1)} %get-tuple-element.112), channel_id=1, source_target_pairs={{0,2},{1,3},{2,0},{3,1},{4,6},{5,7},{6,4},{7,5},{8,10},{9,11},{10,... | collective-permute-start | bytes 393224 | tf_op jit(solution)/shard_map/ppermute | solution.py:589
  46.0 1.4 %collective-permute-done.13.refs_0_ = bf16[4,128,128]{2,1,0:T(8,128)(2,1)S(1)} collective-permute-done((bf16[4,128,128]{2,1,0:T(8,128)(2,1)S(1)}, bf16[4,128,128]{2,1,0:T(8,128)(2,1)S(1)}, u32[]{:S(2)}, u32[]{:S(2)}) %collective-permute-start.13) | collective-permute-done | bytes 131104 | tf_op jit(solution)/shard_map/ppermute | solution.py:589
  48.6 1.4 %collective-permute-start.16 = (bf16[4,128,128]{2,1,0:T(8,128)(2,1)S(1)}, bf16[4,128,128]{2,1,0:T(8,128)(2,1)S(1)}, u32[]{:S(2)}, u32[]{:S(2)}) collective-permute-start(bf16[4,128,128]{2,1,0:T(8,128)(2,1)S(1)} %get-tuple-element.111), channel_id=1, source_target_pairs={{0,2},{1,3},{2,0},{3,1},{4,6},{5,7},{6,4},{7,5},{8,10},{9,11},{10,... | collective-permute-start | bytes 393224 | tf_op jit(solution)/shard_map/ppermute | solution.py:589
  52.4 1.3 %collective-permute-done.16.refs_0_ = bf16[4,128,128]{2,1,0:T(8,128)(2,1)S(1)} collective-permute-done((bf16[4,128,128]{2,1,0:T(8,128)(2,1)S(1)}, bf16[4,128,128]{2,1,0:T(8,128)(2,1)S(1)}, u32[]{:S(2)}, u32[]{:S(2)}) %collective-permute-start.16) | collective-permute-done | bytes 131104 | tf_op jit(solution)/shard_map/ppermute | solution.py:589
  54.8 1.2 %finish.14 = (bf16[128,4096]{1,0:T(8,128)(2,1)}, bf16[128,512]{1,0:T(8,128)(2,1)S(1)}) custom-call(f32[1,128]{1,0:T(1,128)S(1)} %get-tuple-element.92.gain_ref, bf16[4,128,128]{2,1,0:T(8,128)(2,1)S(1)} %get-tuple-element.121.state_ref, bf16[4,128,256]{2,1,0:T(8,128)(2,1)S(1)} %get-tuple-element.97.refs_5_.qo_ref, bf16[128,4096]{1,0:T(8,128)(2,1)S(1)} %copy-done.3, ...), custom_call_target="tpu_custom_call" | custom-call | flops 10000000000 | bytes 100000000 | tf_op jit(solution)/shard_map/finish/pallas_call | solution.py:555
  56.0 1.0 %finish.15 = bf16[128,4096]{1,0:T(8,128)(2,1)} custom-call(f32[1,128]{1,0:T(1,128)S(1)} %get-tuple-element.92.gain_ref, bf16[4,128,128]{2,1,0:T(8,128)(2,1)S(1)} %collective-permute-done.21.state_ref, bf16[4,128,256]{2,1,0:T(8,128)(2,1)S(1)} %get-tuple-element.93.refs_3_.qo_ref, bf16[128,4096]{1,0:T(8,128)(2,1)S(1)} %copy-done.3, ...), custom_call_target="tpu_custom_call", output_to_operand_aliasing={{}: (5, {})} | custom-call | flops 10000000000 | bytes 100000000 | tf_op jit(solution)/shard_map/finish/pallas_call | solution.py:555
  (71 shorter events, 14.1 us)
Async XLA Ops:
  0.7 2.4 %collective-permute-start = (f32[1,8]{1,0:T(1,128)S(1)}, f32[1,8]{1,0:T(1,128)S(1)}, u32[]{:S(2)}, u32[]{:S(2)}) collective-permute-start(f32[1,8]{1,0:T(1,128)S(1)} %bitcast.8), channel_id=1, source_target_pairs={{0,1},{1,0},{2,3},{3,2},{4,5},{5,4},{6,7},{7,6},{8,9},{9,8},{10,11... | collective-permute-start | bytes 104 | tf_op jit(solution)/shard_map/ppermute | solution.py:589
  3.5 2.5 %copy-start = (bf16[128,4096]{1,0:T(8,128)(2,1)S(1)}, bf16[128,4096]{1,0:T(8,128)(2,1)}, u32[]{:S(2)}) copy-start(bf16[128,4096]{1,0:T(8,128)(2,1)} %refs_0_.3) | copy-start | bytes 3145732
  5.4 1.7 %collective-permute-start.1 = (bf16[4,128,256]{2,1,0:T(8,128)(2,1)S(1)}, bf16[4,128,256]{2,1,0:T(8,128)(2,1)S(1)}, u32[]{:S(2)}, u32[]{:S(2)}) collective-permute-start(bf16[4,128,256]{2,1,0:T(8,128)(2,1)S(1)} %get-tuple-element.74), channel_id=1, source_target_pairs={{0,1},{1,0},{2,3},{3,2},{4,5},{5,4},{6,7},{7,6},{8,9},{9,8},{10,11... | collective-permute-start | bytes 786440 | tf_op jit(solution)/shard_map/ppermute | solution.py:589
  7.4 3.2 %collective-permute-start.3 = (f32[8,128]{1,0:T(8,128)S(1)}, f32[8,128]{1,0:T(8,128)S(1)}, u32[]{:S(2)}, u32[]{:S(2)}) collective-permute-start(f32[8,128]{1,0:T(8,128)S(1)} %get-tuple-element.76), channel_id=1, source_target_pairs={{0,1},{1,0},{2,3},{3,2},{4,5},{5,4},{6,7},{7,6},{8,9},{9,8},{10,11... | collective-permute-start | bytes 12296 | tf_op jit(solution)/shard_map/ppermute | solution.py:589
  7.8 11.7 %collective-permute-start.7 = (f32[3,8,128]{2,1,0:T(8,128)S(1)}, f32[3,8,128]{2,1,0:T(8,128)S(1)}, u32[]{:S(2)}, u32[]{:S(2)}) collective-permute-start(f32[3,8,128]{2,1,0:T(8,128)S(1)} %get-tuple-element.69.flag_ref), channel_id=1, source_target_pairs={{0,1},{1,0},{2,3},{3,2},{4,5},{5,4},{6,7},{7,6},{8,9},{9,8},{10,11... | collective-permute-start | bytes 36872 | tf_op jit(solution)/shard_map/ppermute | solution.py:589
  7.9 5.1 %collective-permute-start.2 = (f32[8,128]{1,0:T(8,128)S(1)}, f32[8,128]{1,0:T(8,128)S(1)}, u32[]{:S(2)}, u32[]{:S(2)}) collective-permute-start(f32[8,128]{1,0:T(8,128)S(1)} %get-tuple-element.76), channel_id=1, source_target_pairs={{0,2},{1,3},{2,0},{3,1},{4,6},{5,7},{6,4},{7,5},{8,10},{9,11},{10,... | collective-permute-start | bytes 12296 | tf_op jit(solution)/shard_map/ppermute | solution.py:589
  10.5 7.4 %collective-permute-start.6 = (bf16[4,128,256]{2,1,0:T(8,128)(2,1)S(1)}, bf16[4,128,256]{2,1,0:T(8,128)(2,1)S(1)}, u32[]{:S(2)}, u32[]{:S(2)}) collective-permute-start(bf16[4,128,256]{2,1,0:T(8,128)(2,1)S(1)} %get-tuple-element.84), channel_id=1, source_target_pairs={{0,2},{1,3},{2,0},{3,1},{4,6},{5,7},{6,4},{7,5},{8,10},{9,11},{10,... | collective-permute-start | bytes 786440 | tf_op jit(solution)/shard_map/ppermute | solution.py:589
  12.5 2.9 %collective-permute-start.5 = (bf16[4,128,256]{2,1,0:T(8,128)(2,1)S(1)}, bf16[4,128,256]{2,1,0:T(8,128)(2,1)S(1)}, u32[]{:S(2)}, u32[]{:S(2)}) collective-permute-start(bf16[4,128,256]{2,1,0:T(8,128)(2,1)S(1)} %get-tuple-element.83), channel_id=1, source_target_pairs={{0,1},{1,0},{2,3},{3,2},{4,5},{5,4},{6,7},{7,6},{8,9},{9,8},{10,11... | collective-permute-start | bytes 786440 | tf_op jit(solution)/shard_map/ppermute | solution.py:589
  15.3 2.1 %collective-permute-start.4 = (bf16[4,128,256]{2,1,0:T(8,128)(2,1)S(1)}, bf16[4,128,256]{2,1,0:T(8,128)(2,1)S(1)}, u32[]{:S(2)}, u32[]{:S(2)}) collective-permute-start(bf16[4,128,256]{2,1,0:T(8,128)(2,1)S(1)} %get-tuple-element.82), channel_id=1, source_target_pairs={{0,1},{1,0},{2,3},{3,2},{4,5},{5,4},{6,7},{7,6},{8,9},{9,8},{10,11... | collective-permute-start | bytes 786440 | tf_op jit(solution)/shard_map/ppermute | solution.py:589
  15.7 9.3 %collective-permute-start.9 = (bf16[4,128,256]{2,1,0:T(8,128)(2,1)S(1)}, bf16[4,128,256]{2,1,0:T(8,128)(2,1)S(1)}, u32[]{:S(2)}, u32[]{:S(2)}) collective-permute-start(bf16[4,128,256]{2,1,0:T(8,128)(2,1)S(1)} %compose.8.rest_0_), channel_id=1, source_target_pairs={{0,2},{1,3},{2,0},{3,1},{4,6},{5,7},{6,4},{7,5},{8,10},{9,11},{10,... | collective-permute-start | bytes 786440 | tf_op jit(solution)/shard_map/ppermute | solution.py:589
  18.2 4.8 %copy-start.2 = (bf16[128,4096]{1,0:T(8,128)(2,1)S(1)}, bf16[128,4096]{1,0:T(8,128)(2,1)}, u32[]{:S(2)}) copy-start(bf16[128,4096]{1,0:T(8,128)(2,1)} %q_hbm.7) | copy-start | bytes 3145732
  18.2 7.0 %collective-permute-start.10 = (bf16[4,128,256]{2,1,0:T(8,128)(2,1)S(1)}, bf16[4,128,256]{2,1,0:T(8,128)(2,1)S(1)}, u32[]{:S(2)}, u32[]{:S(2)}) collective-permute-start(bf16[4,128,256]{2,1,0:T(8,128)(2,1)S(1)} %compose.10.refs_6_), channel_id=1, source_target_pairs={{0,4},{4,0},{8,12},{12,8},{16,20},{20,16},{24,28},{28,24},{1,5},{5... | collective-permute-start | bytes 786440 | tf_op jit(solution)/shard_map/ppermute | solution.py:589
  21.4 3.3 %collective-permute-start.8 = (bf16[4,128,256]{2,1,0:T(8,128)(2,1)S(1)}, bf16[4,128,256]{2,1,0:T(8,128)(2,1)S(1)}, u32[]{:S(2)}, u32[]{:S(2)}) collective-permute-start(bf16[4,128,256]{2,1,0:T(8,128)(2,1)S(1)} %get-tuple-element.88), channel_id=1, source_target_pairs={{0,1},{1,0},{2,3},{3,2},{4,5},{5,4},{6,7},{7,6},{8,9},{9,8},{10,11... | collective-permute-start | bytes 786440 | tf_op jit(solution)/shard_map/ppermute | solution.py:589
  25.5 6.1 %collective-permute-start.11 = (bf16[4,128,256]{2,1,0:T(8,128)(2,1)S(1)}, bf16[4,128,256]{2,1,0:T(8,128)(2,1)S(1)}, u32[]{:S(2)}, u32[]{:S(2)}) collective-permute-start(bf16[4,128,256]{2,1,0:T(8,128)(2,1)S(1)} %compose.13.refs_0_), channel_id=1, source_target_pairs={{0,8},{4,12},{8,0},{12,4},{16,24},{20,28},{24,16},{28,20},{1,9},{5... | collective-permute-start | bytes 786440 | tf_op jit(solution)/shard_map/ppermute | solution.py:589
  31.9 6.2 %collective-permute-start.12 = (bf16[4,128,128]{2,1,0:T(8,128)(2,1)S(1)}, bf16[4,128,128]{2,1,0:T(8,128)(2,1)S(1)}, u32[]{:S(2)}, u32[]{:S(2)}) collective-permute-start(bf16[4,128,128]{2,1,0:T(8,128)(2,1)S(1)} %get-tuple-element.104), channel_id=1, source_target_pairs={{0,16},{4,20},{8,24},{12,28},{16,0},{20,4},{24,8},{28,12},{1,17},{... | collective-permute-start | bytes 393224 | tf_op jit(solution)/shard_map/ppermute | solution.py:589
  38.4 4.7 %collective-permute-start.14 = (f32[8,128]{1,0:T(8,128)S(1)}, f32[8,128]{1,0:T(8,128)S(1)}, u32[]{:S(2)}, u32[]{:S(2)}) collective-permute-start(f32[8,128]{1,0:T(8,128)S(1)} %get-tuple-element.108), channel_id=1, source_target_pairs={{0,1},{1,0},{2,3},{3,2},{4,5},{5,4},{6,7},{7,6},{8,9},{9,8},{10,11... | collective-permute-start | bytes 12296 | tf_op jit(solution)/shard_map/ppermute | solution.py:589
  42.3 5.1 %collective-permute-start.13 = (bf16[4,128,128]{2,1,0:T(8,128)(2,1)S(1)}, bf16[4,128,128]{2,1,0:T(8,128)(2,1)S(1)}, u32[]{:S(2)}, u32[]{:S(2)}) collective-permute-start(bf16[4,128,128]{2,1,0:T(8,128)(2,1)S(1)} %get-tuple-element.106), channel_id=1, source_target_pairs={{0,4},{4,0},{8,12},{12,8},{16,20},{20,16},{24,28},{28,24},{1,5},{5... | collective-permute-start | bytes 393224 | tf_op jit(solution)/shard_map/ppermute | solution.py:589
  43.5 2.2 %collective-permute-start.15 = (bf16[4,128,128]{2,1,0:T(8,128)(2,1)S(1)}, bf16[4,128,128]{2,1,0:T(8,128)(2,1)S(1)}, u32[]{:S(2)}, u32[]{:S(2)}) collective-permute-start(bf16[4,128,128]{2,1,0:T(8,128)(2,1)S(1)} %get-tuple-element.109), channel_id=1, source_target_pairs={{0,1},{1,0},{2,3},{3,2},{4,5},{5,4},{6,7},{7,6},{8,9},{9,8},{10,11... | collective-permute-start | bytes 393224 | tf_op jit(solution)/shard_map/ppermute | solution.py:589
  43.9 6.6 %collective-permute-start.17 = (bf16[4,128,128]{2,1,0:T(8,128)(2,1)S(1)}, bf16[4,128,128]{2,1,0:T(8,128)(2,1)S(1)}, u32[]{:S(2)}, u32[]{:S(2)}) collective-permute-start(bf16[4,128,128]{2,1,0:T(8,128)(2,1)S(1)} %get-tuple-element.112), channel_id=1, source_target_pairs={{0,2},{1,3},{2,0},{3,1},{4,6},{5,7},{6,4},{7,5},{8,10},{9,11},{10,... | collective-permute-start | bytes 393224 | tf_op jit(solution)/shard_map/ppermute | solution.py:589
  47.7 2.7 %collective-permute-start.18 = (f32[8,128]{1,0:T(8,128)S(1)}, f32[8,128]{1,0:T(8,128)S(1)}, u32[]{:S(2)}, u32[]{:S(2)}) collective-permute-start(f32[8,128]{1,0:T(8,128)S(1)} %get-tuple-element.114), channel_id=1, source_target_pairs={{0,1},{1,0},{2,3},{3,2},{4,5},{5,4},{6,7},{7,6},{8,9},{9,8},{10,11... | collective-permute-start | bytes 12296 | tf_op jit(solution)/shard_map/ppermute | solution.py:589
  48.6 5.1 %collective-permute-start.16 = (bf16[4,128,128]{2,1,0:T(8,128)(2,1)S(1)}, bf16[4,128,128]{2,1,0:T(8,128)(2,1)S(1)}, u32[]{:S(2)}, u32[]{:S(2)}) collective-permute-start(bf16[4,128,128]{2,1,0:T(8,128)(2,1)S(1)} %get-tuple-element.111), channel_id=1, source_target_pairs={{0,2},{1,3},{2,0},{3,1},{4,6},{5,7},{6,4},{7,5},{8,10},{9,11},{10,... | collective-permute-start | bytes 393224 | tf_op jit(solution)/shard_map/ppermute | solution.py:589
  50.1 1.4 %collective-permute-start.20 = (bf16[4,128,128]{2,1,0:T(8,128)(2,1)S(1)}, bf16[4,128,128]{2,1,0:T(8,128)(2,1)S(1)}, u32[]{:S(2)}, u32[]{:S(2)}) collective-permute-start(bf16[4,128,128]{2,1,0:T(8,128)(2,1)S(1)} %get-tuple-element.116), channel_id=1, source_target_pairs={{0,1},{1,0},{2,3},{3,2},{4,5},{5,4},{6,7},{7,6},{8,9},{9,8},{10,11... | collective-permute-start | bytes 393224 | tf_op jit(solution)/shard_map/ppermute | solution.py:589
  50.7 1.4 %collective-permute-start.19 = (bf16[4,128,128]{2,1,0:T(8,128)(2,1)S(1)}, bf16[4,128,128]{2,1,0:T(8,128)(2,1)S(1)}, u32[]{:S(2)}, u32[]{:S(2)}) collective-permute-start(bf16[4,128,128]{2,1,0:T(8,128)(2,1)S(1)} %get-tuple-element.115), channel_id=1, source_target_pairs={{0,1},{1,0},{2,3},{3,2},{4,5},{5,4},{6,7},{7,6},{8,9},{9,8},{10,11... | collective-permute-start | bytes 393224 | tf_op jit(solution)/shard_map/ppermute | solution.py:589
  53.9 2.1 %collective-permute-start.21 = (bf16[4,128,128]{2,1,0:T(8,128)(2,1)S(1)}, bf16[4,128,128]{2,1,0:T(8,128)(2,1)S(1)}, u32[]{:S(2)}, u32[]{:S(2)}) collective-permute-start(bf16[4,128,128]{2,1,0:T(8,128)(2,1)S(1)} %get-tuple-element.120), channel_id=1, source_target_pairs={{0,1},{1,0},{2,3},{3,2},{4,5},{5,4},{6,7},{7,6},{8,9},{9,8},{10,11... | collective-permute-start | bytes 393224 | tf_op jit(solution)/shard_map/ppermute | solution.py:589
  (7 other events, 11.7 us)

commit v5 on v4

--- a/solution.py
+++ b/solution.py
@@ -36,6 +36,10 @@
 
 
 def parity():
+    return jnp.bitwise_and(lax.shift_right_logical(lax.axis_index("context"), 1), 1)
+
+
+def quarter_parity():
     return jnp.bitwise_and(lax.axis_index("context"), 1)
 
 
@@ -403,6 +407,111 @@
     return done if with_token else done[0]
 
 
+def split_kernel(bit, own_ref, got_ref, *rest):
+    later = is_later(bit)
+    quarter = own_ref.shape[0] // 2
+    for number, out_ref in enumerate(rest[-2:]):
+        first = jnp.bitwise_xor(1 - number, quarter_parity()) * quarter
+        for j in range(quarter):
+            earlier_block, later_block = pick(later, own_ref[first + j], got_ref[first + j])
+            out_ref[j] = joined(earlier_block, later_block).astype(BF16)
+
+
+def compose_split(bit, own, got, *after):
+    part = jax.ShapeDtypeStruct((own.shape[0] // 2,) + own.shape[1:], BF16)
+    return pl.pallas_call(
+        functools.partial(split_kernel, bit),
+        out_shape=(part, part),
+        in_specs=[whole_vmem()] * (2 + len(after)),
+        out_specs=(whole_vmem(),) * 2,
+        compiler_params=params(),
+        cost_estimate=cost(),
+        name="compose",
+    )(own, got, *after)
+
+
+def place_in_four():
+    return jnp.bitwise_and(lax.axis_index("context"), 3)
+
+
+def choose(index, values):
+    chosen = values[0]
+    for number in range(1, len(values)):
+        chosen = jnp.where(index == number, values[number], chosen)
+    return chosen
+
+
+def four_kernel(last, *refs):
+    blocks, (total_ref, before_ref) = refs[:4], refs[-2:]
+    heads, size = blocks[0].shape[:2]
+    every = range(heads)
+    own = place_in_four()
+    ordered = [
+        [choose(jnp.bitwise_xor(own, place), [ref[j] for ref in blocks]) for j in every] for place in range(4)
+    ]
+    running = ordered[0]
+    for place in range(1, 4):
+        for j in every:
+            before_ref[place - 1, j] = running[j]
+        running = [joined(running[j], ordered[place][j]).astype(BF16) for j in every]
+    for j in every:
+        total_ref[j] = running[j][:, size:] if last else running[j]
+
+
+def four(last, blocks, *after):
+    heads, size = blocks[0].shape[:2]
+    arrays = tuple(blocks) + after
+    return pl.pallas_call(
+        functools.partial(four_kernel, last),
+        out_shape=(
+            jax.ShapeDtypeStruct((heads, size, size if last else 2 * size), BF16),
+            jax.ShapeDtypeStruct((3,) + blocks[0].shape, BF16),
+        ),
+        in_specs=[whole_vmem()] * len(arrays),
+        out_specs=(whole_vmem(),) * 2,
+        compiler_params=params(),
+        cost_estimate=cost(),
+        name="four",
+    )(*arrays)
+
+
+def spread_kernel(top, with_outer, carried_ref, before_ref, *rest):
+    outs = rest[-4:]
+    heads, size = carried_ref.shape[:2]
+    every = range(heads)
+    own = place_in_four()
+
+    def through(block, state):
+        return (dot(block[:, :size], state) + block[:, size:].astype(F32)).astype(BF16)
+
+    later = is_later(top)
+    if with_outer:
+        outer = rest[0]
+        state = [
+            jnp.where(later, through(outer[j], carried_ref[j]), outer[j, :, size:]) for j in every
+        ]
+    else:
+        state = [jnp.where(later, carried_ref[j], jnp.zeros_like(carried_ref[j])) for j in every]
+    entering = [state] + [[through(before_ref[place, j], state[j]) for j in every] for place in range(3)]
+    for distance in (3, 2, 1, 0):
+        there = jnp.bitwise_xor(own, distance)
+        for j in every:
+            outs[distance][j] = choose(there, [entering[place][j] for place in range(4)])
+
+
+def spread(top, carried, before, outer, *after):
+    arrays = (carried, before) + (() if outer is None else (outer,)) + after
+    return pl.pallas_call(
+        functools.partial(spread_kernel, top, outer is not None),
+        out_shape=(jax.ShapeDtypeStruct(carried.shape, BF16),) * 4,
+        in_specs=[whole_vmem()] * len(arrays),
+        out_specs=(whole_vmem(),) * 4,
+        compiler_params=params(),
+        cost_estimate=cost(),
+        name="spread",
+    )(*arrays)
+
+
 def doubling_kernel(bit, first, last, *refs):
     later = is_later(bit)
     own_ref, got_ref = refs[:2]
@@ -439,9 +548,9 @@
     )(*arrays)
 
 
-def descend_kernel(bits, top, threaded, with_token, *refs):
+def descend_kernel(bits, joint, threaded, with_token, *refs):
     count = len(bits)
-    start = 2 if top is not None else 1
+    start = 2 if joint else 1
     blocks = refs[start : start + 2 * count]
     outs = refs[start + 2 * count + threaded :]
     sends, kept_ref = outs[:count], outs[count]
@@ -449,11 +558,15 @@
         outs[-1][...] = jnp.zeros_like(outs[-1])
     size = kept_ref.shape[-1]
     every = range(kept_ref.shape[0])
-    if top is None:
+    if joint:
+        quarter = refs[0].shape[0]
+        flip = quarter_parity() == 1
+        state = []
+        for j in every:
+            same, other = refs[j // quarter], refs[1 - j // quarter]
+            state.append(jnp.where(flip, other[j % quarter], same[j % quarter]))
+    else:
         state = [refs[0][j] for j in every]
-    else:
-        carried = [dot(refs[1][j, :, :size], refs[0][j]) + refs[1][j, :, size:].astype(F32) for j in every]
-        state = [jnp.where(is_later(top), carried[j].astype(BF16), refs[1][j, :, size:]) for j in every]
     for level, bit in enumerate(bits):
         later = is_later(bit)
         own_ref, got_ref = blocks[2 * level : 2 * level + 2]
@@ -468,8 +581,8 @@
         kept_ref[j] = state[j]
 
 
-def descend(bits, top, sources, blocks, thread, *after, with_token=False):
-    heads, size = sources[0].shape[0], sources[0].shape[1]
+def descend(bits, sources, blocks, thread, *after, with_token=False):
+    heads, size = sum(array.shape[0] for array in sources), sources[0].shape[1]
     arrays = list(sources) + [array for pair in blocks for array in pair]
     specs = [whole_vmem()] * len(arrays)
     outs = len(bits) + 1
@@ -488,7 +601,7 @@
     arrays += after
     specs += [whole_vmem()] * len(after)
     return pl.pallas_call(
-        functools.partial(descend_kernel, bits, top, int(thread is not None) + len(after), with_token),
+        functools.partial(descend_kernel, bits, len(sources) > 1, int(thread is not None) + len(after), with_token),
         out_shape=tuple(shapes),
         in_specs=specs,
         out_specs=tuple(out_specs),
@@ -537,7 +650,7 @@
     arrays = [gain, state, qo, gate] + [strip for strip, _ in stored] + list(after)
     specs = [whole_vmem()] * len(arrays)
     aliases = {}
-    if result is not None:
+    if result is not None and (stored or is_last):
         aliases = {len(arrays): 0}
         arrays.append(result)
         specs.append(in_hbm())
@@ -622,7 +735,6 @@
     far, got, near, chip = {}, {}, {}, {}
     first_done = ab[far_parts[-1], 1]
     fetched_near = fetch(near_parts, half, size, None, *inputs, first_done)
-    early = swap(flags, "head", 1)
     far[1], token = fold(
         1 << under, 1, under, *far_biases, fetched_near[0], with_token=True, carried=len(far_biases)
     )
@@ -635,9 +747,10 @@
     far[0] = fold(1 << under, 0, under)
     got[0] = swap(far[0], "head", 1 << under)
     near[1] = fold(0, 1, under, far[0])
-    chip[1] = compose(head_bit[under], near[1], got[1])
-    across = swap(chip[1], "context", 1)
-    work(near_parts, 0, fetched_near, gap, near_tables, chip[1], early)
+    to_three, to_two = compose_split(head_bit[under], near[1], got[1])
+    from_three = swap(to_three, "context", 3)
+    from_two = swap(to_two, "context", 2)
+    work(near_parts, 0, fetched_near, gap, near_tables, ab[near_parts[-1], 1], far[0])
 
     def look(part, *after):
         names, data, known = (
@@ -649,48 +762,38 @@
         return gain
 
     every_part = far_parts + near_parts
-    look(every_part[0], ab[near_parts[-1], 0])
-    near[0] = fold(0, 0, under, qo[every_part[0], 0])
-    chip[0] = compose(head_bit[under], near[0], got[0])
+    near[0] = fold(0, 0, under)
+    to_one, mine = compose_split(head_bit[under], near[0], got[0])
+    from_one = swap(to_one, "context", 1)
     for turn in (1, 0):
         levels[under][0, turn] = (near[turn], got[turn])
 
-    x_pair = (chip[0], across)
-    total = compose(context_bit[0], *x_pair)
-    before = None
+    for part in every_part[:2]:
+        look(part, mine)
+    only_last = context_bits == 3
+    outlooks = [qo[part, 0] for part in every_part[:2]]
+    total, before = four(only_last, (mine, from_one, from_two, from_three), *outlooks)
+    outer = None
     held = [array for level in levels[:under] for pair in level.values() for array in pair]
-    for part in every_part[1:]:
-        gain = look(part, chip[0], *held)
-    for bit in range(1, context_bits - 1):
+    for part in every_part[2:]:
+        gain = look(part, total, *held)
+    done_by = [qo[part, turn] for part in every_part for turn in (0, 1)] + held
+    for bit in range(2, context_bits - 1):
         other = swap(total, "context", 1 << bit)
-        done_by = tuple(qo[part, turn] for part in every_part for turn in (0, 1)) + tuple(held) if bit == 1 else ()
-        total, before = doubling(context_bit[bit], bit == context_bits - 2, total, other, before, *done_by)
+        total, outer = doubling(context_bit[bit], bit == context_bits - 2, total, other, outer)
     other = swap(total, "context", 1 << (context_bits - 1))
 
     states = {}
-    result = None
-    descending = list(reversed(range(head_bits)))
-    first = descend([context_bit[0]], context_bit[-1], (other, before), [x_pair], None, with_token=True)
-    arriving = [(0, 1, head_bits, swap(first[0], "context", 1))]
-    outs = descend(
-        [head_bit[bit] for bit in descending],
-        None,
-        (first[1],),
-        [levels[bit][0, 0] for bit in descending],
-        None,
-        swap(first[-1], "head", 1),
-    )
-    states[0, 0] = outs[-1]
-    for level, bit in enumerate(descending):
-        arriving.append((1 << bit, 0, bit, swap(outs[level], "head", 1 << bit)))
-    ready = [(0, 0)]
+    entering = spread(context_bit[-1], other, before, outer, gate_input, *done_by)
+    from_far = {distance: swap(entering[distance], "context", distance) for distance in (3, 2, 1)}
     total_units = 2 * head_count
-
-    strips = []
-
-    def write(part, turn, result):
+    strips, waiting, results = [], [], [None]
+
+    def write(part, turn):
         number = len(strips) + 1
-        stored = strips if number == total_units - 1 else strips[-1:] if number == total_units else []
+        stored = []
+        if number in (total_units // 2, total_units - 1, total_units):
+            stored, waiting[:] = waiting[:], []
         chained = [strips[-1][0]] if strips and not stored else []
         result, strip = finish(
             (part, turn),
@@ -699,43 +802,56 @@
             qo[part, turn],
             gate_input,
             gain,
-            result,
-            list(stored),
+            results[-1],
+            [(strips[entry][0], strips[entry][1]) for entry in stored],
             *chained,
         )
+        results.append(result)
+        waiting.append(len(strips))
         strips.append((strip, (part, turn)))
-        return result
-
-    while arriving or ready:
-        for part, turn in ready:
-            result = write(part, turn, result)
-        ready = []
-        leaves = [entry for entry in arriving if entry[2] == 0]
-        inner = [entry for entry in arriving if entry[2] > 0]
-        arriving = []
-        for part, turn, _, state in leaves:
+
+    leaves = []
+    inner = [
+        (0, 0, head_bits, (entering[0], from_far[1])),
+        (0, 1, head_bits, (from_far[2], from_far[3])),
+    ]
+
+    def pass_on(part, turn, below, sources):
+        down = list(reversed(range(below)))
+        outs = descend(
+            [head_bit[bit] for bit in down],
+            sources,
+            [levels[bit][part, turn] for bit in down],
+            strips[-1][0] if strips else None,
+        )
+        states[part, turn] = outs[below]
+        if strips:
+            strips[-1] = (outs[below + 1], strips[-1][1])
+        for level, bit in enumerate(down):
+            entry = (part | 1 << bit, turn, bit, (swap(outs[level], "head", 1 << bit),))
+            (inner if bit else leaves).append(entry)
+
+    def write_leaves(entries):
+        for part, turn, _, (state,) in entries:
             states[part, turn] = state
-            result = write(part, turn, result)
-        tokens = ()
-        for number, (part, turn, below, state) in enumerate(inner):
-            down = list(reversed(range(below)))
-            more = number + 1 < len(inner)
-            outs = descend(
-                [head_bit[bit] for bit in down],
-                None,
-                (state,),
-                [levels[bit][part, turn] for bit in down],
-                strips[-1][0],
-                *tokens,
-                with_token=more,
-            )
-            states[part, turn] = outs[below]
-            strips[-1] = (outs[below + 1], strips[-1][1])
-            ready.append((part, turn))
-            for level, bit in enumerate(down):
-                arriving.append((part | 1 << bit, turn, bit, swap(outs[level], "head", 1 << bit)))
-            tokens = (swap(outs[-1], "head", 1),) if more else ()
-    return result
+            write(part, turn)
+
+    depth = head_bits
+    while inner:
+        inner.sort(key=lambda entry: (-entry[2], entry[1]))
+        part, turn, below, sources = inner.pop(0)
+        if below < depth or turn and below == head_bits:
+            write_leaves(leaves)
+            leaves.clear()
+            depth = below
+        known = len(leaves)
+        pass_on(part, turn, below, sources)
+        if not inner:
+            write_leaves(leaves[:known])
+            del leaves[:known]
+        write(part, turn)
+    write_leaves(leaves)
+    return results[-1]
 
 
 def solution(mesh):

time: 57.4 us -> 56.3 us (0.981)
  waiting for transfers between devices: 8.91 us -> 5.6 us
  starting transfers between devices: 23.2 us -> 24.9 us
    ppermute x22, waiting for transfers between devices: 8.91 us -> 5.6 us  [swap(): return lax.ppermute(array, axis, [(i, i ^ distance) for i in range(count)])]
    ppermute x22, starting transfers between devices: 23.2 us -> 24.9 us  [swap(): return lax.ppermute(array, axis, [(i, i ^ distance) for i in range(count)])]
    pallas_call x7 -> x4, Pallas kernels: 1.59 us -> 0.9 us  [compose(): pl.pallas_call(functools.partial(compose_kernel, bit, with_token, carried...]
    pallas_call x6 -> x8, Pallas kernels: 1.71 us -> 2.39 us  [the longest x4 1.16 us: descend(): pl.pallas_call(functools.partial(descend_kernel, bits, len(sources) > 1,...]
  transfers between devices with their start and end apart: 22 -> 22, of which waited for: 7 -> 6; matrix products, arithmetic and copies ran while one was open for 0% -> 0% of each run, Pallas kernels for 33% -> 35%
where the time goes in v5:
time: 56.3 us; the launch traced here: 56.2 us
  starting transfers between devices  24.9 us (44%)
  Pallas kernels  23.8 us (42%)
  waiting for transfers between devices  5.6 us (10%)
  local copies, waits for them, and re-layouts  1.34 us (2%)
    ppermute x22, starting transfers between devices, swap(): return lax.ppermute(array, axis, [(i, i ^ distance) for i in range(count)])  24.9 us
    pallas_call x4, Pallas kernels, local(): pl.pallas_call(functools.partial(local_kernel, units), out_shape=(result,...  7.67 us
    ppermute x22, waiting for transfers between devices, swap(): return lax.ppermute(array, axis, [(i, i ^ distance) for i in range(count)])  5.6 us
    pallas_call x8, Pallas kernels, finish(): pl.pallas_call(functools.partial(finish_kernel, unit, [earlier for _, ear...  4.58 us
    pallas_call x4, Pallas kernels, outlook(): pl.pallas_call(functools.partial(outlook_kernel, at, part), out_shape=(ja...  4.12 us
    pallas_call x2, Pallas kernels, fetch(): pl.pallas_call(functools.partial(fetch_kernel, parts, half, doc_start is...  3.44 us
    unnamed x18, local copies, waits for them, and re-layouts  1.34 us
    pallas_call x4, Pallas kernels, descend(): pl.pallas_call(functools.partial(descend_kernel, bits, len(sources) > 1,...  1.16 us
  transfers between devices with their start and end apart: 22, of which 6 were waited for; matrix products, arithmetic and copies ran while one was open for 0% of the time, Pallas kernels for 35%

profile of v5, /device:TPU:1, one launch (start us, length us, event | category | flops | bytes accessed | tf_op | source)
XLA Modules:
  0.0 56.2 jit_solution(12397164634176875301)
XLA Ops:
  0.7 2.4 %fetch.2 = (bf16[2,2,4,128,128]{4,3,2,1,0:T(8,128)(2,1)S(1)}, bf16[2,2,4,128,128]{4,3,2,1,0:T(8,128)(2,1)S(1)}, bf16[2,2,128,512]{3,2,1,0:T(8,128)(2,1)S(1)}, f32[128,128]{1,0:T(8,128)S(1)}, f32[3,8,128]{2,1,0:T(8,128)S(1)}) custom-call(s32[8]{0:T(128)S(1)} %copy-done.6, bf16[128,4096]{1,0:T(8,128)(2,1)} %refs_0_.3, bf16[128,4096]{1,0:T(8,128)(2,1)} %refs_1_.3), custom_call_target="tpu_custom_call" | custom-call | flops 10000000000 | bytes 100000000 | tf_op jit(solution)/shard_map/fetch/pallas_call | solution.py:196
  3.5 1.9 %local_tokens.4 = (bf16[4,128,256]{2,1,0:T(8,128)(2,1)S(1)}, bf16[4,128,256]{2,1,0:T(8,128)(2,1)S(1)}, bf16[4,128,256]{2,1,0:T(8,128)(2,1)S(1)}, bf16[4,128,256]{2,1,0:T(8,128)(2,1)S(1)}) custom-call(bf16[2,2,4,128,128]{4,3,2,1,0:T(8,128)(2,1)S(1)} %get-tuple-element.71.refs_0_, bf16[2,2,4,128,128]{4,3,2,1,0:T(8,128)(2,1)S(1)} %get-tuple-element.72.refs_1_.turned_ref, ...), custom_call_target="tpu_custom_call" | custom-call | flops 10000000000 | bytes 100000000 | tf_op jit(solution)/shard_map/local_tokens/pallas_call | solution.py:307
  6.0 1.1 %fetch.3 = (bf16[2,2,4,128,128]{4,3,2,1,0:T(8,128)(2,1)S(1)}, bf16[2,2,4,128,128]{4,3,2,1,0:T(8,128)(2,1)S(1)}, bf16[2,2,128,512]{3,2,1,0:T(8,128)(2,1)S(1)}) custom-call(bf16[128,4096]{1,0:T(8,128)(2,1)S(1)} %copy-done, bf16[128,4096]{1,0:T(8,128)(2,1)S(1)} %copy-done.1, bf16[4,128,256]{2,1,0:T(8,128)(2,1)S(1)} %get-tuple-element.78.refs_2_.own_ref.refs_3_.rest_9_.refs_1_), custom_call_target="tpu_custom_call" | custom-call | flops 10000000000 | bytes 100000000 | tf_op jit(solution)/shard_map/fetch/pallas_call | solution.py:196
  7.8 2.4 %collective-permute-start.2 = (f32[8,128]{1,0:T(8,128)S(1)}, f32[8,128]{1,0:T(8,128)S(1)}, u32[]{:S(2)}, u32[]{:S(2)}) collective-permute-start(f32[8,128]{1,0:T(8,128)S(1)} %get-tuple-element.82), channel_id=1, source_target_pairs={{0,2},{1,3},{2,0},{3,1},{4,6},{5,7},{6,4},{7,5},{8,10},{9,11},{10,... | collective-permute-start | bytes 12296 | tf_op jit(solution)/shard_map/ppermute | solution.py:702
  10.2 1.9 %local_tokens.5 = (bf16[4,128,256]{2,1,0:T(8,128)(2,1)S(1)}, bf16[4,128,256]{2,1,0:T(8,128)(2,1)S(1)}, bf16[4,128,256]{2,1,0:T(8,128)(2,1)S(1)}, bf16[4,128,256]{2,1,0:T(8,128)(2,1)S(1)}) custom-call(bf16[2,2,4,128,128]{4,3,2,1,0:T(8,128)(2,1)S(1)} %get-tuple-element.71.refs_0_, bf16[2,2,4,128,128]{4,3,2,1,0:T(8,128)(2,1)S(1)} %get-tuple-element.72.refs_1_.turned_ref, ...), custom_call_target="tpu_custom_call" | custom-call | flops 10000000000 | bytes 100000000 | tf_op jit(solution)/shard_map/local_tokens/pallas_call | solution.py:307
  13.2 1.9 %local_tokens.6 = (bf16[4,128,256]{2,1,0:T(8,128)(2,1)S(1)}, bf16[4,128,256]{2,1,0:T(8,128)(2,1)S(1)}, bf16[4,128,256]{2,1,0:T(8,128)(2,1)S(1)}, bf16[4,128,256]{2,1,0:T(8,128)(2,1)S(1)}) custom-call(bf16[2,2,4,128,128]{4,3,2,1,0:T(8,128)(2,1)S(1)} %get-tuple-element.81.rest_2_.refs_0_, ...), custom_call_target="tpu_custom_call" | custom-call | flops 10000000000 | bytes 100000000 | tf_op jit(solution)/shard_map/local_tokens/pallas_call | solution.py:307
  15.5 1.8 %collective-permute-start.6 = (bf16[4,128,256]{2,1,0:T(8,128)(2,1)S(1)}, bf16[4,128,256]{2,1,0:T(8,128)(2,1)S(1)}, u32[]{:S(2)}, u32[]{:S(2)}) collective-permute-start(bf16[4,128,256]{2,1,0:T(8,128)(2,1)S(1)} %compose.7.refs_7_.rest_0_), channel_id=1, source_target_pairs={{0,2},{1,3},{2,0},{3,1},{4,6},{5,7},{6,4},{7,5},{8,10},{9,11},{10,... | collective-permute-start | bytes 786440 | tf_op jit(solution)/shard_map/ppermute | solution.py:702
  17.2 1.9 %local_tokens.7 = (bf16[4,128,256]{2,1,0:T(8,128)(2,1)S(1)}, bf16[4,128,256]{2,1,0:T(8,128)(2,1)S(1)}, bf16[4,128,256]{2,1,0:T(8,128)(2,1)S(1)}, bf16[4,128,256]{2,1,0:T(8,128)(2,1)S(1)}) custom-call(bf16[2,2,4,128,128]{4,3,2,1,0:T(8,128)(2,1)S(1)} %get-tuple-element.81.rest_2_.refs_0_, ...), custom_call_target="tpu_custom_call" | custom-call | flops 10000000000 | bytes 100000000 | tf_op jit(solution)/shard_map/local_tokens/pallas_call | solution.py:307
  20.5 1.4 %collective-permute-start.10 = (bf16[2,128,256]{2,1,0:T(8,128)(2,1)S(1)}, bf16[2,128,256]{2,1,0:T(8,128)(2,1)S(1)}, u32[]{:S(2)}, u32[]{:S(2)}) collective-permute-start(bf16[2,128,256]{2,1,0:T(8,128)(2,1)S(1)} %get-tuple-element.97), channel_id=1, source_target_pairs={{0,8},{4,12},{8,0},{12,4},{16,24},{20,28},{24,16},{28,20},{1,9},{5... | collective-permute-start | bytes 393224 | tf_op jit(solution)/shard_map/ppermute | solution.py:702
  21.9 1.1 %collective-permute-start.11 = (bf16[2,128,256]{2,1,0:T(8,128)(2,1)S(1)}, bf16[2,128,256]{2,1,0:T(8,128)(2,1)S(1)}, u32[]{:S(2)}, u32[]{:S(2)}) collective-permute-start(bf16[2,128,256]{2,1,0:T(8,128)(2,1)S(1)} %get-tuple-element.98), channel_id=1, source_target_pairs={{0,12},{4,8},{8,4},{12,0},{16,28},{20,24},{24,20},{28,16},{1,13},{... | collective-permute-start | bytes 393224 | tf_op jit(solution)/shard_map/ppermute | solution.py:702
  23.7 1.2 %collective-permute-start.7 = (bf16[2,128,256]{2,1,0:T(8,128)(2,1)S(1)}, bf16[2,128,256]{2,1,0:T(8,128)(2,1)S(1)}, u32[]{:S(2)}, u32[]{:S(2)}) collective-permute-start(bf16[2,128,256]{2,1,0:T(8,128)(2,1)S(1)} %get-tuple-element.94), channel_id=1, source_target_pairs={{0,4},{4,0},{8,12},{12,8},{16,20},{20,16},{24,28},{28,24},{1,5},{5... | collective-permute-start | bytes 393224 | tf_op jit(solution)/shard_map/ppermute | solution.py:702
  25.6 1.1 %outlook.5 = (bf16[4,128,256]{2,1,0:T(8,128)(2,1)S(1)}, bf16[4,128,256]{2,1,0:T(8,128)(2,1)S(1)}, f32[1,128]{1,0:T(1,128)}) custom-call(bf16[128,4096]{1,0:T(8,128)(2,1)S(1)} %copy-done.2, bf16[2,2,4,128,128]{4,3,2,1,0:T(8,128)(2,1)S(1)} %get-tuple-element.72.refs_1_.turned_ref, f32[128,128]{1,0:T(8,128)S(1)} %get-tuple-element.74.refs_3_.gap_ref, ...), custom_call_target="tpu_custom_call" | custom-call | flops 10000000000 | bytes 100000000 | tf_op jit(solution)/shard_map/outlook/pallas_call | solution.py:359
  26.6 1.1 %outlook.4 = (bf16[4,128,256]{2,1,0:T(8,128)(2,1)S(1)}, bf16[4,128,256]{2,1,0:T(8,128)(2,1)S(1)}, f32[1,128]{1,0:T(1,128)}) custom-call(bf16[128,4096]{1,0:T(8,128)(2,1)S(1)} %copy-done.2, bf16[2,2,4,128,128]{4,3,2,1,0:T(8,128)(2,1)S(1)} %get-tuple-element.72.refs_1_.turned_ref, f32[128,128]{1,0:T(8,128)S(1)} %get-tuple-element.74.refs_3_.gap_ref, ...), custom_call_target="tpu_custom_call" | custom-call | flops 10000000000 | bytes 100000000 | tf_op jit(solution)/shard_map/outlook/pallas_call | solution.py:359
  27.7 1.7 %collective-permute-done.11.refs_3_ = bf16[2,128,256]{2,1,0:T(8,128)(2,1)S(1)} collective-permute-done((bf16[2,128,256]{2,1,0:T(8,128)(2,1)S(1)}, bf16[2,128,256]{2,1,0:T(8,128)(2,1)S(1)}, u32[]{:S(2)}, u32[]{:S(2)}) %collective-permute-start.11) | collective-permute-done | bytes 131104 | tf_op jit(solution)/shard_map/ppermute | solution.py:702
  29.5 1.9 %collective-permute-done.7.refs_1_ = bf16[2,128,256]{2,1,0:T(8,128)(2,1)S(1)} collective-permute-done((bf16[2,128,256]{2,1,0:T(8,128)(2,1)S(1)}, bf16[2,128,256]{2,1,0:T(8,128)(2,1)S(1)}, u32[]{:S(2)}, u32[]{:S(2)}) %collective-permute-start.7) | collective-permute-done | bytes 131104 | tf_op jit(solution)/shard_map/ppermute | solution.py:702
  31.9 2.2 %collective-permute-start.12 = (bf16[2,128,128]{2,1,0:T(8,128)(2,1)S(1)}, bf16[2,128,128]{2,1,0:T(8,128)(2,1)S(1)}, u32[]{:S(2)}, u32[]{:S(2)}) collective-permute-start(bf16[2,128,128]{2,1,0:T(8,128)(2,1)S(1)} %get-tuple-element.105.refs_2_), channel_id=1, source_target_pairs={{0,16},{4,20},{8,24},{12,28},{16,0},{20,4},{24,8},{28,12},{1,17},{... | collective-permute-start | bytes 196616 | tf_op jit(solution)/shard_map/ppermute | solution.py:702
  34.9 1.3 %outlook.7 = (bf16[4,128,256]{2,1,0:T(8,128)(2,1)S(1)}, bf16[4,128,256]{2,1,0:T(8,128)(2,1)S(1)}, f32[1,128]{1,0:T(1,128)}) custom-call(bf16[128,4096]{1,0:T(8,128)(2,1)S(1)} %copy-done.2, bf16[2,2,4,128,128]{4,3,2,1,0:T(8,128)(2,1)S(1)} %get-tuple-element.79.refs_1_.turned_ref, f32[128,128]{1,0:T(8,128)S(1)} %get-tuple-element.74.refs_3_.gap_ref, ...), custom_call_target="tpu_custom_call" | custom-call | flops 10000000000 | bytes 100000000 | tf_op jit(solution)/shard_map/outlook/pallas_call | solution.py:359
  36.4 1.6 %collective-permute-start.15 = (bf16[2,128,128]{2,1,0:T(8,128)(2,1)S(1)}, bf16[2,128,128]{2,1,0:T(8,128)(2,1)S(1)}, u32[]{:S(2)}, u32[]{:S(2)}) collective-permute-start(bf16[2,128,128]{2,1,0:T(8,128)(2,1)S(1)} %get-tuple-element.119), channel_id=1, source_target_pairs={{0,4},{4,0},{8,12},{12,8},{16,20},{20,16},{24,28},{28,24},{1,5},{5... | collective-permute-start | bytes 196616 | tf_op jit(solution)/shard_map/ppermute | solution.py:702
  38.0 2.2 %collective-permute-start.13 = (bf16[2,128,128]{2,1,0:T(8,128)(2,1)S(1)}, bf16[2,128,128]{2,1,0:T(8,128)(2,1)S(1)}, u32[]{:S(2)}, u32[]{:S(2)}) collective-permute-start(bf16[2,128,128]{2,1,0:T(8,128)(2,1)S(1)} %get-tuple-element.116), channel_id=1, source_target_pairs={{0,8},{4,12},{8,0},{12,4},{16,24},{20,28},{24,16},{28,20},{1,9},{5... | collective-permute-start | bytes 196616 | tf_op jit(solution)/shard_map/ppermute | solution.py:702
  40.6 3.3 %collective-permute-start.16 = (bf16[4,128,128]{2,1,0:T(8,128)(2,1)S(1)}, bf16[4,128,128]{2,1,0:T(8,128)(2,1)S(1)}, u32[]{:S(2)}, u32[]{:S(2)}) collective-permute-start(bf16[4,128,128]{2,1,0:T(8,128)(2,1)S(1)} %get-tuple-element.120), channel_id=1, source_target_pairs={{0,1},{1,0},{2,3},{3,2},{4,5},{5,4},{6,7},{7,6},{8,9},{9,8},{10,11... | collective-permute-start | bytes 393224 | tf_op jit(solution)/shard_map/ppermute | solution.py:702
  43.9 2.2 %collective-permute-start.18 = (bf16[4,128,128]{2,1,0:T(8,128)(2,1)S(1)}, bf16[4,128,128]{2,1,0:T(8,128)(2,1)S(1)}, u32[]{:S(2)}, u32[]{:S(2)}) collective-permute-start(bf16[4,128,128]{2,1,0:T(8,128)(2,1)S(1)} %get-tuple-element.123), channel_id=1, source_target_pairs={{0,2},{1,3},{2,0},{3,1},{4,6},{5,7},{6,4},{7,5},{8,10},{9,11},{10,... | collective-permute-start | bytes 393224 | tf_op jit(solution)/shard_map/ppermute | solution.py:702
  49.5 1.0 %finish.11 = (bf16[128,4096]{1,0:T(8,128)(2,1)}, bf16[128,512]{1,0:T(8,128)(2,1)S(1)}) custom-call(f32[1,128]{1,0:T(1,128)S(1)} %get-tuple-element.106.gain_ref, bf16[4,128,128]{2,1,0:T(8,128)(2,1)S(1)} %collective-permute-done.19.state_ref, bf16[4,128,256]{2,1,0:T(8,128)(2,1)S(1)} %get-tuple-element.113.rest_6_.qo_ref, bf16[128,4096]{1,0:T(8,128)(2,1)S(1)} %copy-done.3, ...), custom_call_target="tpu_custom_call" | custom-call | flops 10000000000 | bytes 100000000 | tf_op jit(solution)/shard_map/finish/pallas_call | solution.py:668
  52.6 1.0 %collective-permute-start.20 = (bf16[4,128,128]{2,1,0:T(8,128)(2,1)S(1)}, bf16[4,128,128]{2,1,0:T(8,128)(2,1)S(1)}, u32[]{:S(2)}, u32[]{:S(2)}) collective-permute-start(bf16[4,128,128]{2,1,0:T(8,128)(2,1)S(1)} %get-tuple-element.130), channel_id=1, source_target_pairs={{0,1},{1,0},{2,3},{3,2},{4,5},{5,4},{6,7},{7,6},{8,9},{9,8},{10,11... | collective-permute-start | bytes 393224 | tf_op jit(solution)/shard_map/ppermute | solution.py:702
  54.0 1.0 %finish.14 = (bf16[128,4096]{1,0:T(8,128)(2,1)}, bf16[128,512]{1,0:T(8,128)(2,1)S(1)}) custom-call(f32[1,128]{1,0:T(1,128)S(1)} %get-tuple-element.106.gain_ref, bf16[4,128,128]{2,1,0:T(8,128)(2,1)S(1)} %get-tuple-element.131.state_ref, bf16[4,128,256]{2,1,0:T(8,128)(2,1)S(1)} %get-tuple-element.109.rest_4_.qo_ref, ...), custom_call_target="tpu_custom_call", output_to_operand_aliasing={{0}: (7, {})} | custom-call | flops 10000000000 | bytes 100000000 | tf_op jit(solution)/shard_map/finish/pallas_call | solution.py:668
  (70 shorter events, 15.0 us)
Async XLA Ops:
  0.7 2.4 %collective-permute-start = (f32[1,8]{1,0:T(1,128)S(1)}, f32[1,8]{1,0:T(1,128)S(1)}, u32[]{:S(2)}, u32[]{:S(2)}) collective-permute-start(f32[1,8]{1,0:T(1,128)S(1)} %bitcast.8), channel_id=1, source_target_pairs={{0,1},{1,0},{2,3},{3,2},{4,5},{5,4},{6,7},{7,6},{8,9},{9,8},{10,11... | collective-permute-start | bytes 104 | tf_op jit(solution)/shard_map/ppermute | solution.py:702
  3.5 2.5 %copy-start = (bf16[128,4096]{1,0:T(8,128)(2,1)S(1)}, bf16[128,4096]{1,0:T(8,128)(2,1)}, u32[]{:S(2)}) copy-start(bf16[128,4096]{1,0:T(8,128)(2,1)} %refs_0_.3) | copy-start | bytes 3145732
  3.5 2.5 %copy-start.1 = (bf16[128,4096]{1,0:T(8,128)(2,1)S(1)}, bf16[128,4096]{1,0:T(8,128)(2,1)}, u32[]{:S(2)}) copy-start(bf16[128,4096]{1,0:T(8,128)(2,1)} %refs_1_.3) | copy-start | bytes 3145732
  5.4 1.7 %collective-permute-start.1 = (bf16[4,128,256]{2,1,0:T(8,128)(2,1)S(1)}, bf16[4,128,256]{2,1,0:T(8,128)(2,1)S(1)}, u32[]{:S(2)}, u32[]{:S(2)}) collective-permute-start(bf16[4,128,256]{2,1,0:T(8,128)(2,1)S(1)} %get-tuple-element.80), channel_id=1, source_target_pairs={{0,1},{1,0},{2,3},{3,2},{4,5},{5,4},{6,7},{7,6},{8,9},{9,8},{10,11... | collective-permute-start | bytes 786440 | tf_op jit(solution)/shard_map/ppermute | solution.py:702
  7.4 2.9 %collective-permute-start.3 = (f32[8,128]{1,0:T(8,128)S(1)}, f32[8,128]{1,0:T(8,128)S(1)}, u32[]{:S(2)}, u32[]{:S(2)}) collective-permute-start(f32[8,128]{1,0:T(8,128)S(1)} %get-tuple-element.82), channel_id=1, source_target_pairs={{0,1},{1,0},{2,3},{3,2},{4,5},{5,4},{6,7},{7,6},{8,9},{9,8},{10,11... | collective-permute-start | bytes 12296 | tf_op jit(solution)/shard_map/ppermute | solution.py:702
  7.8 5.1 %collective-permute-start.2 = (f32[8,128]{1,0:T(8,128)S(1)}, f32[8,128]{1,0:T(8,128)S(1)}, u32[]{:S(2)}, u32[]{:S(2)}) collective-permute-start(f32[8,128]{1,0:T(8,128)S(1)} %get-tuple-element.82), channel_id=1, source_target_pairs={{0,2},{1,3},{2,0},{3,1},{4,6},{5,7},{6,4},{7,5},{8,10},{9,11},{10,... | collective-permute-start | bytes 12296 | tf_op jit(solution)/shard_map/ppermute | solution.py:702
  10.2 10.1 %collective-permute-start.9 = (bf16[4,128,256]{2,1,0:T(8,128)(2,1)S(1)}, bf16[4,128,256]{2,1,0:T(8,128)(2,1)S(1)}, u32[]{:S(2)}, u32[]{:S(2)}) collective-permute-start(bf16[4,128,256]{2,1,0:T(8,128)(2,1)S(1)} %get-tuple-element.96), channel_id=1, source_target_pairs={{0,2},{1,3},{2,0},{3,1},{4,6},{5,7},{6,4},{7,5},{8,10},{9,11},{10,... | collective-permute-start | bytes 786440 | tf_op jit(solution)/shard_map/ppermute | solution.py:702
  12.1 3.1 %collective-permute-start.4 = (bf16[4,128,256]{2,1,0:T(8,128)(2,1)S(1)}, bf16[4,128,256]{2,1,0:T(8,128)(2,1)S(1)}, u32[]{:S(2)}, u32[]{:S(2)}) collective-permute-start(bf16[4,128,256]{2,1,0:T(8,128)(2,1)S(1)} %get-tuple-element.88), channel_id=1, source_target_pairs={{0,1},{1,0},{2,3},{3,2},{4,5},{5,4},{6,7},{7,6},{8,9},{9,8},{10,11... | collective-permute-start | bytes 786440 | tf_op jit(solution)/shard_map/ppermute | solution.py:702
  15.1 4.9 %collective-permute-start.8 = (bf16[4,128,256]{2,1,0:T(8,128)(2,1)S(1)}, bf16[4,128,256]{2,1,0:T(8,128)(2,1)S(1)}, u32[]{:S(2)}, u32[]{:S(2)}) collective-permute-start(bf16[4,128,256]{2,1,0:T(8,128)(2,1)S(1)} %get-tuple-element.95), channel_id=1, source_target_pairs={{0,1},{1,0},{2,3},{3,2},{4,5},{5,4},{6,7},{7,6},{8,9},{9,8},{10,11... | collective-permute-start | bytes 786440 | tf_op jit(solution)/shard_map/ppermute | solution.py:702
  15.5 8.0 %collective-permute-start.6 = (bf16[4,128,256]{2,1,0:T(8,128)(2,1)S(1)}, bf16[4,128,256]{2,1,0:T(8,128)(2,1)S(1)}, u32[]{:S(2)}, u32[]{:S(2)}) collective-permute-start(bf16[4,128,256]{2,1,0:T(8,128)(2,1)S(1)} %compose.7.refs_7_.rest_0_), channel_id=1, source_target_pairs={{0,2},{1,3},{2,0},{3,1},{4,6},{5,7},{6,4},{7,5},{8,10},{9,11},{10,... | collective-permute-start | bytes 786440 | tf_op jit(solution)/shard_map/ppermute | solution.py:702
  19.2 3.8 %collective-permute-start.5 = (bf16[4,128,256]{2,1,0:T(8,128)(2,1)S(1)}, bf16[4,128,256]{2,1,0:T(8,128)(2,1)S(1)}, u32[]{:S(2)}, u32[]{:S(2)}) collective-permute-start(bf16[4,128,256]{2,1,0:T(8,128)(2,1)S(1)} %get-tuple-element.92), channel_id=1, source_target_pairs={{0,1},{1,0},{2,3},{3,2},{4,5},{5,4},{6,7},{7,6},{8,9},{9,8},{10,11... | collective-permute-start | bytes 786440 | tf_op jit(solution)/shard_map/ppermute | solution.py:702
  20.5 7.2 %collective-permute-start.10 = (bf16[2,128,256]{2,1,0:T(8,128)(2,1)S(1)}, bf16[2,128,256]{2,1,0:T(8,128)(2,1)S(1)}, u32[]{:S(2)}, u32[]{:S(2)}) collective-permute-start(bf16[2,128,256]{2,1,0:T(8,128)(2,1)S(1)} %get-tuple-element.97), channel_id=1, source_target_pairs={{0,8},{4,12},{8,0},{12,4},{16,24},{20,28},{24,16},{28,20},{1,9},{5... | collective-permute-start | bytes 393224 | tf_op jit(solution)/shard_map/ppermute | solution.py:702
  21.9 7.6 %collective-permute-start.11 = (bf16[2,128,256]{2,1,0:T(8,128)(2,1)S(1)}, bf16[2,128,256]{2,1,0:T(8,128)(2,1)S(1)}, u32[]{:S(2)}, u32[]{:S(2)}) collective-permute-start(bf16[2,128,256]{2,1,0:T(8,128)(2,1)S(1)} %get-tuple-element.98), channel_id=1, source_target_pairs={{0,12},{4,8},{8,4},{12,0},{16,28},{20,24},{24,20},{28,16},{1,13},{... | collective-permute-start | bytes 393224 | tf_op jit(solution)/shard_map/ppermute | solution.py:702
  23.7 7.7 %collective-permute-start.7 = (bf16[2,128,256]{2,1,0:T(8,128)(2,1)S(1)}, bf16[2,128,256]{2,1,0:T(8,128)(2,1)S(1)}, u32[]{:S(2)}, u32[]{:S(2)}) collective-permute-start(bf16[2,128,256]{2,1,0:T(8,128)(2,1)S(1)} %get-tuple-element.94), channel_id=1, source_target_pairs={{0,4},{4,0},{8,12},{12,8},{16,20},{20,16},{24,28},{28,24},{1,5},{5... | collective-permute-start | bytes 393224 | tf_op jit(solution)/shard_map/ppermute | solution.py:702
  31.9 4.3 %collective-permute-start.12 = (bf16[2,128,128]{2,1,0:T(8,128)(2,1)S(1)}, bf16[2,128,128]{2,1,0:T(8,128)(2,1)S(1)}, u32[]{:S(2)}, u32[]{:S(2)}) collective-permute-start(bf16[2,128,128]{2,1,0:T(8,128)(2,1)S(1)} %get-tuple-element.105.refs_2_), channel_id=1, source_target_pairs={{0,16},{4,20},{8,24},{12,28},{16,0},{20,4},{24,8},{28,12},{1,17},{... | collective-permute-start | bytes 196616 | tf_op jit(solution)/shard_map/ppermute | solution.py:702
  36.4 3.7 %collective-permute-start.15 = (bf16[2,128,128]{2,1,0:T(8,128)(2,1)S(1)}, bf16[2,128,128]{2,1,0:T(8,128)(2,1)S(1)}, u32[]{:S(2)}, u32[]{:S(2)}) collective-permute-start(bf16[2,128,128]{2,1,0:T(8,128)(2,1)S(1)} %get-tuple-element.119), channel_id=1, source_target_pairs={{0,4},{4,0},{8,12},{12,8},{16,20},{20,16},{24,28},{28,24},{1,5},{5... | collective-permute-start | bytes 196616 | tf_op jit(solution)/shard_map/ppermute | solution.py:702
  38.0 8.8 %collective-permute-start.13 = (bf16[2,128,128]{2,1,0:T(8,128)(2,1)S(1)}, bf16[2,128,128]{2,1,0:T(8,128)(2,1)S(1)}, u32[]{:S(2)}, u32[]{:S(2)}) collective-permute-start(bf16[2,128,128]{2,1,0:T(8,128)(2,1)S(1)} %get-tuple-element.116), channel_id=1, source_target_pairs={{0,8},{4,12},{8,0},{12,4},{16,24},{20,28},{24,16},{28,20},{1,9},{5... | collective-permute-start | bytes 196616 | tf_op jit(solution)/shard_map/ppermute | solution.py:702
  40.2 6.6 %collective-permute-start.14 = (bf16[2,128,128]{2,1,0:T(8,128)(2,1)S(1)}, bf16[2,128,128]{2,1,0:T(8,128)(2,1)S(1)}, u32[]{:S(2)}, u32[]{:S(2)}) collective-permute-start(bf16[2,128,128]{2,1,0:T(8,128)(2,1)S(1)} %get-tuple-element.117), channel_id=1, source_target_pairs={{0,12},{4,8},{8,4},{12,0},{16,28},{20,24},{24,20},{28,16},{1,13},{... | collective-permute-start | bytes 196616 | tf_op jit(solution)/shard_map/ppermute | solution.py:702
  40.6 5.9 %collective-permute-start.16 = (bf16[4,128,128]{2,1,0:T(8,128)(2,1)S(1)}, bf16[4,128,128]{2,1,0:T(8,128)(2,1)S(1)}, u32[]{:S(2)}, u32[]{:S(2)}) collective-permute-start(bf16[4,128,128]{2,1,0:T(8,128)(2,1)S(1)} %get-tuple-element.120), channel_id=1, source_target_pairs={{0,1},{1,0},{2,3},{3,2},{4,5},{5,4},{6,7},{7,6},{8,9},{9,8},{10,11... | collective-permute-start | bytes 393224 | tf_op jit(solution)/shard_map/ppermute | solution.py:702
  43.9 6.7 %collective-permute-start.18 = (bf16[4,128,128]{2,1,0:T(8,128)(2,1)S(1)}, bf16[4,128,128]{2,1,0:T(8,128)(2,1)S(1)}, u32[]{:S(2)}, u32[]{:S(2)}) collective-permute-start(bf16[4,128,128]{2,1,0:T(8,128)(2,1)S(1)} %get-tuple-element.123), channel_id=1, source_target_pairs={{0,2},{1,3},{2,0},{3,1},{4,6},{5,7},{6,4},{7,5},{8,10},{9,11},{10,... | collective-permute-start | bytes 393224 | tf_op jit(solution)/shard_map/ppermute | solution.py:702
  47.2 5.2 %collective-permute-start.17 = (bf16[4,128,128]{2,1,0:T(8,128)(2,1)S(1)}, bf16[4,128,128]{2,1,0:T(8,128)(2,1)S(1)}, u32[]{:S(2)}, u32[]{:S(2)}) collective-permute-start(bf16[4,128,128]{2,1,0:T(8,128)(2,1)S(1)} %get-tuple-element.122), channel_id=1, source_target_pairs={{0,2},{1,3},{2,0},{3,1},{4,6},{5,7},{6,4},{7,5},{8,10},{9,11},{10,... | collective-permute-start | bytes 393224 | tf_op jit(solution)/shard_map/ppermute | solution.py:702
  47.9 1.6 %collective-permute-start.19 = (bf16[4,128,128]{2,1,0:T(8,128)(2,1)S(1)}, bf16[4,128,128]{2,1,0:T(8,128)(2,1)S(1)}, u32[]{:S(2)}, u32[]{:S(2)}) collective-permute-start(bf16[4,128,128]{2,1,0:T(8,128)(2,1)S(1)} %get-tuple-element.124), channel_id=1, source_target_pairs={{0,1},{1,0},{2,3},{3,2},{4,5},{5,4},{6,7},{7,6},{8,9},{9,8},{10,11... | collective-permute-start | bytes 393224 | tf_op jit(solution)/shard_map/ppermute | solution.py:702
  50.8 2.9 %collective-permute-start.21 = (bf16[4,128,128]{2,1,0:T(8,128)(2,1)S(1)}, bf16[4,128,128]{2,1,0:T(8,128)(2,1)S(1)}, u32[]{:S(2)}, u32[]{:S(2)}) collective-permute-start(bf16[4,128,128]{2,1,0:T(8,128)(2,1)S(1)} %get-tuple-element.133), channel_id=1, source_target_pairs={{0,1},{1,0},{2,3},{3,2},{4,5},{5,4},{6,7},{7,6},{8,9},{9,8},{10,11... | collective-permute-start | bytes 393224 | tf_op jit(solution)/shard_map/ppermute | solution.py:702
  52.6 2.4 %collective-permute-start.20 = (bf16[4,128,128]{2,1,0:T(8,128)(2,1)S(1)}, bf16[4,128,128]{2,1,0:T(8,128)(2,1)S(1)}, u32[]{:S(2)}, u32[]{:S(2)}) collective-permute-start(bf16[4,128,128]{2,1,0:T(8,128)(2,1)S(1)} %get-tuple-element.130), channel_id=1, source_target_pairs={{0,1},{1,0},{2,3},{3,2},{4,5},{5,4},{6,7},{7,6},{8,9},{9,8},{10,11... | collective-permute-start | bytes 393224 | tf_op jit(solution)/shard_map/ppermute | solution.py:702
  (7 other events, 10.0 us)

commit v6 on v5

--- a/solution.py
+++ b/solution.py
@@ -124,7 +124,7 @@
         in_specs=[whole_vmem()] * len(arrays),
         out_specs=(whole_vmem(),) * 2,
         compiler_params=params(),
-        cost_estimate=cost(),
+        cost_estimate=cost(False),
         name="gates",
     )(*arrays)
 
@@ -407,23 +407,23 @@
     return done if with_token else done[0]
 
 
-def split_kernel(bit, own_ref, got_ref, *rest):
+def split_kernel(bit, halves, own_ref, got_ref, *rest):
     later = is_later(bit)
     quarter = own_ref.shape[0] // 2
-    for number, out_ref in enumerate(rest[-2:]):
-        first = jnp.bitwise_xor(1 - number, quarter_parity()) * quarter
+    for number, out_ref in zip(halves, rest[-len(halves) :]):
+        first = jnp.bitwise_xor(number, quarter_parity()) * quarter
         for j in range(quarter):
             earlier_block, later_block = pick(later, own_ref[first + j], got_ref[first + j])
             out_ref[j] = joined(earlier_block, later_block).astype(BF16)
 
 
-def compose_split(bit, own, got, *after):
+def compose_split(bit, halves, own, got, *after):
     part = jax.ShapeDtypeStruct((own.shape[0] // 2,) + own.shape[1:], BF16)
     return pl.pallas_call(
-        functools.partial(split_kernel, bit),
-        out_shape=(part, part),
+        functools.partial(split_kernel, bit, halves),
+        out_shape=(part,) * len(halves),
         in_specs=[whole_vmem()] * (2 + len(after)),
-        out_specs=(whole_vmem(),) * 2,
+        out_specs=(whole_vmem(),) * len(halves),
         compiler_params=params(),
         cost_estimate=cost(),
         name="compose",
@@ -733,24 +733,23 @@
     tables = gates(far_parts, decay_rows, beta_rows, flags, [(array, 0) for array in far_biases])
     work(far_parts, 1, fetched, gap, tables)
     far, got, near, chip = {}, {}, {}, {}
-    first_done = ab[far_parts[-1], 1]
-    fetched_near = fetch(near_parts, half, size, None, *inputs, first_done)
     far[1], token = fold(
-        1 << under, 1, under, *far_biases, fetched_near[0], with_token=True, carried=len(far_biases)
+        1 << under, 1, under, *far_biases, with_token=True, carried=len(far_biases)
     )
     near_bias = swap(token, "head", 1 << under)
     got[1] = swap(far[1], "head", 1 << under)
     work(far_parts, 0, fetched, gap, tables, swap(token, "head", 1))
+    fetched_near = fetch(near_parts, half, size, None, *inputs, ab[far_parts[-1], 0])
     near_biases = [(near_bias, row) for row in range(len(near_parts))]
     near_tables = gates(near_parts, decay_rows, beta_rows, flags, near_biases, ab[far_parts[-1], 0])
-    work(near_parts, 1, fetched_near, gap, near_tables)
-    far[0] = fold(1 << under, 0, under)
+    early = swap(flags, "head", 1)
+    far[0] = fold(1 << under, 0, under, fetched_near[0])
     got[0] = swap(far[0], "head", 1 << under)
-    near[1] = fold(0, 1, under, far[0])
-    to_three, to_two = compose_split(head_bit[under], near[1], got[1])
+    work(near_parts, 1, fetched_near, gap, near_tables, far[0], early)
+    near[1] = fold(0, 1, under)
+    (to_three,) = compose_split(head_bit[under], (1,), near[1], got[1])
     from_three = swap(to_three, "context", 3)
-    from_two = swap(to_two, "context", 2)
-    work(near_parts, 0, fetched_near, gap, near_tables, ab[near_parts[-1], 1], far[0])
+    work(near_parts, 0, fetched_near, gap, near_tables, ab[near_parts[-1], 1], early)
 
     def look(part, *after):
         names, data, known = (
@@ -763,8 +762,10 @@
 
     every_part = far_parts + near_parts
     near[0] = fold(0, 0, under)
-    to_one, mine = compose_split(head_bit[under], near[0], got[0])
+    to_one, mine = compose_split(head_bit[under], (1, 0), near[0], got[0])
     from_one = swap(to_one, "context", 1)
+    (to_two,) = compose_split(head_bit[under], (0,), near[1], got[1], mine)
+    from_two = swap(to_two, "context", 2)
     for turn in (1, 0):
         levels[under][0, turn] = (near[turn], got[turn])
 

time: 56.3 us -> 55.1 us (0.979)
  waiting for transfers between devices: 5.6 us -> 4.73 us
  starting transfers between devices: 24.9 us -> 24.1 us
    ppermute x22 -> x23, waiting for transfers between devices: 5.6 us -> 4.73 us  [swap(): return lax.ppermute(array, axis, [(i, i ^ distance) for i in range(count)])]
    ppermute x22 -> x23, starting transfers between devices: 24.9 us -> 24.1 us  [swap(): return lax.ppermute(array, axis, [(i, i ^ distance) for i in range(count)])]
  transfers between devices with their start and end apart: 22 -> 23, of which waited for: 6 -> 7; matrix products, arithmetic and copies ran while one was open for 0% -> 0% of each run, Pallas kernels for 35% -> 36%
where the time goes in v6:
time: 55.1 us; the launch traced here: 55 us
  starting transfers between devices  24.1 us (44%)
  Pallas kernels  23.8 us (43%)
  waiting for transfers between devices  4.73 us (9%)
  local copies, waits for them, and re-layouts  1.79 us (3%)
    ppermute x23, starting transfers between devices, swap(): return lax.ppermute(array, axis, [(i, i ^ distance) for i in range(count)])  24.1 us
    pallas_call x4, Pallas kernels, local(): pl.pallas_call(functools.partial(local_kernel, units), out_shape=(result,...  7.69 us
    ppermute x23, waiting for transfers between devices, swap(): return lax.ppermute(array, axis, [(i, i ^ distance) for i in range(count)])  4.73 us
    pallas_call x8, Pallas kernels, finish(): pl.pallas_call(functools.partial(finish_kernel, unit, [earlier for _, ear...  4.58 us
    pallas_call x4, Pallas kernels, outlook(): pl.pallas_call(functools.partial(outlook_kernel, at, part), out_shape=(ja...  3.95 us
    pallas_call x2, Pallas kernels, fetch(): pl.pallas_call(functools.partial(fetch_kernel, parts, half, doc_start is...  3.44 us
    unnamed x18, local copies, waits for them, and re-layouts  1.79 us
    pallas_call x4, Pallas kernels, descend(): pl.pallas_call(functools.partial(descend_kernel, bits, len(sources) > 1,...  1.17 us
  transfers between devices with their start and end apart: 23, of which 7 were waited for; matrix products, arithmetic and copies ran while one was open for 0% of the time, Pallas kernels for 36%

profile of v6, /device:TPU:1, one launch (start us, length us, event | category | flops | bytes accessed | tf_op | source)
XLA Modules:
  0.0 55.0 jit_solution(6689482658547891730)
XLA Ops:
  0.7 2.4 %fetch.2 = (bf16[2,2,4,128,128]{4,3,2,1,0:T(8,128)(2,1)S(1)}, bf16[2,2,4,128,128]{4,3,2,1,0:T(8,128)(2,1)S(1)}, bf16[2,2,128,512]{3,2,1,0:T(8,128)(2,1)S(1)}, f32[128,128]{1,0:T(8,128)S(1)}, f32[3,8,128]{2,1,0:T(8,128)S(1)}) custom-call(s32[8]{0:T(128)S(1)} %copy-done.7, bf16[128,4096]{1,0:T(8,128)(2,1)} %refs_0_.3, bf16[128,4096]{1,0:T(8,128)(2,1)} %refs_1_.3), custom_call_target="tpu_custom_call" | custom-call | flops 10000000000 | bytes 100000000 | tf_op jit(solution)/shard_map/fetch/pallas_call | solution.py:196
  3.5 1.9 %local_tokens.4 = (bf16[4,128,256]{2,1,0:T(8,128)(2,1)S(1)}, bf16[4,128,256]{2,1,0:T(8,128)(2,1)S(1)}, bf16[4,128,256]{2,1,0:T(8,128)(2,1)S(1)}, bf16[4,128,256]{2,1,0:T(8,128)(2,1)S(1)}) custom-call(bf16[2,2,4,128,128]{4,3,2,1,0:T(8,128)(2,1)S(1)} %get-tuple-element.69.refs_0_, bf16[2,2,4,128,128]{4,3,2,1,0:T(8,128)(2,1)S(1)} %get-tuple-element.70.refs_1_.turned_ref, ...), custom_call_target="tpu_custom_call" | custom-call | flops 10000000000 | bytes 100000000 | tf_op jit(solution)/shard_map/local_tokens/pallas_call | solution.py:307
  5.9 1.2 %collective-permute-done.1.got_ref.refs_4_.rest_10_.refs_2_ = bf16[4,128,256]{2,1,0:T(8,128)(2,1)S(1)} collective-permute-done((bf16[4,128,256]{2,1,0:T(8,128)(2,1)S(1)}, bf16[4,128,256]{2,1,0:T(8,128)(2,1)S(1)}, u32[]{:S(2)}, u32[]{:S(2)}) %collective-permute-start.1) | collective-permute-done | bytes 262176 | tf_op jit(solution)/shard_map/ppermute | solution.py:702
  7.9 2.6 %collective-permute-start.3 = (f32[8,128]{1,0:T(8,128)S(1)}, f32[8,128]{1,0:T(8,128)S(1)}, u32[]{:S(2)}, u32[]{:S(2)}) collective-permute-start(f32[8,128]{1,0:T(8,128)S(1)} %get-tuple-element.78), channel_id=1, source_target_pairs={{0,2},{1,3},{2,0},{3,1},{4,6},{5,7},{6,4},{7,5},{8,10},{9,11},{10,... | collective-permute-start | bytes 12296 | tf_op jit(solution)/shard_map/ppermute | solution.py:702
  10.6 1.9 %local_tokens.5 = (bf16[4,128,256]{2,1,0:T(8,128)(2,1)S(1)}, bf16[4,128,256]{2,1,0:T(8,128)(2,1)S(1)}, bf16[4,128,256]{2,1,0:T(8,128)(2,1)S(1)}, bf16[4,128,256]{2,1,0:T(8,128)(2,1)S(1)}) custom-call(bf16[2,2,4,128,128]{4,3,2,1,0:T(8,128)(2,1)S(1)} %get-tuple-element.69.refs_0_, bf16[2,2,4,128,128]{4,3,2,1,0:T(8,128)(2,1)S(1)} %get-tuple-element.70.refs_1_.turned_ref, ...), custom_call_target="tpu_custom_call" | custom-call | flops 10000000000 | bytes 100000000 | tf_op jit(solution)/shard_map/local_tokens/pallas_call | solution.py:307
  13.0 1.1 %fetch.3 = (bf16[2,2,4,128,128]{4,3,2,1,0:T(8,128)(2,1)S(1)}, bf16[2,2,4,128,128]{4,3,2,1,0:T(8,128)(2,1)S(1)}, bf16[2,2,128,512]{3,2,1,0:T(8,128)(2,1)S(1)}) custom-call(bf16[128,4096]{1,0:T(8,128)(2,1)S(1)} %copy-done.3, bf16[128,4096]{1,0:T(8,128)(2,1)S(1)} %copy-done.4, ...), custom_call_target="tpu_custom_call" | custom-call | flops 10000000000 | bytes 100000000 | tf_op jit(solution)/shard_map/fetch/pallas_call | solution.py:196
  14.7 1.8 %collective-permute-start.7 = (bf16[4,128,256]{2,1,0:T(8,128)(2,1)S(1)}, bf16[4,128,256]{2,1,0:T(8,128)(2,1)S(1)}, u32[]{:S(2)}, u32[]{:S(2)}) collective-permute-start(bf16[4,128,256]{2,1,0:T(8,128)(2,1)S(1)} %compose.8.refs_6_), channel_id=1, source_target_pairs={{0,2},{1,3},{2,0},{3,1},{4,6},{5,7},{6,4},{7,5},{8,10},{9,11},{10,... | collective-permute-start | bytes 786440 | tf_op jit(solution)/shard_map/ppermute | solution.py:702
  16.5 1.9 %local_tokens.6 = (bf16[4,128,256]{2,1,0:T(8,128)(2,1)S(1)}, bf16[4,128,256]{2,1,0:T(8,128)(2,1)S(1)}, bf16[4,128,256]{2,1,0:T(8,128)(2,1)S(1)}, bf16[4,128,256]{2,1,0:T(8,128)(2,1)S(1)}) custom-call(bf16[2,2,4,128,128]{4,3,2,1,0:T(8,128)(2,1)S(1)} %get-tuple-element.83.rest_0_.refs_0_, ...), custom_call_target="tpu_custom_call" | custom-call | flops 10000000000 | bytes 100000000 | tf_op jit(solution)/shard_map/local_tokens/pallas_call | solution.py:307
  19.0 1.9 %local_tokens.7 = (bf16[4,128,256]{2,1,0:T(8,128)(2,1)S(1)}, bf16[4,128,256]{2,1,0:T(8,128)(2,1)S(1)}, bf16[4,128,256]{2,1,0:T(8,128)(2,1)S(1)}, bf16[4,128,256]{2,1,0:T(8,128)(2,1)S(1)}) custom-call(bf16[2,2,4,128,128]{4,3,2,1,0:T(8,128)(2,1)S(1)} %get-tuple-element.83.rest_0_.refs_0_, ...), custom_call_target="tpu_custom_call" | custom-call | flops 10000000000 | bytes 100000000 | tf_op jit(solution)/shard_map/local_tokens/pallas_call | solution.py:307
  21.4 2.3 %collective-permute-start.12 = (bf16[2,128,256]{2,1,0:T(8,128)(2,1)S(1)}, bf16[2,128,256]{2,1,0:T(8,128)(2,1)S(1)}, u32[]{:S(2)}, u32[]{:S(2)}) collective-permute-start(bf16[2,128,256]{2,1,0:T(8,128)(2,1)S(1)} %compose.13), channel_id=1, source_target_pairs={{0,12},{4,8},{8,4},{12,0},{16,28},{20,24},{24,20},{28,16},{1,13},{... | collective-permute-start | bytes 393224 | tf_op jit(solution)/shard_map/ppermute | solution.py:702
  24.4 1.0 %collective-permute-start.11 = (bf16[2,128,256]{2,1,0:T(8,128)(2,1)S(1)}, bf16[2,128,256]{2,1,0:T(8,128)(2,1)S(1)}, u32[]{:S(2)}, u32[]{:S(2)}) collective-permute-start(bf16[2,128,256]{2,1,0:T(8,128)(2,1)S(1)} %compose.12), channel_id=1, source_target_pairs={{0,8},{4,12},{8,0},{12,4},{16,24},{20,28},{24,16},{28,20},{1,9},{5... | collective-permute-start | bytes 393224 | tf_op jit(solution)/shard_map/ppermute | solution.py:702
  25.4 1.2 %collective-permute-start.8 = (bf16[2,128,256]{2,1,0:T(8,128)(2,1)S(1)}, bf16[2,128,256]{2,1,0:T(8,128)(2,1)S(1)}, u32[]{:S(2)}, u32[]{:S(2)}) collective-permute-start(bf16[2,128,256]{2,1,0:T(8,128)(2,1)S(1)} %get-tuple-element.92), channel_id=1, source_target_pairs={{0,4},{4,0},{8,12},{12,8},{16,20},{20,16},{24,28},{28,24},{1,5},{5... | collective-permute-start | bytes 393224 | tf_op jit(solution)/shard_map/ppermute | solution.py:702
  27.3 1.1 %outlook.5 = (bf16[4,128,256]{2,1,0:T(8,128)(2,1)S(1)}, bf16[4,128,256]{2,1,0:T(8,128)(2,1)S(1)}, f32[1,128]{1,0:T(1,128)}) custom-call(bf16[128,4096]{1,0:T(8,128)(2,1)S(1)} %copy-done.5, bf16[2,2,4,128,128]{4,3,2,1,0:T(8,128)(2,1)S(1)} %get-tuple-element.70.refs_1_.turned_ref, f32[128,128]{1,0:T(8,128)S(1)} %get-tuple-element.72.refs_3_.gap_ref, ...), custom_call_target="tpu_custom_call" | custom-call | flops 10000000000 | bytes 100000000 | tf_op jit(solution)/shard_map/outlook/pallas_call | solution.py:359
  28.3 1.1 %outlook.4 = (bf16[4,128,256]{2,1,0:T(8,128)(2,1)S(1)}, bf16[4,128,256]{2,1,0:T(8,128)(2,1)S(1)}, f32[1,128]{1,0:T(1,128)}) custom-call(bf16[128,4096]{1,0:T(8,128)(2,1)S(1)} %copy-done.5, bf16[2,2,4,128,128]{4,3,2,1,0:T(8,128)(2,1)S(1)} %get-tuple-element.70.refs_1_.turned_ref, f32[128,128]{1,0:T(8,128)S(1)} %get-tuple-element.72.refs_3_.gap_ref, ...), custom_call_target="tpu_custom_call" | custom-call | flops 10000000000 | bytes 100000000 | tf_op jit(solution)/shard_map/outlook/pallas_call | solution.py:359
  30.6 2.4 %collective-permute-start.13 = (bf16[2,128,128]{2,1,0:T(8,128)(2,1)S(1)}, bf16[2,128,128]{2,1,0:T(8,128)(2,1)S(1)}, u32[]{:S(2)}, u32[]{:S(2)}) collective-permute-start(bf16[2,128,128]{2,1,0:T(8,128)(2,1)S(1)} %get-tuple-element.101.refs_2_), channel_id=1, source_target_pairs={{0,16},{4,20},{8,24},{12,28},{16,0},{20,4},{24,8},{28,12},{1,17},{... | collective-permute-start | bytes 196616 | tf_op jit(solution)/shard_map/ppermute | solution.py:702
  32.9 1.1 %outlook.7 = (bf16[4,128,256]{2,1,0:T(8,128)(2,1)S(1)}, bf16[4,128,256]{2,1,0:T(8,128)(2,1)S(1)}, f32[1,128]{1,0:T(1,128)}) custom-call(bf16[128,4096]{1,0:T(8,128)(2,1)S(1)} %copy-done.5, bf16[2,2,4,128,128]{4,3,2,1,0:T(8,128)(2,1)S(1)} %get-tuple-element.80.refs_1_.turned_ref, f32[128,128]{1,0:T(8,128)S(1)} %get-tuple-element.72.refs_3_.gap_ref, ...), custom_call_target="tpu_custom_call" | custom-call | flops 10000000000 | bytes 100000000 | tf_op jit(solution)/shard_map/outlook/pallas_call | solution.py:359
  35.5 1.0 %collective-permute-start.16 = (bf16[2,128,128]{2,1,0:T(8,128)(2,1)S(1)}, bf16[2,128,128]{2,1,0:T(8,128)(2,1)S(1)}, u32[]{:S(2)}, u32[]{:S(2)}) collective-permute-start(bf16[2,128,128]{2,1,0:T(8,128)(2,1)S(1)} %get-tuple-element.115), channel_id=1, source_target_pairs={{0,4},{4,0},{8,12},{12,8},{16,20},{20,16},{24,28},{28,24},{1,5},{5... | collective-permute-start | bytes 196616 | tf_op jit(solution)/shard_map/ppermute | solution.py:702
  36.5 1.1 %collective-permute-start.14 = (bf16[2,128,128]{2,1,0:T(8,128)(2,1)S(1)}, bf16[2,128,128]{2,1,0:T(8,128)(2,1)S(1)}, u32[]{:S(2)}, u32[]{:S(2)}) collective-permute-start(bf16[2,128,128]{2,1,0:T(8,128)(2,1)S(1)} %get-tuple-element.112), channel_id=1, source_target_pairs={{0,8},{4,12},{8,0},{12,4},{16,24},{20,28},{24,16},{28,20},{1,9},{5... | collective-permute-start | bytes 196616 | tf_op jit(solution)/shard_map/ppermute | solution.py:702
  39.0 4.4 %collective-permute-start.17 = (bf16[4,128,128]{2,1,0:T(8,128)(2,1)S(1)}, bf16[4,128,128]{2,1,0:T(8,128)(2,1)S(1)}, u32[]{:S(2)}, u32[]{:S(2)}) collective-permute-start(bf16[4,128,128]{2,1,0:T(8,128)(2,1)S(1)} %get-tuple-element.116), channel_id=1, source_target_pairs={{0,1},{1,0},{2,3},{3,2},{4,5},{5,4},{6,7},{7,6},{8,9},{9,8},{10,11... | collective-permute-start | bytes 393224 | tf_op jit(solution)/shard_map/ppermute | solution.py:702
  47.0 1.0 %finish.11 = (bf16[128,4096]{1,0:T(8,128)(2,1)}, bf16[128,512]{1,0:T(8,128)(2,1)S(1)}) custom-call(f32[1,128]{1,0:T(1,128)S(1)} %get-tuple-element.102.gain_ref, bf16[4,128,128]{2,1,0:T(8,128)(2,1)S(1)} %collective-permute-done.20.state_ref, bf16[4,128,256]{2,1,0:T(8,128)(2,1)S(1)} %get-tuple-element.109.rest_6_.qo_ref, bf16[128,4096]{1,0:T(8,128)(2,1)S(1)} %copy-done.6, ...), custom_call_target="tpu_custom_call" | custom-call | flops 10000000000 | bytes 100000000 | tf_op jit(solution)/shard_map/finish/pallas_call | solution.py:668
  48.7 1.1 %collective-permute-start.22 = (bf16[4,128,128]{2,1,0:T(8,128)(2,1)S(1)}, bf16[4,128,128]{2,1,0:T(8,128)(2,1)S(1)}, u32[]{:S(2)}, u32[]{:S(2)}) collective-permute-start(bf16[4,128,128]{2,1,0:T(8,128)(2,1)S(1)} %get-tuple-element.129), channel_id=1, source_target_pairs={{0,1},{1,0},{2,3},{3,2},{4,5},{5,4},{6,7},{7,6},{8,9},{9,8},{10,11... | collective-permute-start | bytes 393224 | tf_op jit(solution)/shard_map/ppermute | solution.py:702
  50.2 1.4 %collective-permute-done.18.refs_0_ = bf16[4,128,128]{2,1,0:T(8,128)(2,1)S(1)} collective-permute-done((bf16[4,128,128]{2,1,0:T(8,128)(2,1)S(1)}, bf16[4,128,128]{2,1,0:T(8,128)(2,1)S(1)}, u32[]{:S(2)}, u32[]{:S(2)}) %collective-permute-start.18) | collective-permute-done | bytes 131104 | tf_op jit(solution)/shard_map/ppermute | solution.py:702
  52.8 1.0 %finish.14 = (bf16[128,4096]{1,0:T(8,128)(2,1)}, bf16[128,512]{1,0:T(8,128)(2,1)S(1)}) custom-call(f32[1,128]{1,0:T(1,128)S(1)} %get-tuple-element.102.gain_ref, bf16[4,128,128]{2,1,0:T(8,128)(2,1)S(1)} %get-tuple-element.127.state_ref, bf16[4,128,256]{2,1,0:T(8,128)(2,1)S(1)} %get-tuple-element.105.rest_4_.qo_ref, ...), custom_call_target="tpu_custom_call", output_to_operand_aliasing={{0}: (7, {})} | custom-call | flops 10000000000 | bytes 100000000 | tf_op jit(solution)/shard_map/finish/pallas_call | solution.py:668
  53.8 1.0 %finish.15 = bf16[128,4096]{1,0:T(8,128)(2,1)} custom-call(f32[1,128]{1,0:T(1,128)S(1)} %get-tuple-element.102.gain_ref, bf16[4,128,128]{2,1,0:T(8,128)(2,1)S(1)} %collective-permute-done.21.state_ref, bf16[4,128,256]{2,1,0:T(8,128)(2,1)S(1)} %get-tuple-element.104.rest_2_.qo_ref, bf16[128,4096]{1,0:T(8,128)(2,1)S(1)} %copy-done.6, ...), custom_call_target="tpu_custom_call", output_to_operand_aliasing={{}: (5, {})} | custom-call | flops 10000000000 | bytes 100000000 | tf_op jit(solution)/shard_map/finish/pallas_call | solution.py:668
  (73 shorter events, 15.6 us)
Async XLA Ops:
  0.7 2.4 %collective-permute-start = (f32[1,8]{1,0:T(1,128)S(1)}, f32[1,8]{1,0:T(1,128)S(1)}, u32[]{:S(2)}, u32[]{:S(2)}) collective-permute-start(f32[1,8]{1,0:T(1,128)S(1)} %bitcast.8), channel_id=1, source_target_pairs={{0,1},{1,0},{2,3},{3,2},{4,5},{5,4},{6,7},{7,6},{8,9},{9,8},{10,11... | collective-permute-start | bytes 104 | tf_op jit(solution)/shard_map/ppermute | solution.py:702
  5.4 1.7 %collective-permute-start.1 = (bf16[4,128,256]{2,1,0:T(8,128)(2,1)S(1)}, bf16[4,128,256]{2,1,0:T(8,128)(2,1)S(1)}, u32[]{:S(2)}, u32[]{:S(2)}) collective-permute-start(bf16[4,128,256]{2,1,0:T(8,128)(2,1)S(1)} %get-tuple-element.77), channel_id=1, source_target_pairs={{0,1},{1,0},{2,3},{3,2},{4,5},{5,4},{6,7},{7,6},{8,9},{9,8},{10,11... | collective-permute-start | bytes 786440 | tf_op jit(solution)/shard_map/ppermute | solution.py:702
  7.3 3.2 %collective-permute-start.2 = (f32[8,128]{1,0:T(8,128)S(1)}, f32[8,128]{1,0:T(8,128)S(1)}, u32[]{:S(2)}, u32[]{:S(2)}) collective-permute-start(f32[8,128]{1,0:T(8,128)S(1)} %get-tuple-element.78), channel_id=1, source_target_pairs={{0,1},{1,0},{2,3},{3,2},{4,5},{5,4},{6,7},{7,6},{8,9},{9,8},{10,11... | collective-permute-start | bytes 12296 | tf_op jit(solution)/shard_map/ppermute | solution.py:702
  7.8 8.7 %collective-permute-start.5 = (f32[3,8,128]{2,1,0:T(8,128)S(1)}, f32[3,8,128]{2,1,0:T(8,128)S(1)}, u32[]{:S(2)}, u32[]{:S(2)}) collective-permute-start(f32[3,8,128]{2,1,0:T(8,128)S(1)} %get-tuple-element.73.flag_ref), channel_id=1, source_target_pairs={{0,1},{1,0},{2,3},{3,2},{4,5},{5,4},{6,7},{7,6},{8,9},{9,8},{10,11... | collective-permute-start | bytes 36872 | tf_op jit(solution)/shard_map/ppermute | solution.py:702
  7.9 6.2 %collective-permute-start.3 = (f32[8,128]{1,0:T(8,128)S(1)}, f32[8,128]{1,0:T(8,128)S(1)}, u32[]{:S(2)}, u32[]{:S(2)}) collective-permute-start(f32[8,128]{1,0:T(8,128)S(1)} %get-tuple-element.78), channel_id=1, source_target_pairs={{0,2},{1,3},{2,0},{3,1},{4,6},{5,7},{6,4},{7,5},{8,10},{9,11},{10,... | collective-permute-start | bytes 12296 | tf_op jit(solution)/shard_map/ppermute | solution.py:702
  10.5 2.5 %copy-start.4 = (bf16[128,4096]{1,0:T(8,128)(2,1)S(1)}, bf16[128,4096]{1,0:T(8,128)(2,1)}, u32[]{:S(2)}) copy-start(bf16[128,4096]{1,0:T(8,128)(2,1)} %refs_1_.3) | copy-start | bytes 3145732
  10.5 10.7 %collective-permute-start.10 = (bf16[4,128,256]{2,1,0:T(8,128)(2,1)S(1)}, bf16[4,128,256]{2,1,0:T(8,128)(2,1)S(1)}, u32[]{:S(2)}, u32[]{:S(2)}) collective-permute-start(bf16[4,128,256]{2,1,0:T(8,128)(2,1)S(1)} %get-tuple-element.94), channel_id=1, source_target_pairs={{0,2},{1,3},{2,0},{3,1},{4,6},{5,7},{6,4},{7,5},{8,10},{9,11},{10,... | collective-permute-start | bytes 786440 | tf_op jit(solution)/shard_map/ppermute | solution.py:702
  12.5 2.0 %collective-permute-start.4 = (bf16[4,128,256]{2,1,0:T(8,128)(2,1)S(1)}, bf16[4,128,256]{2,1,0:T(8,128)(2,1)S(1)}, u32[]{:S(2)}, u32[]{:S(2)}) collective-permute-start(bf16[4,128,256]{2,1,0:T(8,128)(2,1)S(1)} %get-tuple-element.85), channel_id=1, source_target_pairs={{0,1},{1,0},{2,3},{3,2},{4,5},{5,4},{6,7},{7,6},{8,9},{9,8},{10,11... | collective-permute-start | bytes 786440 | tf_op jit(solution)/shard_map/ppermute | solution.py:702
  14.7 9.3 %collective-permute-start.7 = (bf16[4,128,256]{2,1,0:T(8,128)(2,1)S(1)}, bf16[4,128,256]{2,1,0:T(8,128)(2,1)S(1)}, u32[]{:S(2)}, u32[]{:S(2)}) collective-permute-start(bf16[4,128,256]{2,1,0:T(8,128)(2,1)S(1)} %compose.8.refs_6_), channel_id=1, source_target_pairs={{0,2},{1,3},{2,0},{3,1},{4,6},{5,7},{6,4},{7,5},{8,10},{9,11},{10,... | collective-permute-start | bytes 786440 | tf_op jit(solution)/shard_map/ppermute | solution.py:702
  18.4 2.6 %collective-permute-start.9 = (bf16[4,128,256]{2,1,0:T(8,128)(2,1)S(1)}, bf16[4,128,256]{2,1,0:T(8,128)(2,1)S(1)}, u32[]{:S(2)}, u32[]{:S(2)}) collective-permute-start(bf16[4,128,256]{2,1,0:T(8,128)(2,1)S(1)} %get-tuple-element.93), channel_id=1, source_target_pairs={{0,1},{1,0},{2,3},{3,2},{4,5},{5,4},{6,7},{7,6},{8,9},{9,8},{10,11... | collective-permute-start | bytes 786440 | tf_op jit(solution)/shard_map/ppermute | solution.py:702
  20.9 2.8 %collective-permute-start.6 = (bf16[4,128,256]{2,1,0:T(8,128)(2,1)S(1)}, bf16[4,128,256]{2,1,0:T(8,128)(2,1)S(1)}, u32[]{:S(2)}, u32[]{:S(2)}) collective-permute-start(bf16[4,128,256]{2,1,0:T(8,128)(2,1)S(1)} %get-tuple-element.90), channel_id=1, source_target_pairs={{0,1},{1,0},{2,3},{3,2},{4,5},{5,4},{6,7},{7,6},{8,9},{9,8},{10,11... | collective-permute-start | bytes 786440 | tf_op jit(solution)/shard_map/ppermute | solution.py:702
  21.4 8.0 %collective-permute-start.12 = (bf16[2,128,256]{2,1,0:T(8,128)(2,1)S(1)}, bf16[2,128,256]{2,1,0:T(8,128)(2,1)S(1)}, u32[]{:S(2)}, u32[]{:S(2)}) collective-permute-start(bf16[2,128,256]{2,1,0:T(8,128)(2,1)S(1)} %compose.13), channel_id=1, source_target_pairs={{0,12},{4,8},{8,4},{12,0},{16,28},{20,24},{24,20},{28,16},{1,13},{... | collective-permute-start | bytes 393224 | tf_op jit(solution)/shard_map/ppermute | solution.py:702
  24.4 5.6 %collective-permute-start.11 = (bf16[2,128,256]{2,1,0:T(8,128)(2,1)S(1)}, bf16[2,128,256]{2,1,0:T(8,128)(2,1)S(1)}, u32[]{:S(2)}, u32[]{:S(2)}) collective-permute-start(bf16[2,128,256]{2,1,0:T(8,128)(2,1)S(1)} %compose.12), channel_id=1, source_target_pairs={{0,8},{4,12},{8,0},{12,4},{16,24},{20,28},{24,16},{28,20},{1,9},{5... | collective-permute-start | bytes 393224 | tf_op jit(solution)/shard_map/ppermute | solution.py:702
  25.4 4.6 %collective-permute-start.8 = (bf16[2,128,256]{2,1,0:T(8,128)(2,1)S(1)}, bf16[2,128,256]{2,1,0:T(8,128)(2,1)S(1)}, u32[]{:S(2)}, u32[]{:S(2)}) collective-permute-start(bf16[2,128,256]{2,1,0:T(8,128)(2,1)S(1)} %get-tuple-element.92), channel_id=1, source_target_pairs={{0,4},{4,0},{8,12},{12,8},{16,20},{20,16},{24,28},{28,24},{1,5},{5... | collective-permute-start | bytes 393224 | tf_op jit(solution)/shard_map/ppermute | solution.py:702
  30.6 4.2 %collective-permute-start.13 = (bf16[2,128,128]{2,1,0:T(8,128)(2,1)S(1)}, bf16[2,128,128]{2,1,0:T(8,128)(2,1)S(1)}, u32[]{:S(2)}, u32[]{:S(2)}) collective-permute-start(bf16[2,128,128]{2,1,0:T(8,128)(2,1)S(1)} %get-tuple-element.101.refs_2_), channel_id=1, source_target_pairs={{0,16},{4,20},{8,24},{12,28},{16,0},{20,4},{24,8},{28,12},{1,17},{... | collective-permute-start | bytes 196616 | tf_op jit(solution)/shard_map/ppermute | solution.py:702
  35.5 3.2 %collective-permute-start.16 = (bf16[2,128,128]{2,1,0:T(8,128)(2,1)S(1)}, bf16[2,128,128]{2,1,0:T(8,128)(2,1)S(1)}, u32[]{:S(2)}, u32[]{:S(2)}) collective-permute-start(bf16[2,128,128]{2,1,0:T(8,128)(2,1)S(1)} %get-tuple-element.115), channel_id=1, source_target_pairs={{0,4},{4,0},{8,12},{12,8},{16,20},{20,16},{24,28},{28,24},{1,5},{5... | collective-permute-start | bytes 196616 | tf_op jit(solution)/shard_map/ppermute | solution.py:702
  36.5 8.3 %collective-permute-start.14 = (bf16[2,128,128]{2,1,0:T(8,128)(2,1)S(1)}, bf16[2,128,128]{2,1,0:T(8,128)(2,1)S(1)}, u32[]{:S(2)}, u32[]{:S(2)}) collective-permute-start(bf16[2,128,128]{2,1,0:T(8,128)(2,1)S(1)} %get-tuple-element.112), channel_id=1, source_target_pairs={{0,8},{4,12},{8,0},{12,4},{16,24},{20,28},{24,16},{28,20},{1,9},{5... | collective-permute-start | bytes 196616 | tf_op jit(solution)/shard_map/ppermute | solution.py:702
  37.6 7.2 %collective-permute-start.15 = (bf16[2,128,128]{2,1,0:T(8,128)(2,1)S(1)}, bf16[2,128,128]{2,1,0:T(8,128)(2,1)S(1)}, u32[]{:S(2)}, u32[]{:S(2)}) collective-permute-start(bf16[2,128,128]{2,1,0:T(8,128)(2,1)S(1)} %get-tuple-element.113), channel_id=1, source_target_pairs={{0,12},{4,8},{8,4},{12,0},{16,28},{20,24},{24,20},{28,16},{1,13},{... | collective-permute-start | bytes 196616 | tf_op jit(solution)/shard_map/ppermute | solution.py:702
  39.0 5.4 %collective-permute-start.17 = (bf16[4,128,128]{2,1,0:T(8,128)(2,1)S(1)}, bf16[4,128,128]{2,1,0:T(8,128)(2,1)S(1)}, u32[]{:S(2)}, u32[]{:S(2)}) collective-permute-start(bf16[4,128,128]{2,1,0:T(8,128)(2,1)S(1)} %get-tuple-element.116), channel_id=1, source_target_pairs={{0,1},{1,0},{2,3},{3,2},{4,5},{5,4},{6,7},{7,6},{8,9},{9,8},{10,11... | collective-permute-start | bytes 393224 | tf_op jit(solution)/shard_map/ppermute | solution.py:702
  43.5 5.1 %collective-permute-start.19 = (bf16[4,128,128]{2,1,0:T(8,128)(2,1)S(1)}, bf16[4,128,128]{2,1,0:T(8,128)(2,1)S(1)}, u32[]{:S(2)}, u32[]{:S(2)}) collective-permute-start(bf16[4,128,128]{2,1,0:T(8,128)(2,1)S(1)} %get-tuple-element.119), channel_id=1, source_target_pairs={{0,2},{1,3},{2,0},{3,1},{4,6},{5,7},{6,4},{7,5},{8,10},{9,11},{10,... | collective-permute-start | bytes 393224 | tf_op jit(solution)/shard_map/ppermute | solution.py:702
  45.2 1.8 %collective-permute-start.20 = (bf16[4,128,128]{2,1,0:T(8,128)(2,1)S(1)}, bf16[4,128,128]{2,1,0:T(8,128)(2,1)S(1)}, u32[]{:S(2)}, u32[]{:S(2)}) collective-permute-start(bf16[4,128,128]{2,1,0:T(8,128)(2,1)S(1)} %get-tuple-element.120), channel_id=1, source_target_pairs={{0,1},{1,0},{2,3},{3,2},{4,5},{5,4},{6,7},{7,6},{8,9},{9,8},{10,11... | collective-permute-start | bytes 393224 | tf_op jit(solution)/shard_map/ppermute | solution.py:702
  46.0 5.6 %collective-permute-start.18 = (bf16[4,128,128]{2,1,0:T(8,128)(2,1)S(1)}, bf16[4,128,128]{2,1,0:T(8,128)(2,1)S(1)}, u32[]{:S(2)}, u32[]{:S(2)}) collective-permute-start(bf16[4,128,128]{2,1,0:T(8,128)(2,1)S(1)} %get-tuple-element.118), channel_id=1, source_target_pairs={{0,2},{1,3},{2,0},{3,1},{4,6},{5,7},{6,4},{7,5},{8,10},{9,11},{10,... | collective-permute-start | bytes 393224 | tf_op jit(solution)/shard_map/ppermute | solution.py:702
  48.7 3.7 %collective-permute-start.22 = (bf16[4,128,128]{2,1,0:T(8,128)(2,1)S(1)}, bf16[4,128,128]{2,1,0:T(8,128)(2,1)S(1)}, u32[]{:S(2)}, u32[]{:S(2)}) collective-permute-start(bf16[4,128,128]{2,1,0:T(8,128)(2,1)S(1)} %get-tuple-element.129), channel_id=1, source_target_pairs={{0,1},{1,0},{2,3},{3,2},{4,5},{5,4},{6,7},{7,6},{8,9},{9,8},{10,11... | collective-permute-start | bytes 393224 | tf_op jit(solution)/shard_map/ppermute | solution.py:702
  51.8 2.1 %collective-permute-start.21 = (bf16[4,128,128]{2,1,0:T(8,128)(2,1)S(1)}, bf16[4,128,128]{2,1,0:T(8,128)(2,1)S(1)}, u32[]{:S(2)}, u32[]{:S(2)}) collective-permute-start(bf16[4,128,128]{2,1,0:T(8,128)(2,1)S(1)} %get-tuple-element.126), channel_id=1, source_target_pairs={{0,1},{1,0},{2,3},{3,2},{4,5},{5,4},{6,7},{7,6},{8,9},{9,8},{10,11... | collective-permute-start | bytes 393224 | tf_op jit(solution)/shard_map/ppermute | solution.py:702
  (8 other events, 13.0 us)

commit v7 on v6

--- a/solution.py
+++ b/solution.py
@@ -817,13 +817,14 @@
         (0, 1, head_bits, (from_far[2], from_far[3])),
     ]
 
-    def pass_on(part, turn, below, sources):
+    def pass_on(part, turn, below, sources, *after):
         down = list(reversed(range(below)))
         outs = descend(
             [head_bit[bit] for bit in down],
             sources,
             [levels[bit][part, turn] for bit in down],
             strips[-1][0] if strips else None,
+            *after,
         )
         states[part, turn] = outs[below]
         if strips:
@@ -841,12 +842,13 @@
     while inner:
         inner.sort(key=lambda entry: (-entry[2], entry[1]))
         part, turn, below, sources = inner.pop(0)
-        if below < depth or turn and below == head_bits:
+        if below < depth:
             write_leaves(leaves)
             leaves.clear()
             depth = below
         known = len(leaves)
-        pass_on(part, turn, below, sources)
+        ahead = [leaves[0][3][0]] if turn and below == head_bits else []
+        pass_on(part, turn, below, sources, *ahead)
         if not inner:
             write_leaves(leaves[:known])
             del leaves[:known]

time: 55.1 us -> 55.1 us (level)
  transfers between devices with their start and end apart: 23 -> 23, of which waited for: 7 -> 6; matrix products, arithmetic and copies ran while one was open for 0% -> 0% of each run, Pallas kernels for 36% -> 36%
where the time goes in v7:
time: 55.1 us; the launch traced here: 55 us
  starting transfers between devices  24.4 us (44%)
  Pallas kernels  23.8 us (43%)
  waiting for transfers between devices  4.47 us (8%)
  local copies, waits for them, and re-layouts  1.79 us (3%)
    ppermute x23, starting transfers between devices, swap(): return lax.ppermute(array, axis, [(i, i ^ distance) for i in range(count)])  24.4 us
    pallas_call x4, Pallas kernels, local(): pl.pallas_call(functools.partial(local_kernel, units), out_shape=(result,...  7.69 us
    pallas_call x8, Pallas kernels, finish(): pl.pallas_call(functools.partial(finish_kernel, unit, [earlier for _, ear...  4.57 us
    ppermute x23, waiting for transfers between devices, swap(): return lax.ppermute(array, axis, [(i, i ^ distance) for i in range(count)])  4.47 us
    pallas_call x4, Pallas kernels, outlook(): pl.pallas_call(functools.partial(outlook_kernel, at, part), out_shape=(ja...  3.94 us
    pallas_call x2, Pallas kernels, fetch(): pl.pallas_call(functools.partial(fetch_kernel, parts, half, doc_start is...  3.44 us
    unnamed x18, local copies, waits for them, and re-layouts  1.79 us
    pallas_call x4, Pallas kernels, descend(): pl.pallas_call(functools.partial(descend_kernel, bits, len(sources) > 1,...  1.16 us
  transfers between devices with their start and end apart: 23, of which 6 were waited for; matrix products, arithmetic and copies ran while one was open for 0% of the time, Pallas kernels for 36%

profile of v7, /device:TPU:1, one launch (start us, length us, event | category | flops | bytes accessed | tf_op | source)
XLA Modules:
  0.0 55.0 jit_solution(18130050756588534728)
XLA Ops:
  0.7 2.4 %fetch.2 = (bf16[2,2,4,128,128]{4,3,2,1,0:T(8,128)(2,1)S(1)}, bf16[2,2,4,128,128]{4,3,2,1,0:T(8,128)(2,1)S(1)}, bf16[2,2,128,512]{3,2,1,0:T(8,128)(2,1)S(1)}, f32[128,128]{1,0:T(8,128)S(1)}, f32[3,8,128]{2,1,0:T(8,128)S(1)}) custom-call(s32[8]{0:T(128)S(1)} %copy-done.7, bf16[128,4096]{1,0:T(8,128)(2,1)} %refs_0_.3, bf16[128,4096]{1,0:T(8,128)(2,1)} %refs_1_.3), custom_call_target="tpu_custom_call" | custom-call | flops 10000000000 | bytes 100000000 | tf_op jit(solution)/shard_map/fetch/pallas_call | solution.py:196
  3.5 1.9 %local_tokens.4 = (bf16[4,128,256]{2,1,0:T(8,128)(2,1)S(1)}, bf16[4,128,256]{2,1,0:T(8,128)(2,1)S(1)}, bf16[4,128,256]{2,1,0:T(8,128)(2,1)S(1)}, bf16[4,128,256]{2,1,0:T(8,128)(2,1)S(1)}) custom-call(bf16[2,2,4,128,128]{4,3,2,1,0:T(8,128)(2,1)S(1)} %get-tuple-element.69.refs_0_, bf16[2,2,4,128,128]{4,3,2,1,0:T(8,128)(2,1)S(1)} %get-tuple-element.70.refs_1_.turned_ref, ...), custom_call_target="tpu_custom_call" | custom-call | flops 10000000000 | bytes 100000000 | tf_op jit(solution)/shard_map/local_tokens/pallas_call | solution.py:307
  5.9 1.2 %collective-permute-done.1.got_ref.refs_4_.rest_10_.refs_2_ = bf16[4,128,256]{2,1,0:T(8,128)(2,1)S(1)} collective-permute-done((bf16[4,128,256]{2,1,0:T(8,128)(2,1)S(1)}, bf16[4,128,256]{2,1,0:T(8,128)(2,1)S(1)}, u32[]{:S(2)}, u32[]{:S(2)}) %collective-permute-start.1) | collective-permute-done | bytes 262176 | tf_op jit(solution)/shard_map/ppermute | solution.py:702
  7.9 2.6 %collective-permute-start.3 = (f32[8,128]{1,0:T(8,128)S(1)}, f32[8,128]{1,0:T(8,128)S(1)}, u32[]{:S(2)}, u32[]{:S(2)}) collective-permute-start(f32[8,128]{1,0:T(8,128)S(1)} %get-tuple-element.78), channel_id=1, source_target_pairs={{0,2},{1,3},{2,0},{3,1},{4,6},{5,7},{6,4},{7,5},{8,10},{9,11},{10,... | collective-permute-start | bytes 12296 | tf_op jit(solution)/shard_map/ppermute | solution.py:702
  10.6 1.9 %local_tokens.5 = (bf16[4,128,256]{2,1,0:T(8,128)(2,1)S(1)}, bf16[4,128,256]{2,1,0:T(8,128)(2,1)S(1)}, bf16[4,128,256]{2,1,0:T(8,128)(2,1)S(1)}, bf16[4,128,256]{2,1,0:T(8,128)(2,1)S(1)}) custom-call(bf16[2,2,4,128,128]{4,3,2,1,0:T(8,128)(2,1)S(1)} %get-tuple-element.69.refs_0_, bf16[2,2,4,128,128]{4,3,2,1,0:T(8,128)(2,1)S(1)} %get-tuple-element.70.refs_1_.turned_ref, ...), custom_call_target="tpu_custom_call" | custom-call | flops 10000000000 | bytes 100000000 | tf_op jit(solution)/shard_map/local_tokens/pallas_call | solution.py:307
  13.0 1.1 %fetch.3 = (bf16[2,2,4,128,128]{4,3,2,1,0:T(8,128)(2,1)S(1)}, bf16[2,2,4,128,128]{4,3,2,1,0:T(8,128)(2,1)S(1)}, bf16[2,2,128,512]{3,2,1,0:T(8,128)(2,1)S(1)}) custom-call(bf16[128,4096]{1,0:T(8,128)(2,1)S(1)} %copy-done.3, bf16[128,4096]{1,0:T(8,128)(2,1)S(1)} %copy-done.4, ...), custom_call_target="tpu_custom_call" | custom-call | flops 10000000000 | bytes 100000000 | tf_op jit(solution)/shard_map/fetch/pallas_call | solution.py:196
  14.7 1.8 %collective-permute-start.7 = (bf16[4,128,256]{2,1,0:T(8,128)(2,1)S(1)}, bf16[4,128,256]{2,1,0:T(8,128)(2,1)S(1)}, u32[]{:S(2)}, u32[]{:S(2)}) collective-permute-start(bf16[4,128,256]{2,1,0:T(8,128)(2,1)S(1)} %compose.8.refs_6_), channel_id=1, source_target_pairs={{0,2},{1,3},{2,0},{3,1},{4,6},{5,7},{6,4},{7,5},{8,10},{9,11},{10,... | collective-permute-start | bytes 786440 | tf_op jit(solution)/shard_map/ppermute | solution.py:702
  16.5 1.9 %local_tokens.6 = (bf16[4,128,256]{2,1,0:T(8,128)(2,1)S(1)}, bf16[4,128,256]{2,1,0:T(8,128)(2,1)S(1)}, bf16[4,128,256]{2,1,0:T(8,128)(2,1)S(1)}, bf16[4,128,256]{2,1,0:T(8,128)(2,1)S(1)}) custom-call(bf16[2,2,4,128,128]{4,3,2,1,0:T(8,128)(2,1)S(1)} %get-tuple-element.83.rest_0_.refs_0_, ...), custom_call_target="tpu_custom_call" | custom-call | flops 10000000000 | bytes 100000000 | tf_op jit(solution)/shard_map/local_tokens/pallas_call | solution.py:307
  19.0 1.9 %local_tokens.7 = (bf16[4,128,256]{2,1,0:T(8,128)(2,1)S(1)}, bf16[4,128,256]{2,1,0:T(8,128)(2,1)S(1)}, bf16[4,128,256]{2,1,0:T(8,128)(2,1)S(1)}, bf16[4,128,256]{2,1,0:T(8,128)(2,1)S(1)}) custom-call(bf16[2,2,4,128,128]{4,3,2,1,0:T(8,128)(2,1)S(1)} %get-tuple-element.83.rest_0_.refs_0_, ...), custom_call_target="tpu_custom_call" | custom-call | flops 10000000000 | bytes 100000000 | tf_op jit(solution)/shard_map/local_tokens/pallas_call | solution.py:307
  21.4 2.3 %collective-permute-start.12 = (bf16[2,128,256]{2,1,0:T(8,128)(2,1)S(1)}, bf16[2,128,256]{2,1,0:T(8,128)(2,1)S(1)}, u32[]{:S(2)}, u32[]{:S(2)}) collective-permute-start(bf16[2,128,256]{2,1,0:T(8,128)(2,1)S(1)} %compose.13), channel_id=1, source_target_pairs={{0,12},{4,8},{8,4},{12,0},{16,28},{20,24},{24,20},{28,16},{1,13},{... | collective-permute-start | bytes 393224 | tf_op jit(solution)/shard_map/ppermute | solution.py:702
  25.4 1.2 %collective-permute-start.8 = (bf16[2,128,256]{2,1,0:T(8,128)(2,1)S(1)}, bf16[2,128,256]{2,1,0:T(8,128)(2,1)S(1)}, u32[]{:S(2)}, u32[]{:S(2)}) collective-permute-start(bf16[2,128,256]{2,1,0:T(8,128)(2,1)S(1)} %get-tuple-element.92), channel_id=1, source_target_pairs={{0,4},{4,0},{8,12},{12,8},{16,20},{20,16},{24,28},{28,24},{1,5},{5... | collective-permute-start | bytes 393224 | tf_op jit(solution)/shard_map/ppermute | solution.py:702
  27.3 1.1 %outlook.5 = (bf16[4,128,256]{2,1,0:T(8,128)(2,1)S(1)}, bf16[4,128,256]{2,1,0:T(8,128)(2,1)S(1)}, f32[1,128]{1,0:T(1,128)}) custom-call(bf16[128,4096]{1,0:T(8,128)(2,1)S(1)} %copy-done.5, bf16[2,2,4,128,128]{4,3,2,1,0:T(8,128)(2,1)S(1)} %get-tuple-element.70.refs_1_.turned_ref, f32[128,128]{1,0:T(8,128)S(1)} %get-tuple-element.72.refs_3_.gap_ref, ...), custom_call_target="tpu_custom_call" | custom-call | flops 10000000000 | bytes 100000000 | tf_op jit(solution)/shard_map/outlook/pallas_call | solution.py:359
  28.3 1.1 %outlook.4 = (bf16[4,128,256]{2,1,0:T(8,128)(2,1)S(1)}, bf16[4,128,256]{2,1,0:T(8,128)(2,1)S(1)}, f32[1,128]{1,0:T(1,128)}) custom-call(bf16[128,4096]{1,0:T(8,128)(2,1)S(1)} %copy-done.5, bf16[2,2,4,128,128]{4,3,2,1,0:T(8,128)(2,1)S(1)} %get-tuple-element.70.refs_1_.turned_ref, f32[128,128]{1,0:T(8,128)S(1)} %get-tuple-element.72.refs_3_.gap_ref, ...), custom_call_target="tpu_custom_call" | custom-call | flops 10000000000 | bytes 100000000 | tf_op jit(solution)/shard_map/outlook/pallas_call | solution.py:359
  30.6 2.4 %collective-permute-start.13 = (bf16[2,128,128]{2,1,0:T(8,128)(2,1)S(1)}, bf16[2,128,128]{2,1,0:T(8,128)(2,1)S(1)}, u32[]{:S(2)}, u32[]{:S(2)}) collective-permute-start(bf16[2,128,128]{2,1,0:T(8,128)(2,1)S(1)} %get-tuple-element.101.refs_2_), channel_id=1, source_target_pairs={{0,16},{4,20},{8,24},{12,28},{16,0},{20,4},{24,8},{28,12},{1,17},{... | collective-permute-start | bytes 196616 | tf_op jit(solution)/shard_map/ppermute | solution.py:702
  32.9 1.1 %outlook.7 = (bf16[4,128,256]{2,1,0:T(8,128)(2,1)S(1)}, bf16[4,128,256]{2,1,0:T(8,128)(2,1)S(1)}, f32[1,128]{1,0:T(1,128)}) custom-call(bf16[128,4096]{1,0:T(8,128)(2,1)S(1)} %copy-done.5, bf16[2,2,4,128,128]{4,3,2,1,0:T(8,128)(2,1)S(1)} %get-tuple-element.80.refs_1_.turned_ref, f32[128,128]{1,0:T(8,128)S(1)} %get-tuple-element.72.refs_3_.gap_ref, ...), custom_call_target="tpu_custom_call" | custom-call | flops 10000000000 | bytes 100000000 | tf_op jit(solution)/shard_map/outlook/pallas_call | solution.py:359
  35.5 1.0 %collective-permute-start.16 = (bf16[2,128,128]{2,1,0:T(8,128)(2,1)S(1)}, bf16[2,128,128]{2,1,0:T(8,128)(2,1)S(1)}, u32[]{:S(2)}, u32[]{:S(2)}) collective-permute-start(bf16[2,128,128]{2,1,0:T(8,128)(2,1)S(1)} %get-tuple-element.115), channel_id=1, source_target_pairs={{0,4},{4,0},{8,12},{12,8},{16,20},{20,16},{24,28},{28,24},{1,5},{5... | collective-permute-start | bytes 196616 | tf_op jit(solution)/shard_map/ppermute | solution.py:702
  36.5 1.1 %collective-permute-start.14 = (bf16[2,128,128]{2,1,0:T(8,128)(2,1)S(1)}, bf16[2,128,128]{2,1,0:T(8,128)(2,1)S(1)}, u32[]{:S(2)}, u32[]{:S(2)}) collective-permute-start(bf16[2,128,128]{2,1,0:T(8,128)(2,1)S(1)} %get-tuple-element.112), channel_id=1, source_target_pairs={{0,8},{4,12},{8,0},{12,4},{16,24},{20,28},{24,16},{28,20},{1,9},{5... | collective-permute-start | bytes 196616 | tf_op jit(solution)/shard_map/ppermute | solution.py:702
  39.0 4.4 %collective-permute-start.17 = (bf16[4,128,128]{2,1,0:T(8,128)(2,1)S(1)}, bf16[4,128,128]{2,1,0:T(8,128)(2,1)S(1)}, u32[]{:S(2)}, u32[]{:S(2)}) collective-permute-start(bf16[4,128,128]{2,1,0:T(8,128)(2,1)S(1)} %get-tuple-element.117), channel_id=1, source_target_pairs={{0,1},{1,0},{2,3},{3,2},{4,5},{5,4},{6,7},{7,6},{8,9},{9,8},{10,11... | collective-permute-start | bytes 393224 | tf_op jit(solution)/shard_map/ppermute | solution.py:702
  44.8 1.2 %collective-permute-start.20 = (bf16[4,128,128]{2,1,0:T(8,128)(2,1)S(1)}, bf16[4,128,128]{2,1,0:T(8,128)(2,1)S(1)}, u32[]{:S(2)}, u32[]{:S(2)}) collective-permute-start(bf16[4,128,128]{2,1,0:T(8,128)(2,1)S(1)} %get-tuple-element.120), channel_id=1, source_target_pairs={{0,1},{1,0},{2,3},{3,2},{4,5},{5,4},{6,7},{7,6},{8,9},{9,8},{10,11... | collective-permute-start | bytes 393224 | tf_op jit(solution)/shard_map/ppermute | solution.py:702
  47.0 1.0 %finish.11 = (bf16[128,4096]{1,0:T(8,128)(2,1)}, bf16[128,512]{1,0:T(8,128)(2,1)S(1)}) custom-call(f32[1,128]{1,0:T(1,128)S(1)} %get-tuple-element.102.gain_ref, bf16[4,128,128]{2,1,0:T(8,128)(2,1)S(1)} %collective-permute-done.20.state_ref, bf16[4,128,256]{2,1,0:T(8,128)(2,1)S(1)} %get-tuple-element.109.rest_6_.qo_ref, bf16[128,4096]{1,0:T(8,128)(2,1)S(1)} %copy-done.6, ...), custom_call_target="tpu_custom_call" | custom-call | flops 10000000000 | bytes 100000000 | tf_op jit(solution)/shard_map/finish/pallas_call | solution.py:668
  48.7 1.1 %collective-permute-start.22 = (bf16[4,128,128]{2,1,0:T(8,128)(2,1)S(1)}, bf16[4,128,128]{2,1,0:T(8,128)(2,1)S(1)}, u32[]{:S(2)}, u32[]{:S(2)}) collective-permute-start(bf16[4,128,128]{2,1,0:T(8,128)(2,1)S(1)} %get-tuple-element.129), channel_id=1, source_target_pairs={{0,1},{1,0},{2,3},{3,2},{4,5},{5,4},{6,7},{7,6},{8,9},{9,8},{10,11... | collective-permute-start | bytes 393224 | tf_op jit(solution)/shard_map/ppermute | solution.py:702
  50.2 1.4 %collective-permute-done.18.refs_0_ = bf16[4,128,128]{2,1,0:T(8,128)(2,1)S(1)} collective-permute-done((bf16[4,128,128]{2,1,0:T(8,128)(2,1)S(1)}, bf16[4,128,128]{2,1,0:T(8,128)(2,1)S(1)}, u32[]{:S(2)}, u32[]{:S(2)}) %collective-permute-start.18) | collective-permute-done | bytes 131104 | tf_op jit(solution)/shard_map/ppermute | solution.py:702
  52.8 1.0 %finish.14 = (bf16[128,4096]{1,0:T(8,128)(2,1)}, bf16[128,512]{1,0:T(8,128)(2,1)S(1)}) custom-call(f32[1,128]{1,0:T(1,128)S(1)} %get-tuple-element.102.gain_ref, bf16[4,128,128]{2,1,0:T(8,128)(2,1)S(1)} %get-tuple-element.127.state_ref, bf16[4,128,256]{2,1,0:T(8,128)(2,1)S(1)} %get-tuple-element.105.rest_4_.qo_ref, ...), custom_call_target="tpu_custom_call", output_to_operand_aliasing={{0}: (7, {})} | custom-call | flops 10000000000 | bytes 100000000 | tf_op jit(solution)/shard_map/finish/pallas_call | solution.py:668
  53.8 1.0 %finish.15 = bf16[128,4096]{1,0:T(8,128)(2,1)} custom-call(f32[1,128]{1,0:T(1,128)S(1)} %get-tuple-element.102.gain_ref, bf16[4,128,128]{2,1,0:T(8,128)(2,1)S(1)} %collective-permute-done.21.state_ref, bf16[4,128,256]{2,1,0:T(8,128)(2,1)S(1)} %get-tuple-element.104.rest_2_.qo_ref, bf16[128,4096]{1,0:T(8,128)(2,1)S(1)} %copy-done.6, ...), custom_call_target="tpu_custom_call", output_to_operand_aliasing={{}: (5, {})} | custom-call | flops 10000000000 | bytes 100000000 | tf_op jit(solution)/shard_map/finish/pallas_call | solution.py:668
  (73 shorter events, 15.5 us)
Async XLA Ops:
  0.7 2.4 %collective-permute-start = (f32[1,8]{1,0:T(1,128)S(1)}, f32[1,8]{1,0:T(1,128)S(1)}, u32[]{:S(2)}, u32[]{:S(2)}) collective-permute-start(f32[1,8]{1,0:T(1,128)S(1)} %bitcast.8), channel_id=1, source_target_pairs={{0,1},{1,0},{2,3},{3,2},{4,5},{5,4},{6,7},{7,6},{8,9},{9,8},{10,11... | collective-permute-start | bytes 104 | tf_op jit(solution)/shard_map/ppermute | solution.py:702
  5.4 1.7 %collective-permute-start.1 = (bf16[4,128,256]{2,1,0:T(8,128)(2,1)S(1)}, bf16[4,128,256]{2,1,0:T(8,128)(2,1)S(1)}, u32[]{:S(2)}, u32[]{:S(2)}) collective-permute-start(bf16[4,128,256]{2,1,0:T(8,128)(2,1)S(1)} %get-tuple-element.77), channel_id=1, source_target_pairs={{0,1},{1,0},{2,3},{3,2},{4,5},{5,4},{6,7},{7,6},{8,9},{9,8},{10,11... | collective-permute-start | bytes 786440 | tf_op jit(solution)/shard_map/ppermute | solution.py:702
  7.3 3.2 %collective-permute-start.2 = (f32[8,128]{1,0:T(8,128)S(1)}, f32[8,128]{1,0:T(8,128)S(1)}, u32[]{:S(2)}, u32[]{:S(2)}) collective-permute-start(f32[8,128]{1,0:T(8,128)S(1)} %get-tuple-element.78), channel_id=1, source_target_pairs={{0,1},{1,0},{2,3},{3,2},{4,5},{5,4},{6,7},{7,6},{8,9},{9,8},{10,11... | collective-permute-start | bytes 12296 | tf_op jit(solution)/shard_map/ppermute | solution.py:702
  7.8 8.7 %collective-permute-start.5 = (f32[3,8,128]{2,1,0:T(8,128)S(1)}, f32[3,8,128]{2,1,0:T(8,128)S(1)}, u32[]{:S(2)}, u32[]{:S(2)}) collective-permute-start(f32[3,8,128]{2,1,0:T(8,128)S(1)} %get-tuple-element.73.flag_ref), channel_id=1, source_target_pairs={{0,1},{1,0},{2,3},{3,2},{4,5},{5,4},{6,7},{7,6},{8,9},{9,8},{10,11... | collective-permute-start | bytes 36872 | tf_op jit(solution)/shard_map/ppermute | solution.py:702
  7.9 6.2 %collective-permute-start.3 = (f32[8,128]{1,0:T(8,128)S(1)}, f32[8,128]{1,0:T(8,128)S(1)}, u32[]{:S(2)}, u32[]{:S(2)}) collective-permute-start(f32[8,128]{1,0:T(8,128)S(1)} %get-tuple-element.78), channel_id=1, source_target_pairs={{0,2},{1,3},{2,0},{3,1},{4,6},{5,7},{6,4},{7,5},{8,10},{9,11},{10,... | collective-permute-start | bytes 12296 | tf_op jit(solution)/shard_map/ppermute | solution.py:702
  10.5 2.5 %copy-start.4 = (bf16[128,4096]{1,0:T(8,128)(2,1)S(1)}, bf16[128,4096]{1,0:T(8,128)(2,1)}, u32[]{:S(2)}) copy-start(bf16[128,4096]{1,0:T(8,128)(2,1)} %refs_1_.3) | copy-start | bytes 3145732
  10.5 10.7 %collective-permute-start.10 = (bf16[4,128,256]{2,1,0:T(8,128)(2,1)S(1)}, bf16[4,128,256]{2,1,0:T(8,128)(2,1)S(1)}, u32[]{:S(2)}, u32[]{:S(2)}) collective-permute-start(bf16[4,128,256]{2,1,0:T(8,128)(2,1)S(1)} %get-tuple-element.94), channel_id=1, source_target_pairs={{0,2},{1,3},{2,0},{3,1},{4,6},{5,7},{6,4},{7,5},{8,10},{9,11},{10,... | collective-permute-start | bytes 786440 | tf_op jit(solution)/shard_map/ppermute | solution.py:702
  12.5 2.0 %collective-permute-start.4 = (bf16[4,128,256]{2,1,0:T(8,128)(2,1)S(1)}, bf16[4,128,256]{2,1,0:T(8,128)(2,1)S(1)}, u32[]{:S(2)}, u32[]{:S(2)}) collective-permute-start(bf16[4,128,256]{2,1,0:T(8,128)(2,1)S(1)} %get-tuple-element.85), channel_id=1, source_target_pairs={{0,1},{1,0},{2,3},{3,2},{4,5},{5,4},{6,7},{7,6},{8,9},{9,8},{10,11... | collective-permute-start | bytes 786440 | tf_op jit(solution)/shard_map/ppermute | solution.py:702
  14.7 9.3 %collective-permute-start.7 = (bf16[4,128,256]{2,1,0:T(8,128)(2,1)S(1)}, bf16[4,128,256]{2,1,0:T(8,128)(2,1)S(1)}, u32[]{:S(2)}, u32[]{:S(2)}) collective-permute-start(bf16[4,128,256]{2,1,0:T(8,128)(2,1)S(1)} %compose.8.refs_6_), channel_id=1, source_target_pairs={{0,2},{1,3},{2,0},{3,1},{4,6},{5,7},{6,4},{7,5},{8,10},{9,11},{10,... | collective-permute-start | bytes 786440 | tf_op jit(solution)/shard_map/ppermute | solution.py:702
  18.4 2.6 %collective-permute-start.9 = (bf16[4,128,256]{2,1,0:T(8,128)(2,1)S(1)}, bf16[4,128,256]{2,1,0:T(8,128)(2,1)S(1)}, u32[]{:S(2)}, u32[]{:S(2)}) collective-permute-start(bf16[4,128,256]{2,1,0:T(8,128)(2,1)S(1)} %get-tuple-element.93), channel_id=1, source_target_pairs={{0,1},{1,0},{2,3},{3,2},{4,5},{5,4},{6,7},{7,6},{8,9},{9,8},{10,11... | collective-permute-start | bytes 786440 | tf_op jit(solution)/shard_map/ppermute | solution.py:702
  20.9 2.8 %collective-permute-start.6 = (bf16[4,128,256]{2,1,0:T(8,128)(2,1)S(1)}, bf16[4,128,256]{2,1,0:T(8,128)(2,1)S(1)}, u32[]{:S(2)}, u32[]{:S(2)}) collective-permute-start(bf16[4,128,256]{2,1,0:T(8,128)(2,1)S(1)} %get-tuple-element.90), channel_id=1, source_target_pairs={{0,1},{1,0},{2,3},{3,2},{4,5},{5,4},{6,7},{7,6},{8,9},{9,8},{10,11... | collective-permute-start | bytes 786440 | tf_op jit(solution)/shard_map/ppermute | solution.py:702
  21.4 8.0 %collective-permute-start.12 = (bf16[2,128,256]{2,1,0:T(8,128)(2,1)S(1)}, bf16[2,128,256]{2,1,0:T(8,128)(2,1)S(1)}, u32[]{:S(2)}, u32[]{:S(2)}) collective-permute-start(bf16[2,128,256]{2,1,0:T(8,128)(2,1)S(1)} %compose.13), channel_id=1, source_target_pairs={{0,12},{4,8},{8,4},{12,0},{16,28},{20,24},{24,20},{28,16},{1,13},{... | collective-permute-start | bytes 393224 | tf_op jit(solution)/shard_map/ppermute | solution.py:702
  24.4 5.6 %collective-permute-start.11 = (bf16[2,128,256]{2,1,0:T(8,128)(2,1)S(1)}, bf16[2,128,256]{2,1,0:T(8,128)(2,1)S(1)}, u32[]{:S(2)}, u32[]{:S(2)}) collective-permute-start(bf16[2,128,256]{2,1,0:T(8,128)(2,1)S(1)} %compose.12), channel_id=1, source_target_pairs={{0,8},{4,12},{8,0},{12,4},{16,24},{20,28},{24,16},{28,20},{1,9},{5... | collective-permute-start | bytes 393224 | tf_op jit(solution)/shard_map/ppermute | solution.py:702
  25.4 4.6 %collective-permute-start.8 = (bf16[2,128,256]{2,1,0:T(8,128)(2,1)S(1)}, bf16[2,128,256]{2,1,0:T(8,128)(2,1)S(1)}, u32[]{:S(2)}, u32[]{:S(2)}) collective-permute-start(bf16[2,128,256]{2,1,0:T(8,128)(2,1)S(1)} %get-tuple-element.92), channel_id=1, source_target_pairs={{0,4},{4,0},{8,12},{12,8},{16,20},{20,16},{24,28},{28,24},{1,5},{5... | collective-permute-start | bytes 393224 | tf_op jit(solution)/shard_map/ppermute | solution.py:702
  30.6 4.2 %collective-permute-start.13 = (bf16[2,128,128]{2,1,0:T(8,128)(2,1)S(1)}, bf16[2,128,128]{2,1,0:T(8,128)(2,1)S(1)}, u32[]{:S(2)}, u32[]{:S(2)}) collective-permute-start(bf16[2,128,128]{2,1,0:T(8,128)(2,1)S(1)} %get-tuple-element.101.refs_2_), channel_id=1, source_target_pairs={{0,16},{4,20},{8,24},{12,28},{16,0},{20,4},{24,8},{28,12},{1,17},{... | collective-permute-start | bytes 196616 | tf_op jit(solution)/shard_map/ppermute | solution.py:702
  35.5 3.2 %collective-permute-start.16 = (bf16[2,128,128]{2,1,0:T(8,128)(2,1)S(1)}, bf16[2,128,128]{2,1,0:T(8,128)(2,1)S(1)}, u32[]{:S(2)}, u32[]{:S(2)}) collective-permute-start(bf16[2,128,128]{2,1,0:T(8,128)(2,1)S(1)} %get-tuple-element.115), channel_id=1, source_target_pairs={{0,4},{4,0},{8,12},{12,8},{16,20},{20,16},{24,28},{28,24},{1,5},{5... | collective-permute-start | bytes 196616 | tf_op jit(solution)/shard_map/ppermute | solution.py:702
  36.5 7.6 %collective-permute-start.14 = (bf16[2,128,128]{2,1,0:T(8,128)(2,1)S(1)}, bf16[2,128,128]{2,1,0:T(8,128)(2,1)S(1)}, u32[]{:S(2)}, u32[]{:S(2)}) collective-permute-start(bf16[2,128,128]{2,1,0:T(8,128)(2,1)S(1)} %get-tuple-element.112), channel_id=1, source_target_pairs={{0,8},{4,12},{8,0},{12,4},{16,24},{20,28},{24,16},{28,20},{1,9},{5... | collective-permute-start | bytes 196616 | tf_op jit(solution)/shard_map/ppermute | solution.py:702
  37.6 6.5 %collective-permute-start.15 = (bf16[2,128,128]{2,1,0:T(8,128)(2,1)S(1)}, bf16[2,128,128]{2,1,0:T(8,128)(2,1)S(1)}, u32[]{:S(2)}, u32[]{:S(2)}) collective-permute-start(bf16[2,128,128]{2,1,0:T(8,128)(2,1)S(1)} %get-tuple-element.113), channel_id=1, source_target_pairs={{0,12},{4,8},{8,4},{12,0},{16,28},{20,24},{24,20},{28,16},{1,13},{... | collective-permute-start | bytes 196616 | tf_op jit(solution)/shard_map/ppermute | solution.py:702
  39.0 5.4 %collective-permute-start.17 = (bf16[4,128,128]{2,1,0:T(8,128)(2,1)S(1)}, bf16[4,128,128]{2,1,0:T(8,128)(2,1)S(1)}, u32[]{:S(2)}, u32[]{:S(2)}) collective-permute-start(bf16[4,128,128]{2,1,0:T(8,128)(2,1)S(1)} %get-tuple-element.117), channel_id=1, source_target_pairs={{0,1},{1,0},{2,3},{3,2},{4,5},{5,4},{6,7},{7,6},{8,9},{9,8},{10,11... | collective-permute-start | bytes 393224 | tf_op jit(solution)/shard_map/ppermute | solution.py:702
  43.5 5.1 %collective-permute-start.19 = (bf16[4,128,128]{2,1,0:T(8,128)(2,1)S(1)}, bf16[4,128,128]{2,1,0:T(8,128)(2,1)S(1)}, u32[]{:S(2)}, u32[]{:S(2)}) collective-permute-start(bf16[4,128,128]{2,1,0:T(8,128)(2,1)S(1)} %get-tuple-element.119), channel_id=1, source_target_pairs={{0,2},{1,3},{2,0},{3,1},{4,6},{5,7},{6,4},{7,5},{8,10},{9,11},{10,... | collective-permute-start | bytes 393224 | tf_op jit(solution)/shard_map/ppermute | solution.py:702
  44.8 2.1 %collective-permute-start.20 = (bf16[4,128,128]{2,1,0:T(8,128)(2,1)S(1)}, bf16[4,128,128]{2,1,0:T(8,128)(2,1)S(1)}, u32[]{:S(2)}, u32[]{:S(2)}) collective-permute-start(bf16[4,128,128]{2,1,0:T(8,128)(2,1)S(1)} %get-tuple-element.120), channel_id=1, source_target_pairs={{0,1},{1,0},{2,3},{3,2},{4,5},{5,4},{6,7},{7,6},{8,9},{9,8},{10,11... | collective-permute-start | bytes 393224 | tf_op jit(solution)/shard_map/ppermute | solution.py:702
  46.0 5.6 %collective-permute-start.18 = (bf16[4,128,128]{2,1,0:T(8,128)(2,1)S(1)}, bf16[4,128,128]{2,1,0:T(8,128)(2,1)S(1)}, u32[]{:S(2)}, u32[]{:S(2)}) collective-permute-start(bf16[4,128,128]{2,1,0:T(8,128)(2,1)S(1)} %get-tuple-element.118), channel_id=1, source_target_pairs={{0,2},{1,3},{2,0},{3,1},{4,6},{5,7},{6,4},{7,5},{8,10},{9,11},{10,... | collective-permute-start | bytes 393224 | tf_op jit(solution)/shard_map/ppermute | solution.py:702
  48.7 3.7 %collective-permute-start.22 = (bf16[4,128,128]{2,1,0:T(8,128)(2,1)S(1)}, bf16[4,128,128]{2,1,0:T(8,128)(2,1)S(1)}, u32[]{:S(2)}, u32[]{:S(2)}) collective-permute-start(bf16[4,128,128]{2,1,0:T(8,128)(2,1)S(1)} %get-tuple-element.129), channel_id=1, source_target_pairs={{0,1},{1,0},{2,3},{3,2},{4,5},{5,4},{6,7},{7,6},{8,9},{9,8},{10,11... | collective-permute-start | bytes 393224 | tf_op jit(solution)/shard_map/ppermute | solution.py:702
  51.8 2.1 %collective-permute-start.21 = (bf16[4,128,128]{2,1,0:T(8,128)(2,1)S(1)}, bf16[4,128,128]{2,1,0:T(8,128)(2,1)S(1)}, u32[]{:S(2)}, u32[]{:S(2)}) collective-permute-start(bf16[4,128,128]{2,1,0:T(8,128)(2,1)S(1)} %get-tuple-element.126), channel_id=1, source_target_pairs={{0,1},{1,0},{2,3},{3,2},{4,5},{5,4},{6,7},{7,6},{8,9},{9,8},{10,11... | collective-permute-start | bytes 393224 | tf_op jit(solution)/shard_map/ppermute | solution.py:702
  (8 other events, 13.0 us)
